TPU v7x, 32 devices: a whole 2x2x4 slice. The times are simulated.
32 devices in a mesh: groups: 2 (over x), seq: 8 (over z, y), role: 2 (over core).
Axes of the slice: x: 2, y: 2, z: 4, core: 2. Of those that a mesh axis runs over, the one named last changes fastest.
Arguments:
- pair_rep: bfloat16 [512, 256, 128], P(('groups', 'seq', 'role')), parts along dimension 0, may hold values from -6 to 6
- tri_gain: float32 [2, 128], replicated, may hold values from 0.1 to 1.9
- tri_proj: bfloat16 [2, 128, 512], replicated, may hold values from -0.5 to 0.5
- tri_gate: bfloat16 [2, 128, 128], replicated, may hold values from -0.5 to 0.5
- tri_mid_gain: float32 [2, 128], replicated, may hold values from 0.1 to 1.9
- tri_out: bfloat16 [2, 128, 128], replicated, may hold values from -0.5 to 0.5
- trans_gain: float32 [128], replicated, may hold values from 0.1 to 1.9
- trans_up: bfloat16 [128, 1024], replicated, may hold values from -0.5 to 0.5
- trans_down: bfloat16 [512, 128], replicated, may hold values from -0.25 to 0.25
Outputs:
- pair_out: bfloat16 [512, 256, 128], P(('groups', 'seq', 'role')), parts along dimension 0
There are 2 independent parts, one for each index of `groups`. A program takes and returns all parts, laid end to end along the dimension named above; an argument that names none is the same for every part. Nothing has to cross between parts.
All inputs are finite; a program needn't handle non-finite values.
Results may differ from a plain program's by a relative error of at most 0.012.
Values may be sent and summed in bfloat16 or wider, within the bound.
No kernel may reach another device: no remote copies, remote signals or barrier semaphores. Data moves between devices by JAX's collectives and lax.ppermute only.
A program may use at most 64 MiB of HBM per device.

v0:
```python
import math

import jax
import jax.numpy as jnp
from jax import lax
from jax.sharding import PartitionSpec as P

epsilon = 1e-05


def layer_norm(values, gain):
    average = jnp.mean(values, axis=-1, keepdims=True)
    centred = values - average
    spread = jnp.mean(centred * centred, axis=-1, keepdims=True)
    return centred * lax.rsqrt(spread + epsilon) * gain


def multiply(left_side, right_side, which):
    if which == 0:
        return jnp.einsum("cik,cjk->cij", left_side, right_side, preferred_element_type=jnp.float32)
    return jnp.einsum("cki,ckj->cij", left_side, right_side, preferred_element_type=jnp.float32)


def local(
    pair_rep, tri_gain, tri_proj, tri_gate, tri_mid_gain, tri_out, trans_gain, trans_up, trans_down
):
    rows, width, channels = pair_rep.shape
    inner = tri_out.shape[1]
    hidden_width = trans_down.shape[0]
    seq_count = lax.axis_size("seq")
    role_count = lax.axis_size("role")
    groups_total = seq_count * role_count
    per_device = inner // groups_total
    block_rows = math.gcd(rows, 4)
    current = pair_rep
    for which in range(2):
        pieces = []
        gate_list = []
        for start_row in range(0, rows, block_rows):
            block_in = current[start_row : start_row + block_rows].astype(jnp.float32)
            normed = layer_norm(block_in, tri_gain[which]).astype(jnp.bfloat16)
            projected = jnp.einsum(
                "rnd,de->ern", normed, tri_proj[which], preferred_element_type=jnp.float32
            )
            left_side = projected[:inner] * jax.nn.sigmoid(projected[inner : 2 * inner])
            right_side = projected[2 * inner : 3 * inner] * jax.nn.sigmoid(projected[3 * inner :])
            pieces.append(jnp.stack([left_side, right_side]).astype(jnp.bfloat16))
            gate_list.append(
                jax.nn.sigmoid(
                    jnp.einsum(
                        "rnd,de->rne", normed, tri_gate[which], preferred_element_type=jnp.float32
                    )
                )
            )
        stacked = jnp.concatenate(pieces, axis=2)
        gating = jnp.concatenate(gate_list, axis=0)
        sending = stacked.reshape(2, groups_total, per_device, 1, rows, width)

        def product_fn(arrived, which=which):
            count_items = arrived.shape[2]
            whole = arrived.reshape(2, count_items, width, width)
            result = multiply(whole[0], whole[1], which).astype(jnp.bfloat16)
            return result.reshape(1, count_items, width, width)

        result = product_fn(
            lax.all_to_all(sending, ("seq", "role"), split_axis=1, concat_axis=3, tiled=True)
        )
        returned = lax.all_to_all(
            result.reshape(1, per_device, groups_total, rows, width),
            ("seq", "role"),
            split_axis=2,
            concat_axis=0,
            tiled=True,
        )
        mixed = returned.reshape(inner, rows, width).astype(jnp.float32)
        average = jnp.mean(mixed, axis=0, keepdims=True)
        centred = mixed - average
        spread = jnp.mean(centred * centred, axis=0, keepdims=True)
        normed_mid = (
            centred * lax.rsqrt(spread + epsilon) * tri_mid_gain[which][:, None, None]
        ).astype(jnp.bfloat16)
        update = jnp.einsum(
            "crn,ce->rne", normed_mid, tri_out[which], preferred_element_type=jnp.float32
        )
        current = (current.astype(jnp.float32) + gating * update).astype(jnp.bfloat16)
    outputs = []
    for start_row in range(0, rows, block_rows):
        block_in = current[start_row : start_row + block_rows].astype(jnp.float32)
        normed = layer_norm(block_in, trans_gain).astype(jnp.bfloat16)
        values = jnp.einsum("rnd,de->rne", normed, trans_up, preferred_element_type=jnp.float32)
        hidden = (jax.nn.silu(values[..., :hidden_width]) * values[..., hidden_width:]).astype(
            jnp.bfloat16
        )
        down = jnp.einsum("rnd,de->rne", hidden, trans_down, preferred_element_type=jnp.float32)
        outputs.append((block_in + down).astype(jnp.bfloat16))
    return jnp.concatenate(outputs, axis=0)


def solution(mesh):
    in_specs = (P(("groups", "seq", "role"), None, None), P(), P(), P(), P(), P(), P(), P(), P())
    out_specs = P(("groups", "seq", "role"), None, None)
    return jax.shard_map(local, mesh=mesh, in_specs=in_specs, out_specs=out_specs, check_vma=False)
```

profile of v0, /device:TPU:25, one launch (start us, length us, event | category | flops | bytes accessed | tf_op | source)
XLA Modules:
  0.0 202.6 jit_solution(14559246247579466240)
XLA Ops:
  0.0 1.7 convert_reduce_fusion.11
  1.7 2.4 %fusion.113 = (f32[4,256]{1,0:T(4,128)S(1)}, f32[4,256]{1,0:T(4,128)S(1)}, f32[4,256]{1,0:T(4,128)S(1)}, f32[4,256]{1,0:T(4,128)S(1)}) fusion(f32[4,256]{1,0:T(4,128)S(1)} %get-tuple-element.56, bf16[16,256,128]{2,1,0:T(8,128)(2,1)} %param.9, f32[4,256]{1,0:T(4,128)S(1)} %get-tuple-element.55, f32[4,256]{1,0:T(4,128)S(1)} %get-tuple-element.54, ...), kind=kLoop, calls=%fused_computation.167 | loop fusion | flops 2093056 | bytes 1081344 | tf_op jit(solution)/shard_map/reduce_sum | solution.py:14
  7.8 1.1 fusion.180
  8.9 1.1 copy.89
  10.0 1.8 copy.90
  11.7 0.8 copy.91
  12.6 1.2 maximum_maximum_fusion
  14.1 52.4 %all_to_all.48 = bf16[2,16,8,1,16,256]{5,2,4,3,0,1:T(8,128)(2,1)S(1)} all-to-all(bf16[2,16,8,1,16,256]{5,2,4,3,0,1:T(8,128)(2,1)S(1)} %copy.97), channel_id=1, replica_groups=mesh['groups'=2,'seq'=8,'role'=2] {'seq','role'}, dimensions={1} | all-to-all | bytes 4194304 | tf_op jit(solution)/shard_map/all_to_all | solution.py:66
  67.7 1.1 copy.100
  68.8 6.3 %all-to-all-start.1 = ((bf16[1,8,16,16,256]{4,3,1,0,2:T(8,128)(2,1)}), bf16[1,8,16,16,256]{4,3,1,0,2:T(8,128)(2,1)S(1)}, u32[]{:S(2)}, u32[]{:S(2)}) async-start(bf16[1,8,16,16,256]{4,3,1,0,2:T(8,128)(2,1)} %copy.100), calls=%async_computation.1 | async-start | bytes 2097152 | tf_op jit(solution)/shard_map/all_to_all | solution.py:68
  75.1 1.3 copy.87
  76.5 0.9 fusion.39
  77.4 1.4 fusion.42
  78.8 1.4 fusion.45
  80.2 1.4 fusion.36
  81.6 16.5 %all-to-all-done.1 = bf16[1,8,16,16,256]{4,3,1,0,2:T(8,128)(2,1)S(1)} async-done(((bf16[1,8,16,16,256]{4,3,1,0,2:T(8,128)(2,1)}), bf16[1,8,16,16,256]{4,3,1,0,2:T(8,128)(2,1)S(1)}, u32[]{:S(2)}, u32[]{:S(2)}) %all-to-all-start.1) | async-done | bytes 1048608 | tf_op jit(solution)/shard_map/all_to_all | solution.py:68
  104.9 1.0 fusion.194
  106.0 1.1 copy.119
  107.7 52.8 %all_to_all.49 = bf16[2,16,8,1,16,256]{5,2,4,3,0,1:T(8,128)(2,1)S(1)} all-to-all(bf16[2,16,8,1,16,256]{5,2,4,3,0,1:T(8,128)(2,1)S(1)} %copy.120), channel_id=1, replica_groups=mesh['groups'=2,'seq'=8,'role'=2] {'seq','role'}, dimensions={1} | all-to-all | bytes 4194304 | tf_op jit(solution)/shard_map/all_to_all | solution.py:66
  161.7 1.1 copy.123
  162.7 6.2 %all-to-all-start.3 = ((bf16[1,8,16,16,256]{4,3,1,0,2:T(8,128)(2,1)}), bf16[1,8,16,16,256]{4,3,1,0,2:T(8,128)(2,1)S(1)}, u32[]{:S(2)}, u32[]{:S(2)}) async-start(bf16[1,8,16,16,256]{4,3,1,0,2:T(8,128)(2,1)} %copy.123), calls=%async_computation.3 | async-start | bytes 2097152 | tf_op jit(solution)/shard_map/all_to_all | solution.py:68
  169.4 1.2 fusion.30
  170.6 1.2 fusion.27
  171.7 1.1 fusion.24
  172.9 19.0 %all-to-all-done.3 = bf16[1,8,16,16,256]{4,3,1,0,2:T(8,128)(2,1)S(1)} async-done(((bf16[1,8,16,16,256]{4,3,1,0,2:T(8,128)(2,1)}), bf16[1,8,16,16,256]{4,3,1,0,2:T(8,128)(2,1)S(1)}, u32[]{:S(2)}, u32[]{:S(2)}) %all-to-all-start.3) | async-done | bytes 1048608 | tf_op jit(solution)/shard_map/all_to_all | solution.py:68
  194.6 0.8 fusion.196
  195.4 0.8 fusion.198
  197.9 0.8 fusion.200
  198.7 0.8 fusion.48
  199.5 0.8 fusion.202
  200.3 0.8 fusion.49
  201.3 1.3 copy.134
  (116 shorter events, 18.3 us)
Async XLA Ops:
  0.0 194.5 %copy-start = (bf16[128,1024]{1,0:T(8,128)(2,1)S(1)}, bf16[128,1024]{1,0:T(8,128)(2,1)}, u32[]{:S(2)}) copy-start(bf16[128,1024]{1,0:T(8,128)(2,1)} %param.16) | copy-start | bytes 786436
  0.0 4.2 %copy-start.1 = (bf16[16,256,128]{2,1,0:T(8,128)(2,1)S(1)}, bf16[16,256,128]{2,1,0:T(8,128)(2,1)}, u32[]{:S(2)}) copy-start(bf16[16,256,128]{2,1,0:T(8,128)(2,1)} %param.9) | copy-start | bytes 3145732
  0.0 4.1 %copy-start.5 = (f32[2,128]{1,0:T(2,128)S(1)}, f32[2,128]{1,0:T(2,128)}, u32[]{:S(2)}) copy-start(f32[2,128]{1,0:T(2,128)} %param.10) | copy-start | bytes 3076
  0.0 4.2 %copy-start.2 = (bf16[2,128,512]{2,1,0:T(8,128)(2,1)S(1)}, bf16[2,128,512]{2,1,0:T(8,128)(2,1)}, u32[]{:S(2)}) copy-start(bf16[2,128,512]{2,1,0:T(8,128)(2,1)} %param.11) | copy-start | bytes 786436
  68.8 7.6 %copy-start.6 = (f32[2,128]{1,0:T(2,128)S(1)}, f32[2,128]{1,0:T(2,128)}, u32[]{:S(2)}) copy-start(f32[2,128]{1,0:T(2,128)} %param.13) | copy-start | bytes 3076
  68.8 7.7 %copy-start.8 = (bf16[2,128,128]{2,1,0:T(8,128)(2,1)S(1)}, bf16[2,128,128]{2,1,0:T(8,128)(2,1)}, u32[]{:S(2)}) copy-start(bf16[2,128,128]{2,1,0:T(8,128)(2,1)} %param.12) | copy-start | bytes 196612
  68.8 29.3 %all-to-all-start.1 = ((bf16[1,8,16,16,256]{4,3,1,0,2:T(8,128)(2,1)}), bf16[1,8,16,16,256]{4,3,1,0,2:T(8,128)(2,1)S(1)}, u32[]{:S(2)}, u32[]{:S(2)}) async-start(bf16[1,8,16,16,256]{4,3,1,0,2:T(8,128)(2,1)} %copy.100), calls=%async_computation.1 | async-start | bytes 2097152 | tf_op jit(solution)/shard_map/all_to_all | solution.py:68
  81.6 17.4 %copy-start.9 = (bf16[2,128,128]{2,1,0:T(8,128)(2,1)S(1)}, bf16[2,128,128]{2,1,0:T(8,128)(2,1)}, u32[]{:S(2)}) copy-start(bf16[2,128,128]{2,1,0:T(8,128)(2,1)} %param.14) | copy-start | bytes 196612
  98.1 1.2 copy-start.3
  98.1 1.4 copy-start.11
  98.1 1.5 copy-start.13
  98.1 1.7 copy-start.15
  162.7 29.2 %all-to-all-start.3 = ((bf16[1,8,16,16,256]{4,3,1,0,2:T(8,128)(2,1)}), bf16[1,8,16,16,256]{4,3,1,0,2:T(8,128)(2,1)S(1)}, u32[]{:S(2)}, u32[]{:S(2)}) async-start(bf16[1,8,16,16,256]{4,3,1,0,2:T(8,128)(2,1)} %copy.123), calls=%async_computation.3 | async-start | bytes 2097152 | tf_op jit(solution)/shard_map/all_to_all | solution.py:68
  172.9 19.9 %copy-start.10 = (bf16[2,128,128]{2,1,0:T(8,128)(2,1)S(1)}, bf16[2,128,128]{2,1,0:T(8,128)(2,1)}, u32[]{:S(2)}) copy-start(bf16[2,128,128]{2,1,0:T(8,128)(2,1)} %param.14) | copy-start | bytes 196612
  191.9 1.0 copy-start.12
  191.9 1.2 copy-start.14
  191.9 1.4 copy-start.16
  193.9 0.7 copy-start.4
  195.4 0.9 copy-start.7
where the time goes:
time: 205 us; the launch traced here: 203 us
  blocking collectives  105 us (51%)
  waiting for transfers between devices  35.6 us (17%)
  matrix products  21.6 us (11%)
  local copies, waits for them, and re-layouts  14.7 us (7%)
  starting transfers between devices  12.5 us (6%)
  other arithmetic  12.3 us (6%)
    all_to_all x2, blocking collectives, local(): lax.all_to_all(sending, ('seq', 'role'), split_axis=1, concat_axis=3, til...  105 us
    all_to_all x2, waiting for transfers between devices, local(): lax.all_to_all(result.reshape(1, per_device, groups_total, rows, width),...  35.6 us
    all_to_all x2, starting transfers between devices, local(): lax.all_to_all(result.reshape(1, per_device, groups_total, rows, width),...  12.5 us
    dot_general x8, matrix products, local(): jnp.einsum('rnd,de->rne', normed, tri_gate[which], preferred_element_type...  8.94 us
    another operation x16, local copies, waits for them, and re-layouts  6.54 us
  transfers between devices with their start and end apart: 2, of which 2 were waited for; matrix products, arithmetic and copies ran while one was open for 5% of the time, Pallas kernels for 0%

commit v1 on v0

v1 whole, which is shorter than its diff:
```python
import functools

import jax
import jax.numpy as jnp
from jax import lax
from jax.experimental import pallas as pl
from jax.experimental.pallas import tpu as pltpu
from jax.sharding import PartitionSpec as P


epsilon = 1e-05
LANES = 128
VMEM_BYTES = 60 * 1024 * 1024
AXES = ("groups", "seq", "role")


def sigmoid(values):
    return 0.5 * jnp.tanh(0.5 * values) + 0.5


def norm_lanes(values, gain):
    average = jnp.mean(values, axis=-1, keepdims=True)
    centred = values - average
    spread = jnp.mean(centred * centred, axis=-1, keepdims=True)
    return (centred * lax.rsqrt(spread + epsilon) * gain).astype(jnp.bfloat16)


def dot(a, b, contract):
    return lax.dot_general(
        a, b, ((contract[:1], contract[1:]), ((), ())), preferred_element_type=jnp.float32
    )


def project(normed, proj_ref, sent_ref, scratch_ref, rows):
    parts, block, lanes = sent_ref.shape
    inner = proj_ref.shape[1] // 4
    half = block // 2
    for side in range(2):
        base = 2 * side * inner
        value = dot(proj_ref[:, base : base + inner], normed, (0, 1))
        gate = dot(proj_ref[:, base + inner : base + 2 * inner], normed, (0, 1))
        value = value * sigmoid(gate)
        for row in range(rows):
            scratch_ref[pl.ds(row, inner, stride=rows), :] = value[:, row * lanes : (row + 1) * lanes]
        sent_ref[:, side * half : (side + 1) * half] = (
            scratch_ref[: inner * rows].reshape(parts, half, lanes).astype(jnp.bfloat16)
        )


def combine(pair, rows, gain, gate_ref, mid_gain, out_ref, got_ref, scratch_ref):
    lanes = got_ref.shape[2]
    inner = out_ref.shape[0]
    got = got_ref[...].astype(jnp.float32).reshape(inner, rows, lanes)
    average = jnp.mean(got, axis=0, keepdims=True)
    centred = got - average
    spread = jnp.mean(centred * centred, axis=0, keepdims=True)
    scratch_ref[: inner * rows] = (centred * lax.rsqrt(spread + epsilon)).reshape(
        inner * rows, lanes
    )
    gating = sigmoid(dot(norm_lanes(pair, gain), gate_ref[...], (1, 0)))
    mid_gain = jnp.broadcast_to(mid_gain, (lanes, inner)).T
    updates = []
    for row in range(rows):
        mid = (scratch_ref[pl.ds(row, inner, stride=rows), :] * mid_gain).astype(jnp.bfloat16)
        updates.append(dot(mid, out_ref[...], (0, 0)))
    update = jnp.concatenate(updates, axis=0)
    return (pair + gating * update).astype(jnp.bfloat16)


def flat(pair):
    rows, lanes, channels = pair.shape
    return pair.astype(jnp.float32).reshape(rows * lanes, channels)


def first_kernel(
    flag_ref, own_ref, other_ref, gain_ref, proj_ref, pair_ref, sent_ref, scratch_ref
):
    rows = own_ref.shape[0]
    pair = jnp.where(flag_ref[0] == 1, flat(own_ref[...]), flat(other_ref[...]))
    pair_ref[...] = pair.astype(jnp.bfloat16).reshape(pair_ref.shape)
    project(norm_lanes(pair, gain_ref[0:1]), proj_ref, sent_ref, scratch_ref, rows)


def middle_kernel(
    near_ref, far_ref, got_ref, gain_ref, gate_ref, mid_gain_ref, out_ref, proj_ref,
    pair_out_ref, sent_ref, scratch_ref,
):
    rows = 2 * near_ref.shape[0]
    pair = jnp.concatenate([flat(near_ref[...]), flat(far_ref[...])], axis=0)
    current = combine(
        pair, rows, gain_ref[0:1], gate_ref, mid_gain_ref[0:1], out_ref, got_ref, scratch_ref
    )
    pair_out_ref[...] = current.reshape(pair_out_ref.shape)
    normed = norm_lanes(current.astype(jnp.float32), gain_ref[1:2])
    project(normed, proj_ref, sent_ref, scratch_ref, rows)


def last_kernel(
    pair_ref, got_ref, gain_ref, gate_ref, mid_gain_ref, out_ref, trans_gain_ref, up_ref, down_ref,
    pair_out_ref, scratch_ref,
):
    rows = pair_ref.shape[0]
    current = combine(
        flat(pair_ref[...]), rows, gain_ref[1:2], gate_ref, mid_gain_ref[1:2], out_ref, got_ref,
        scratch_ref,
    ).astype(jnp.float32)
    normed = norm_lanes(current, trans_gain_ref[...])
    hidden_width = down_ref.shape[0]
    total = current
    block = min(hidden_width, 2 * LANES)
    for start in range(0, hidden_width, block):
        gate = dot(normed, up_ref[:, start : start + block], (1, 0))
        value = dot(normed, up_ref[:, hidden_width + start : hidden_width + start + block], (1, 0))
        hidden = (gate * sigmoid(gate) * value).astype(jnp.bfloat16)
        total = total + dot(hidden, down_ref[start : start + block], (1, 0))
    pair_out_ref[...] = total.astype(jnp.bfloat16).reshape(pair_out_ref.shape)


def outgoing_kernel(side_ref, near_ref, far_ref, sent_ref):
    parts, block, width = near_ref.shape
    per, rows = sent_ref.shape[1], sent_ref.shape[2] // 2
    count = parts * rows
    side = side_ref[0]
    slots = [
        ref[...].astype(jnp.float32).reshape(parts, 2, per, rows, width)
        for ref in (near_ref, far_ref)
    ]
    for item in range(per):
        left, right = [
            [slot[:, which, item].reshape(count, width).astype(jnp.bfloat16) for slot in slots]
            for which in range(2)
        ]
        left = jnp.concatenate(left, axis=0)
        for slot in range(2):
            place = jnp.where(side == 0, slot, 1 - slot)
            part = dot(left, right[slot], (1, 1)).reshape(2, parts, rows, count)
            sent_ref[:, item, :, pl.ds(pl.multiple_of(place * count, LANES), count)] = (
                jnp.concatenate([part[0], part[1]], axis=1).astype(jnp.bfloat16)
            )


def incoming_kernel(side_ref, got_ref, sent_ref):
    parts, _, per, rows, width = got_ref.shape
    half = width // 2
    place = pl.ds(pl.multiple_of(side_ref[0] * half, LANES), half)
    own = rows // 2
    for item in range(per):
        left = got_ref[:, 0, item, :, place].reshape(parts * rows, half)
        right = got_ref[:, 1, item].reshape(parts * rows, width)
        sent_ref[:, item * own : (item + 1) * own] = dot(left, right, (0, 0)).reshape(
            parts, own, width
        ).astype(jnp.bfloat16)


def whole(shape):
    return pl.BlockSpec(shape, lambda step: (0,) * len(shape))


def one_of(shape, which):
    return pl.BlockSpec((None,) + shape, lambda step: (which,) + (0,) * len(shape))


def params():
    return pltpu.CompilerParams(vmem_limit_bytes=VMEM_BYTES)


def after(value, earlier):
    return lax.optimization_barrier((value, earlier))[0]


def local(
    pair_rep, tri_gain, tri_proj, tri_gate, tri_mid_gain, tri_out, trans_gain, trans_up, trans_down
):
    rows, width, channels = pair_rep.shape
    inner = tri_out.shape[1]
    groups, seq, role = (lax.axis_size(axis) for axis in AXES)
    half_seq = seq // 2
    parts = seq * role
    per = inner // parts
    own = rows // 2
    steps = width // LANES

    def number(g, s, c):
        return (g * seq + s) * role + c

    every = [(g, s, c) for g in range(groups) for s in range(seq) for c in range(role)]

    def at_home(g, s):
        return s // half_seq == g % 2

    def across(s):
        return (s + half_seq) % seq

    def permute(value, pairs):
        return lax.ppermute(value, AXES, [(number(*a), number(*b)) for a, b in pairs])

    blocks = [
        [
            number(base + u, side * half_seq + s, c)
            for s in range(half_seq)
            for c in range(role)
            for u in (side, 1 - side)
        ]
        for base in range(0, groups, 2)
        for side in range(2)
    ]

    def exchange(value):
        return lax.all_to_all(
            value, AXES, split_axis=0, concat_axis=0, tiled=True, axis_index_groups=blocks
        )

    side = lax.axis_index("seq") // half_seq
    home = side == lax.axis_index("groups") % 2
    side_flag = side.astype(jnp.int32).reshape(1)
    other_side_flag = 1 - side_flag
    home_flag = home.astype(jnp.int32).reshape(1)

    low, high = pair_rep[:own], pair_rep[own:]
    hopped = permute(high, [((g, s, c), (g ^ 1, s, c)) for g, s, c in every])
    direct = permute(low, [((g, s, c), (g, across(s), c)) for g, s, c in every if not at_home(g, s)])
    relayed = permute(hopped, [((g, s, c), (g, across(s), c)) for g, s, c in every if at_home(g, s)])

    flag_spec = pl.BlockSpec(memory_space=pltpu.SMEM)
    slot_spec = pl.BlockSpec((own, LANES, channels), lambda step: (0, step, 0))
    pair_spec = pl.BlockSpec((rows, LANES, channels), lambda step: (0, step, 0))
    gain_spec, mid_gain_spec = whole(tri_gain.shape), whole(tri_mid_gain.shape)
    scratch = [pltpu.VMEM((inner * rows, LANES), jnp.float32)]

    def shape(*dims):
        return jax.ShapeDtypeStruct(dims, jnp.bfloat16)

    def first(own_rows, other_rows, flops):
        return pl.pallas_call(
            first_kernel,
            grid=(steps,),
            in_specs=[
                flag_spec, slot_spec, slot_spec, gain_spec, one_of(tri_proj.shape[1:], 0),
            ],
            out_specs=[
                slot_spec,
                pl.BlockSpec((parts, 2 * per * own, LANES), lambda step: (0, 0, step)),
            ],
            out_shape=[shape(own, width, channels), shape(parts, 2 * per * own, width)],
            scratch_shapes=scratch,
            compiler_params=params(),
            cost_estimate=pl.CostEstimate(flops=flops, bytes_accessed=4 * 1024 * 1024, transcendentals=0),
            name="project",
        )(home_flag, own_rows, other_rows, tri_gain, tri_proj)

    near, near_sent = first(pair_rep, hopped, 0)
    near_got = exchange(near_sent)
    far, far_sent = first(direct, relayed, 20000000000)
    far_got = exchange(far_sent)

    product = pl.pallas_call(
        outgoing_kernel,
        in_specs=[flag_spec, pl.BlockSpec(), pl.BlockSpec()],
        out_specs=pl.BlockSpec(),
        out_shape=shape(parts, per, rows, width),
        compiler_params=params(),
        name="outgoing",
    )(side_flag, near_got, far_got)
    back = exchange(product).reshape(parts, per * rows, width)

    current, sent = pl.pallas_call(
        middle_kernel,
        grid=(steps,),
        in_specs=[
            slot_spec, slot_spec,
            pl.BlockSpec((parts, per * rows, LANES), lambda step: (0, 0, step)),
            gain_spec, one_of((channels, channels), 0), mid_gain_spec,
            one_of((inner, channels), 0), one_of(tri_proj.shape[1:], 1),
        ],
        out_specs=[
            pair_spec, pl.BlockSpec((parts, 2 * per * rows, LANES), lambda step: (0, 0, step)),
        ],
        out_shape=[shape(rows, width, channels), shape(parts, 2 * per * rows, width)],
        scratch_shapes=scratch,
        compiler_params=params(),
        name="combine_project",
    )(near, far, back, tri_gain, tri_gate, tri_mid_gain, tri_out, tri_proj)
    got = exchange(sent).reshape(parts, 2, per, rows, width)

    def incoming(flag, got):
        return pl.pallas_call(
            incoming_kernel,
            in_specs=[flag_spec, pl.BlockSpec()],
            out_specs=pl.BlockSpec(),
            out_shape=shape(parts, per * own, width),
            compiler_params=params(),
            name="incoming",
        )(flag, got)

    def last(slot, back):
        return pl.pallas_call(
            last_kernel,
            grid=(steps,),
            in_specs=[
                pl.BlockSpec((own, LANES, channels), lambda step: (slot, step, 0)),
                pl.BlockSpec((parts, per * own, LANES), lambda step: (0, 0, step)),
                gain_spec, one_of((channels, channels), 1), mid_gain_spec,
                one_of((inner, channels), 1), whole((1, channels)),
                whole(trans_up.shape), whole(trans_down.shape),
            ],
            out_specs=slot_spec,
            out_shape=shape(own, width, channels),
            scratch_shapes=scratch,
            compiler_params=params(),
            name="combine_transition",
        )(
            current, back, tri_gain, tri_gate, tri_mid_gain, tri_out, trans_gain[None],
            trans_up, trans_down,
        )

    far_product = incoming(other_side_flag, got)
    near_product = incoming(side_flag, after(got, far_product))
    far_back = exchange(far_product)
    near_back = exchange(after(near_product, far_back))
    far_out = last(1, far_back)
    near_out = last(0, near_back)

    from_home = permute(
        far_out, [((g, s, c), (g, across(s), c)) for g, s, c in every if at_home(g, s)]
    )
    from_away = permute(
        far_out, [((g, s, c), (g ^ 1, across(s), c)) for g, s, c in every if not at_home(g, s)]
    )
    from_near = permute(
        near_out, [((g, s, c), (g ^ 1, s, c)) for g, s, c in every if not at_home(g, s)]
    )
    return jnp.concatenate(
        [jnp.where(home, near_out, from_home), jnp.where(home, from_near, from_away)], axis=0
    )


def solution(mesh):
    in_specs = (P(AXES, None, None), P(), P(), P(), P(), P(), P(), P(), P())
    out_specs = P(AXES, None, None)
    return jax.shard_map(local, mesh=mesh, in_specs=in_specs, out_specs=out_specs, check_vma=False)
```

time: 205 us -> 194 us (0.946)
  blocking collectives: 105 us -> 41.6 us
  Pallas kernels: 0 us -> 38.8 us
  waiting for transfers between devices: 35.6 us -> 72.1 us
  starting transfers between devices: 12.5 us -> 34.6 us
  matrix products: 21.6 us -> 0 us
  other arithmetic: 12.3 us -> 1.18 us
  local copies, waits for them, and re-layouts: 14.7 us -> 4.21 us
    all_to_all x2, blocking collectives: 105 us -> 41.6 us  [exchange(): lax.all_to_all(value, AXES, split_axis=0, concat_axis=0, tiled=True, axis...]
    ppermute x0 -> x6, waiting for transfers between devices: none -> 41 us  [permute(): lax.ppermute(value, AXES, [(number(*a), number(*b)) for a, b in pairs])]
    pallas_call x0 -> x8, Pallas kernels: none -> 38.8 us  [the longest x2 13.6 us: last(): pl.pallas_call(last_kernel, grid=(steps,), in_specs=[pl.BlockSpec((own, L...]
    dot_general x28 -> x0, matrix products: 21.6 us -> none  [the longest x8 8.94 us: local(): jnp.einsum('rnd,de->rne', normed, tri_gate[which], preferred_element_type...]
    all_to_all x2 -> x4, starting transfers between devices: 12.5 us -> 23.6 us  [exchange(): lax.all_to_all(value, AXES, split_axis=0, concat_axis=0, tiled=True, axis...]
    ppermute x0 -> x6, starting transfers between devices: none -> 11 us  [permute(): lax.ppermute(value, AXES, [(number(*a), number(*b)) for a, b in pairs])]
    another operation x18 -> x0, local copies, waits for them, and re-layouts: 8.71 us -> none
    reduce_sum x10 -> x0, other arithmetic: 6.12 us -> none  [the longest x3 3.04 us: layer_norm(): spread = jnp.mean(centred * centred, axis=-1, keepdims=True)]
  transfers between devices with their start and end apart: 2 -> 10, of which waited for: 2 -> 6; matrix products, arithmetic and copies ran while one was open for 5% -> 0% of each run, Pallas kernels for 0% -> 12%
where the time goes in v1:
time: 194 us; the launch traced here: 193 us
  waiting for transfers between devices  72.1 us (37%)
  blocking collectives  41.6 us (21%)
  Pallas kernels  38.8 us (20%)
  starting transfers between devices  34.6 us (18%)
  local copies, waits for them, and re-layouts  4.21 us (2%)
    all_to_all x2, blocking collectives, exchange(): lax.all_to_all(value, AXES, split_axis=0, concat_axis=0, tiled=True, axis...  41.6 us
    ppermute x6, waiting for transfers between devices, permute(): lax.ppermute(value, AXES, [(number(*a), number(*b)) for a, b in pairs])  41 us
    all_to_all x4, waiting for transfers between devices, exchange(): lax.all_to_all(value, AXES, split_axis=0, concat_axis=0, tiled=True, axis...  31.1 us
    all_to_all x4, starting transfers between devices, exchange(): lax.all_to_all(value, AXES, split_axis=0, concat_axis=0, tiled=True, axis...  23.6 us
    pallas_call x2, Pallas kernels, last(): pl.pallas_call(last_kernel, grid=(steps,), in_specs=[pl.BlockSpec((own, L...  13.6 us
    ppermute x6, starting transfers between devices, permute(): lax.ppermute(value, AXES, [(number(*a), number(*b)) for a, b in pairs])  11 us
    pallas_call x1, Pallas kernels, local(): pl.pallas_call(middle_kernel, grid=(steps,), in_specs=[slot_spec, slot_sp...  8.84 us
    pallas_call x2, Pallas kernels, first(): pl.pallas_call(first_kernel, grid=(steps,), in_specs=[flag_spec, slot_spe...  7.59 us
  transfers between devices with their start and end apart: 10, of which 6 were waited for; matrix products, arithmetic and copies ran while one was open for 0% of the time, Pallas kernels for 12%

profile of v1, /device:TPU:25, one launch (start us, length us, event | category | flops | bytes accessed | tf_op | source)
XLA Modules:
  0.0 192.6 jit_solution(5771560801055602746)
XLA Ops:
  0.0 1.3 fusion
  1.3 1.3 collective-permute-start
  2.6 2.0 %collective-permute-start.1 = (bf16[8,256,128]{2,1,0:T(8,128)(2,1)S(1)}, bf16[8,256,128]{2,1,0:T(8,128)(2,1)S(1)}, u32[]{:S(2)}, u32[]{:S(2)}) collective-permute-start(bf16[8,256,128]{2,1,0:T(8,128)(2,1)S(1)} %get-tuple-element.21), channel_id=1, source_target_pairs={{8,0},{9,1},{10,2},{11,3},{12,4},{13,5},{14,6},{15,7},{16,24},{17,... | collective-permute-start | bytes 1572872 | tf_op jit(solution)/shard_map/ppermute | solution.py:195
  4.5 9.6 %collective-permute-done.other_ref = bf16[8,256,128]{2,1,0:T(8,128)(2,1)S(1)} collective-permute-done((bf16[8,256,128]{2,1,0:T(8,128)(2,1)S(1)}, bf16[8,256,128]{2,1,0:T(8,128)(2,1)S(1)}, u32[]{:S(2)}, u32[]{:S(2)}) %collective-permute-start) | collective-permute-done | bytes 524320 | tf_op jit(solution)/shard_map/ppermute | solution.py:195
  14.1 1.3 collective-permute-start.2
  15.5 3.8 %project.2 = (bf16[8,256,128]{2,1,0:T(8,128)(2,1)}, bf16[16,128,256]{2,1,0:T(8,128)(2,1)}) custom-call(s32[1]{0:T(128)} %bitcast.flag_ref, bf16[16,256,128]{2,1,0:T(8,128)(2,1)} %own_ref.1, bf16[8,256,128]{2,1,0:T(8,128)(2,1)} %copy-done.4, f32[2,128]{1,0:T(2,128)} %gain_ref.9, bf16[2,128,512]{2,1,0:T(8,128)(2,1)} %proj_ref.5), custom_call_target="tpu_custom_call" | custom-call | bytes 4194304 | tf_op jit(solution)/shard_map/project/pallas_call | solution.py:234
  19.3 7.4 %all-to-all-start = ((bf16[16,128,256]{2,1,0:T(8,128)(2,1)}), bf16[16,128,256]{2,1,0:T(8,128)(2,1)S(1)}, u32[]{:S(2)}, u32[]{:S(2)}) async-start(bf16[16,128,256]{2,1,0:T(8,128)(2,1)} %get-tuple-element.15), calls=%async_computation | async-start | bytes 2097152 | tf_op jit(solution)/shard_map/all_to_all | solution.py:209
  26.6 15.3 %collective-permute-done.2.other_ref = bf16[8,256,128]{2,1,0:T(8,128)(2,1)S(1)} collective-permute-done((bf16[8,256,128]{2,1,0:T(8,128)(2,1)S(1)}, bf16[8,256,128]{2,1,0:T(8,128)(2,1)S(1)}, u32[]{:S(2)}, u32[]{:S(2)}) %collective-permute-start.2) | collective-permute-done | bytes 524320 | tf_op jit(solution)/shard_map/ppermute | solution.py:195
  41.9 0.8 copy-done.6
  42.7 3.8 %project.3 = (bf16[8,256,128]{2,1,0:T(8,128)(2,1)}, bf16[16,128,256]{2,1,0:T(8,128)(2,1)}) custom-call(s32[1]{0:T(128)} %bitcast.flag_ref, bf16[8,256,128]{2,1,0:T(8,128)(2,1)} %copy-done.5, bf16[8,256,128]{2,1,0:T(8,128)(2,1)} %copy-done.6, f32[2,128]{1,0:T(2,128)} %gain_ref.9, bf16[2,128,512]{2,1,0:T(8,128)(2,1)} %proj_ref.5), custom_call_target="tpu_custom_call" | custom-call | flops 20000000000 | bytes 4194304 | tf_op jit(solution)/shard_map/project/pallas_call | solution.py:234
  46.6 22.5 %all_to_all.30.far_ref = bf16[16,128,256]{2,1,0:T(8,128)(2,1)} all-to-all(bf16[16,128,256]{2,1,0:T(8,128)(2,1)} %get-tuple-element.16), channel_id=1, replica_groups={{0,16,1,17,2,18,3,19,4,20,5,21,6,22,7,23},{24,8,25,9,26,10,27,11,28,12,..., dimensions={0} | all-to-all | bytes 2097152 | tf_op jit(solution)/shard_map/all_to_all | solution.py:209
  69.1 3.2 %outgoing.1 = bf16[16,8,16,256]{3,2,1,0:T(8,128)(2,1)} custom-call(s32[1]{0:T(128)} %bitcast.1.side_ref, bf16[16,128,256]{2,1,0:T(8,128)(2,1)} %copy-done.1, bf16[16,128,256]{2,1,0:T(8,128)(2,1)} %all_to_all.30.far_ref), custom_call_target="tpu_custom_call" | custom-call | tf_op jit(solution)/shard_map/outgoing/pallas_call | solution.py:256
  72.3 19.1 %all_to_all.31 = bf16[16,8,16,256]{3,2,1,0:T(8,128)(2,1)} all-to-all(bf16[16,8,16,256]{3,2,1,0:T(8,128)(2,1)} %outgoing.1), channel_id=1, replica_groups={{0,16,1,17,2,18,3,19,4,20,5,21,6,22,7,23},{24,8,25,9,26,10,27,11,28,12,..., dimensions={0} | all-to-all | bytes 2097152 | tf_op jit(solution)/shard_map/all_to_all | solution.py:209
  91.4 8.8 %combine_project.1 = (bf16[16,256,128]{2,1,0:T(8,128)(2,1)}, bf16[16,256,256]{2,1,0:T(8,128)(2,1)}) custom-call(bf16[8,256,128]{2,1,0:T(8,128)(2,1)} %get-tuple-element.13.near_ref, bf16[8,256,128]{2,1,0:T(8,128)(2,1)} %get-tuple-element.14.far_ref, bf16[16,128,256]{2,1,0:T(8,128)(2,1)} %bitcast.7, f32[2,128]{1,0:T(2,128)} %gain_ref.9, ...), custom_call_target="tpu_custom_call" | custom-call | tf_op jit(solution)/shard_map/combine_project/pallas_call | solution.py:266
  100.3 5.0 %all-to-all-start.3 = ((bf16[16,256,256]{2,1,0:T(8,128)(2,1)}), bf16[16,256,256]{2,1,0:T(8,128)(2,1)S(1)}, u32[]{:S(2)}, u32[]{:S(2)}) async-start(bf16[16,256,256]{2,1,0:T(8,128)(2,1)} %get-tuple-element.18), calls=%async_computation.3 | async-start | bytes 4194304 | tf_op jit(solution)/shard_map/all_to_all | solution.py:209
  105.2 25.9 %all-to-all-done.3 = bf16[16,256,256]{2,1,0:T(8,128)(2,1)S(1)} async-done(((bf16[16,256,256]{2,1,0:T(8,128)(2,1)}), bf16[16,256,256]{2,1,0:T(8,128)(2,1)S(1)}, u32[]{:S(2)}, u32[]{:S(2)}) %all-to-all-start.3) | async-done | bytes 2097184 | tf_op jit(solution)/shard_map/all_to_all | solution.py:209
  131.2 1.3 copy-done
  132.5 2.7 %incoming.2 = bf16[16,64,256]{2,1,0:T(8,128)(2,1)} custom-call(s32[1]{0:T(128)S(6)} %sub.8.side_ref, bf16[16,2,8,16,256]{4,3,2,1,0:T(8,128)(2,1)} %bitcast.5), custom_call_target="tpu_custom_call" | custom-call | tf_op jit(solution)/shard_map/incoming/pallas_call | solution.py:286
  135.2 6.5 %all-to-all-start.4 = ((bf16[16,64,256]{2,1,0:T(8,128)(2,1)}), bf16[16,64,256]{2,1,0:T(8,128)(2,1)S(1)}, u32[]{:S(2)}, u32[]{:S(2)}) async-start(bf16[16,64,256]{2,1,0:T(8,128)(2,1)} %incoming.2), calls=%async_computation.4 | async-start | bytes 1048576 | tf_op jit(solution)/shard_map/all_to_all | solution.py:209
  141.8 2.8 %incoming.3 = bf16[16,64,256]{2,1,0:T(8,128)(2,1)} custom-call(s32[1]{0:T(128)} %bitcast.1.side_ref, bf16[16,2,8,16,256]{4,3,2,1,0:T(8,128)(2,1)} %bitcast.6), custom_call_target="tpu_custom_call" | custom-call | tf_op jit(solution)/shard_map/incoming/pallas_call | solution.py:286
  144.5 5.2 %all-to-all-done.4.got_ref = bf16[16,64,256]{2,1,0:T(8,128)(2,1)S(1)} async-done(((bf16[16,64,256]{2,1,0:T(8,128)(2,1)}), bf16[16,64,256]{2,1,0:T(8,128)(2,1)S(1)}, u32[]{:S(2)}, u32[]{:S(2)}) %all-to-all-start.4) | async-done | bytes 524320 | tf_op jit(solution)/shard_map/all_to_all | solution.py:209
  149.7 4.7 %all-to-all-start.5 = ((bf16[16,64,256]{2,1,0:T(8,128)(2,1)}), bf16[16,64,256]{2,1,0:T(8,128)(2,1)S(1)}, u32[]{:S(2)}, u32[]{:S(2)}) async-start(bf16[16,64,256]{2,1,0:T(8,128)(2,1)} %incoming.3), calls=%async_computation.5 | async-start | bytes 1048576 | tf_op jit(solution)/shard_map/all_to_all | solution.py:209
  154.5 6.8 %combine_transition.3 = bf16[8,256,128]{2,1,0:T(8,128)(2,1)} custom-call(bf16[16,256,128]{2,1,0:T(8,128)(2,1)} %get-tuple-element.17.pair_ref, bf16[16,64,256]{2,1,0:T(8,128)(2,1)} %copy-done.3, f32[2,128]{1,0:T(2,128)} %gain_ref.9, bf16[2,128,128]{2,1,0:T(8,128)(2,1)} %gate_ref.5, f32[2,128]{1,0:T(2,128)} %mid_gain_ref.5, bf16[2,128,128]{2,1,0:T(8,128)(2,1)} %out_ref.5, ...), custom_call_target="tpu_custom_call" | custom-call | tf_op jit(solution)/shard_map/combine_transition/pallas_call | solution.py:296
  161.3 1.3 collective-permute-start.3
  162.6 3.5 %collective-permute-start.5 = (bf16[8,256,128]{2,1,0:T(8,128)(2,1)}, bf16[8,256,128]{2,1,0:T(8,128)(2,1)S(1)}, u32[]{:S(2)}, u32[]{:S(2)}) collective-permute-start(bf16[8,256,128]{2,1,0:T(8,128)(2,1)} %combine_transition.3), channel_id=1, source_target_pairs={{8,16},{9,17},{10,18},{11,19},{12,20},{13,21},{14,22},{15,23},{16,... | collective-permute-start | bytes 1572872 | tf_op jit(solution)/shard_map/ppermute | solution.py:195
  166.1 0.8 copy-done.2
  166.9 6.8 %combine_transition.2 = bf16[8,256,128]{2,1,0:T(8,128)(2,1)} custom-call(bf16[16,256,128]{2,1,0:T(8,128)(2,1)} %get-tuple-element.17.pair_ref, bf16[16,64,256]{2,1,0:T(8,128)(2,1)} %copy-done.2, f32[2,128]{1,0:T(2,128)} %gain_ref.9, bf16[2,128,128]{2,1,0:T(8,128)(2,1)} %gate_ref.5, f32[2,128]{1,0:T(2,128)} %mid_gain_ref.5, bf16[2,128,128]{2,1,0:T(8,128)(2,1)} %out_ref.5, ...), custom_call_target="tpu_custom_call" | custom-call | tf_op jit(solution)/shard_map/combine_transition/pallas_call | solution.py:296
  173.7 1.6 collective-permute-start.4
  175.3 14.0 %collective-permute-done.3 = bf16[8,256,128]{2,1,0:T(8,128)(2,1)S(1)} collective-permute-done((bf16[8,256,128]{2,1,0:T(8,128)(2,1)}, bf16[8,256,128]{2,1,0:T(8,128)(2,1)S(1)}, u32[]{:S(2)}, u32[]{:S(2)}) %collective-permute-start.3) | collective-permute-done | bytes 524320 | tf_op jit(solution)/shard_map/ppermute | solution.py:195
  189.3 0.1 broadcast_select_fusion.1
  189.4 2.1 %collective-permute-done.5 = bf16[8,256,128]{2,1,0:T(8,128)(2,1)S(1)} collective-permute-done((bf16[8,256,128]{2,1,0:T(8,128)(2,1)}, bf16[8,256,128]{2,1,0:T(8,128)(2,1)S(1)}, u32[]{:S(2)}, u32[]{:S(2)}) %collective-permute-start.5) | collective-permute-done | bytes 524320 | tf_op jit(solution)/shard_map/ppermute | solution.py:195
  191.6 1.1 pad_maximum_fusion
  (16 shorter events, 0.1 us)
Async XLA Ops:
  1.3 12.9 %collective-permute-start = (bf16[8,256,128]{2,1,0:T(8,128)(2,1)S(1)}, bf16[8,256,128]{2,1,0:T(8,128)(2,1)S(1)}, u32[]{:S(2)}, u32[]{:S(2)}) collective-permute-start(bf16[8,256,128]{2,1,0:T(8,128)(2,1)S(1)} %get-tuple-element.22), channel_id=1, source_target_pairs={{0,16},{1,17},{2,18},{3,19},{4,20},{5,21},{6,22},{7,23},{8,24},{9,... | collective-permute-start | bytes 1572872 | tf_op jit(solution)/shard_map/ppermute | solution.py:195
  2.6 24.1 %collective-permute-start.1 = (bf16[8,256,128]{2,1,0:T(8,128)(2,1)S(1)}, bf16[8,256,128]{2,1,0:T(8,128)(2,1)S(1)}, u32[]{:S(2)}, u32[]{:S(2)}) collective-permute-start(bf16[8,256,128]{2,1,0:T(8,128)(2,1)S(1)} %get-tuple-element.21), channel_id=1, source_target_pairs={{8,0},{9,1},{10,2},{11,3},{12,4},{13,5},{14,6},{15,7},{16,24},{17,... | collective-permute-start | bytes 1572872 | tf_op jit(solution)/shard_map/ppermute | solution.py:195
  14.1 1.3 copy-start.4
  14.1 27.8 %collective-permute-start.2 = (bf16[8,256,128]{2,1,0:T(8,128)(2,1)S(1)}, bf16[8,256,128]{2,1,0:T(8,128)(2,1)S(1)}, u32[]{:S(2)}, u32[]{:S(2)}) collective-permute-start(bf16[8,256,128]{2,1,0:T(8,128)(2,1)S(1)} %collective-permute-done.other_ref), channel_id=1, source_target_pairs={{0,8},{1,9},{2,10},{3,11},{4,12},{5,13},{6,14},{7,15},{24,16},{25,... | collective-permute-start | bytes 1572872 | tf_op jit(solution)/shard_map/ppermute | solution.py:195
  19.3 27.3 %all-to-all-start = ((bf16[16,128,256]{2,1,0:T(8,128)(2,1)}), bf16[16,128,256]{2,1,0:T(8,128)(2,1)S(1)}, u32[]{:S(2)}, u32[]{:S(2)}) async-start(bf16[16,128,256]{2,1,0:T(8,128)(2,1)} %get-tuple-element.15), calls=%async_computation | async-start | bytes 2097152 | tf_op jit(solution)/shard_map/all_to_all | solution.py:209
  26.6 15.3 %copy-start.5 = (bf16[8,256,128]{2,1,0:T(8,128)(2,1)}, bf16[8,256,128]{2,1,0:T(8,128)(2,1)S(1)}, u32[]{:S(2)}) copy-start(bf16[8,256,128]{2,1,0:T(8,128)(2,1)S(1)} %collective-permute-done.1.own_ref) | copy-start | bytes 1572868
  41.9 0.8 copy-start.6
  46.5 22.5 %copy-start.1 = (bf16[16,128,256]{2,1,0:T(8,128)(2,1)}, bf16[16,128,256]{2,1,0:T(8,128)(2,1)S(1)}, u32[]{:S(2)}) copy-start(bf16[16,128,256]{2,1,0:T(8,128)(2,1)S(1)} %all-to-all-done.near_ref) | copy-start | bytes 3145732
  100.3 30.9 %all-to-all-start.3 = ((bf16[16,256,256]{2,1,0:T(8,128)(2,1)}), bf16[16,256,256]{2,1,0:T(8,128)(2,1)S(1)}, u32[]{:S(2)}, u32[]{:S(2)}) async-start(bf16[16,256,256]{2,1,0:T(8,128)(2,1)} %get-tuple-element.18), calls=%async_computation.3 | async-start | bytes 4194304 | tf_op jit(solution)/shard_map/all_to_all | solution.py:209
  131.2 1.3 copy-start
  135.2 14.5 %all-to-all-start.4 = ((bf16[16,64,256]{2,1,0:T(8,128)(2,1)}), bf16[16,64,256]{2,1,0:T(8,128)(2,1)S(1)}, u32[]{:S(2)}, u32[]{:S(2)}) async-start(bf16[16,64,256]{2,1,0:T(8,128)(2,1)} %incoming.2), calls=%async_computation.4 | async-start | bytes 1048576 | tf_op jit(solution)/shard_map/all_to_all | solution.py:209
  149.7 4.7 %copy-start.3 = (bf16[16,64,256]{2,1,0:T(8,128)(2,1)}, bf16[16,64,256]{2,1,0:T(8,128)(2,1)S(1)}, u32[]{:S(2)}) copy-start(bf16[16,64,256]{2,1,0:T(8,128)(2,1)S(1)} %all-to-all-done.4.got_ref) | copy-start | bytes 1572868
  149.7 16.4 %all-to-all-start.5 = ((bf16[16,64,256]{2,1,0:T(8,128)(2,1)}), bf16[16,64,256]{2,1,0:T(8,128)(2,1)S(1)}, u32[]{:S(2)}, u32[]{:S(2)}) async-start(bf16[16,64,256]{2,1,0:T(8,128)(2,1)} %incoming.3), calls=%async_computation.5 | async-start | bytes 1048576 | tf_op jit(solution)/shard_map/all_to_all | solution.py:209
  161.3 28.0 %collective-permute-start.3 = (bf16[8,256,128]{2,1,0:T(8,128)(2,1)}, bf16[8,256,128]{2,1,0:T(8,128)(2,1)S(1)}, u32[]{:S(2)}, u32[]{:S(2)}) collective-permute-start(bf16[8,256,128]{2,1,0:T(8,128)(2,1)} %combine_transition.3), channel_id=1, source_target_pairs={{0,8},{1,9},{2,10},{3,11},{4,12},{5,13},{6,14},{7,15},{24,16},{25,... | collective-permute-start | bytes 1572872 | tf_op jit(solution)/shard_map/ppermute | solution.py:195
  162.6 28.9 %collective-permute-start.5 = (bf16[8,256,128]{2,1,0:T(8,128)(2,1)}, bf16[8,256,128]{2,1,0:T(8,128)(2,1)S(1)}, u32[]{:S(2)}, u32[]{:S(2)}) collective-permute-start(bf16[8,256,128]{2,1,0:T(8,128)(2,1)} %combine_transition.3), channel_id=1, source_target_pairs={{8,16},{9,17},{10,18},{11,19},{12,20},{13,21},{14,22},{15,23},{16,... | collective-permute-start | bytes 1572872 | tf_op jit(solution)/shard_map/ppermute | solution.py:195
  166.1 0.8 copy-start.2
  173.7 17.8 %collective-permute-start.4 = (bf16[8,256,128]{2,1,0:T(8,128)(2,1)}, bf16[8,256,128]{2,1,0:T(8,128)(2,1)S(1)}, u32[]{:S(2)}, u32[]{:S(2)}) collective-permute-start(bf16[8,256,128]{2,1,0:T(8,128)(2,1)} %combine_transition.2), channel_id=1, source_target_pairs={{8,24},{9,25},{10,26},{11,27},{12,28},{13,29},{14,30},{15,31},{16,... | collective-permute-start | bytes 1572872 | tf_op jit(solution)/shard_map/ppermute | solution.py:195

commit v2 on v1

v2 whole, which is shorter than its diff:
```python
import functools

import jax
import jax.numpy as jnp
from jax import lax
from jax.experimental import pallas as pl
from jax.experimental.pallas import tpu as pltpu
from jax.sharding import PartitionSpec as P


epsilon = 1e-05
LANES = 128
VMEM_BYTES = 24 * 1024 * 1024
DIAGONAL = 0
FAR_FLOPS = 20_000_000_000
AXES = ("groups", "seq", "role")


def sigmoid(values):
    return 0.5 * jnp.tanh(0.5 * values) + 0.5


def norm_lanes(values, gain):
    average = jnp.mean(values, axis=-1, keepdims=True)
    centred = values - average
    spread = jnp.mean(centred * centred, axis=-1, keepdims=True)
    return (centred * lax.rsqrt(spread + epsilon) * gain).astype(jnp.bfloat16)


def dot(a, b, contract):
    return lax.dot_general(
        a, b, ((contract[:1], contract[1:]), ((), ())), preferred_element_type=jnp.float32
    )


def column_blocks(width):
    return [slice(start, start + LANES) for start in range(0, width, LANES)]


def project(normed, proj_ref, which, sent_ref, columns, scratch_ref, rows):
    parts, block, _ = sent_ref.shape
    lanes = LANES
    inner = proj_ref.shape[2] // 4
    half = block // 2
    for side in range(2):
        base = 2 * side * inner
        value = dot(proj_ref[which, :, base : base + inner], normed, (0, 1))
        gate = dot(proj_ref[which, :, base + inner : base + 2 * inner], normed, (0, 1))
        value = value * sigmoid(gate)
        for row in range(rows):
            scratch_ref[pl.ds(row, inner, stride=rows), :] = value[:, row * lanes : (row + 1) * lanes]
        sent_ref[:, side * half : (side + 1) * half, columns] = (
            scratch_ref[: inner * rows].reshape(parts, half, lanes).astype(jnp.bfloat16)
        )


def combine(pair, rows, which, gain_ref, gate_ref, mid_gain_ref, out_ref, got, scratch_ref):
    lanes = got.shape[2]
    inner = out_ref.shape[1]
    got = got.astype(jnp.float32).reshape(inner, rows, lanes)
    average = jnp.mean(got, axis=0, keepdims=True)
    centred = got - average
    spread = jnp.mean(centred * centred, axis=0, keepdims=True)
    scratch_ref[: inner * rows] = (centred * lax.rsqrt(spread + epsilon)).reshape(
        inner * rows, lanes
    )
    normed = norm_lanes(pair, gain_ref[which : which + 1])
    gating = sigmoid(dot(normed, gate_ref[which], (1, 0)))
    mid_gain = jnp.broadcast_to(mid_gain_ref[which : which + 1], (lanes, inner)).T
    updates = []
    for row in range(rows):
        mid = (scratch_ref[pl.ds(row, inner, stride=rows), :] * mid_gain).astype(jnp.bfloat16)
        updates.append(dot(mid, out_ref[which], (0, 0)))
    update = jnp.concatenate(updates, axis=0)
    return (pair + gating * update).astype(jnp.bfloat16)


def flat(pair):
    rows, lanes, channels = pair.shape
    return pair.astype(jnp.float32).reshape(rows * lanes, channels)


def first_kernel(flag_ref, own_ref, gain_ref, proj_ref, *refs):
    other_refs, (pair_ref, sent_ref, scratch_ref) = refs[:-3], refs[-3:]
    rows, width, _ = pair_ref.shape
    for columns in column_blocks(width):
        other = jnp.concatenate([flat(ref[:, columns]) for ref in other_refs], axis=0)
        pair = jnp.where(flag_ref[0] == 1, flat(own_ref[:rows, columns]), other)
        pair_ref[:, columns] = pair.astype(jnp.bfloat16).reshape(rows, LANES, -1)
        normed = norm_lanes(pair, gain_ref[0:1])
        project(normed, proj_ref, 0, sent_ref, columns, scratch_ref, rows)


def middle_kernel(
    near_ref, far_ref, got_ref, gain_ref, gate_ref, mid_gain_ref, out_ref, proj_ref,
    pair_out_ref, sent_ref, scratch_ref,
):
    rows, width, _ = pair_out_ref.shape
    for columns in column_blocks(width):
        pair = jnp.concatenate([flat(near_ref[:, columns]), flat(far_ref[:, columns])], axis=0)
        current = combine(
            pair, rows, 0, gain_ref, gate_ref, mid_gain_ref, out_ref, got_ref[:, :, columns],
            scratch_ref,
        )
        pair_out_ref[:, columns] = current.reshape(rows, LANES, -1)
        normed = norm_lanes(current.astype(jnp.float32), gain_ref[1:2])
        project(normed, proj_ref, 1, sent_ref, columns, scratch_ref, rows)


def last_kernel(
    slot, pair_ref, got_ref, gain_ref, gate_ref, mid_gain_ref, out_ref, trans_gain_ref, up_ref,
    down_ref, pair_out_ref, scratch_ref,
):
    rows, width, _ = pair_out_ref.shape
    hidden_width = down_ref.shape[0]
    block = min(hidden_width, 2 * LANES)
    size = got_ref.shape[1] // 2
    for columns in column_blocks(width):
        got = got_ref[:, slot * size : (slot + 1) * size, columns]
        current = combine(
            flat(pair_ref[slot * rows : (slot + 1) * rows, columns]), rows, 1,
            gain_ref, gate_ref, mid_gain_ref, out_ref, got, scratch_ref,
        ).astype(jnp.float32)
        normed = norm_lanes(current, trans_gain_ref[...])
        total = current
        for start in range(0, hidden_width, block):
            stop = start + block
            gate = dot(normed, up_ref[:, start:stop], (1, 0))
            value = dot(normed, up_ref[:, hidden_width + start : hidden_width + stop], (1, 0))
            hidden = (gate * sigmoid(gate) * value).astype(jnp.bfloat16)
            total = total + dot(hidden, down_ref[start:stop], (1, 0))
        pair_out_ref[:, columns] = total.astype(jnp.bfloat16).reshape(rows, LANES, -1)


def outgoing_kernel(side_ref, near_ref, far_ref, sent_ref):
    parts, block, width = near_ref.shape
    per, rows = sent_ref.shape[1], sent_ref.shape[2] // 2
    count = parts * rows
    side = side_ref[0]
    slots = [
        ref[...].astype(jnp.float32).reshape(parts, 2, per, rows, width)
        for ref in (near_ref, far_ref)
    ]
    for item in range(per):
        left, right = [
            [slot[:, which, item].reshape(count, width).astype(jnp.bfloat16) for slot in slots]
            for which in range(2)
        ]
        left = jnp.concatenate(left, axis=0)
        for slot in range(2):
            place = jnp.where(side == 0, slot, 1 - slot)
            part = dot(left, right[slot], (1, 1)).reshape(2, parts, rows, count)
            sent_ref[:, item, :, pl.ds(pl.multiple_of(place * count, LANES), count)] = (
                jnp.concatenate([part[0], part[1]], axis=1).astype(jnp.bfloat16)
            )


def incoming_kernel(side_ref, got_ref, sent_ref):
    parts, _, per, rows, width = got_ref.shape
    half = width // 2
    own = rows // 2
    for item in range(per):
        right = got_ref[:, 1, item].reshape(parts * rows, width)
        for slot in range(2):
            side = side_ref[0] if slot == 0 else 1 - side_ref[0]
            place = pl.ds(pl.multiple_of(side * half, LANES), half)
            left = got_ref[:, 0, item, :, place].reshape(parts * rows, half)
            start = (slot * per + item) * own
            sent_ref[:, start : start + own] = (
                dot(left, right, (0, 0)).reshape(parts, own, width).astype(jnp.bfloat16)
            )


def join_kernel(top_ref, bottom_ref, out_ref):
    rows = top_ref.shape[0]
    out_ref[:rows] = top_ref[...]
    out_ref[rows:] = bottom_ref[...]


def pick_kernel(flag_ref, top_ref, bottom_ref, far_ref, out_ref):
    rows = top_ref.shape[0]

    @pl.when(flag_ref[0] == 1)
    def _():
        out_ref[:rows] = top_ref[...]
        out_ref[rows:] = bottom_ref[...]

    @pl.when(flag_ref[0] == 0)
    def _():
        out_ref[...] = far_ref[...]


def call(kernel, name, out_shape, scratch, *operands, flops=0):
    vmem = pl.BlockSpec(memory_space=pltpu.VMEM)
    smem = pl.BlockSpec(memory_space=pltpu.SMEM)
    several = isinstance(out_shape, (list, tuple))
    return pl.pallas_call(
        kernel,
        in_specs=[smem if operand.dtype == jnp.int32 else vmem for operand in operands],
        out_specs=[vmem] * len(out_shape) if several else vmem,
        out_shape=out_shape,
        scratch_shapes=scratch,
        compiler_params=pltpu.CompilerParams(vmem_limit_bytes=VMEM_BYTES),
        cost_estimate=pl.CostEstimate(flops=flops, bytes_accessed=0, transcendentals=0),
        name=name,
    )(*operands)


def after(value, earlier):
    return lax.optimization_barrier((value, earlier))[0]


def local(
    pair_rep, tri_gain, tri_proj, tri_gate, tri_mid_gain, tri_out, trans_gain, trans_up, trans_down
):
    rows, width, channels = pair_rep.shape
    inner = tri_out.shape[1]
    groups, seq, role = (lax.axis_size(axis) for axis in AXES)
    half_seq = seq // 2
    parts = seq * role
    per = inner // parts
    own = rows // 2

    def number(g, s, c):
        return (g * seq + s) * role + c

    every = [(g, s, c) for g in range(groups) for s in range(seq) for c in range(role)]

    def at_home(g, s):
        return s // half_seq == g % 2

    def across(s):
        return (s + half_seq) % seq

    def permute(value, pairs):
        return lax.ppermute(value, AXES, [(number(*a), number(*b)) for a, b in pairs])

    blocks = [
        [
            number(base + u, side * half_seq + s, c)
            for s in range(half_seq)
            for c in range(role)
            for u in (side, 1 - side)
        ]
        for base in range(0, groups, 2)
        for side in range(2)
    ]

    def exchange(value):
        return lax.all_to_all(
            value, AXES, split_axis=0, concat_axis=0, tiled=True, axis_index_groups=blocks
        )

    side = lax.axis_index("seq") // half_seq
    home = side == lax.axis_index("groups") % 2
    side_flag = side.astype(jnp.int32).reshape(1)
    other_side_flag = 1 - side_flag
    home_flag = home.astype(jnp.int32).reshape(1)

    low, high = pair_rep[:own], pair_rep[own:]
    hopped = permute(high, [((g, s, c), (g ^ 1, s, c)) for g, s, c in every])
    direct = permute(low, [((g, s, c), (g, across(s), c)) for g, s, c in every if not at_home(g, s)])
    cut = own * DIAGONAL // 8
    diagonal = permute(
        high[:cut],
        [((g, s, c), (g ^ 1, across(s), c)) for g, s, c in every if not at_home(g, s)],
    )
    relayed = permute(hopped[cut:], [((g, s, c), (g, across(s), c)) for g, s, c in every if at_home(g, s)])

    scratch = [pltpu.VMEM((inner * rows, LANES), jnp.float32)]

    def shape(*dims):
        return jax.ShapeDtypeStruct(dims, jnp.bfloat16)

    def first(own_rows, other_rows, flops):
        return call(
            first_kernel, "project",
            [shape(own, width, channels), shape(parts, 2 * per * own, width)], scratch,
            home_flag, own_rows, tri_gain, tri_proj, *other_rows, flops=flops,
        )

    near, near_sent = first(low, [hopped], 0)
    near_got = exchange(near_sent)
    far, far_sent = first(direct, [relayed], FAR_FLOPS)
    far_got = exchange(far_sent)

    product = call(
        outgoing_kernel, "outgoing", shape(parts, per, rows, width), [],
        side_flag, near_got, far_got,
    )
    back = exchange(product).reshape(parts, per * rows, width)

    current, sent = call(
        middle_kernel, "combine_project",
        [shape(rows, width, channels), shape(parts, 2 * per * rows, width)], scratch,
        near, far, back, tri_gain, tri_gate, tri_mid_gain, tri_out, tri_proj,
    )
    got = exchange(sent).reshape(parts, 2, per, rows, width)

    product = call(
        incoming_kernel, "incoming", shape(parts, per * rows, width), [], side_flag, got
    )
    back = exchange(product)

    def last(slot, back, flops):
        return call(
            functools.partial(last_kernel, slot), "combine_transition",
            shape(own, width, channels), scratch,
            current, back, tri_gain, tri_gate, tri_mid_gain, tri_out, trans_gain[None],
            trans_up, trans_down, flops=flops,
        )

    far_out = last(1, back, 0)
    near_out = last(0, after(back, far_out), FAR_FLOPS)

    from_home = permute(
        far_out, [((g, s, c), (g, across(s), c)) for g, s, c in every if at_home(g, s)]
    )
    from_away = permute(
        far_out, [((g, s, c), (g ^ 1, across(s), c)) for g, s, c in every if not at_home(g, s)]
    )
    from_near = permute(
        near_out, [((g, s, c), (g ^ 1, s, c)) for g, s, c in every if not at_home(g, s)]
    )
    far = call(join_kernel, "join", shape(rows, width, channels), [], from_home, from_away)
    return call(pick_kernel, "pick", shape(rows, width, channels), [], home_flag, near_out, from_near, far, flops=0)


def solution(mesh):
    in_specs = (P(AXES, None, None), P(), P(), P(), P(), P(), P(), P(), P())
    out_specs = P(AXES, None, None)
    return jax.shard_map(local, mesh=mesh, in_specs=in_specs, out_specs=out_specs, check_vma=False)
```

time: 194 us -> 178 us (0.918)
  blocking collectives: 41.6 us -> 86.8 us
  waiting for transfers between devices: 72.1 us -> 42.7 us
  Pallas kernels: 38.8 us -> 21.8 us
  starting transfers between devices: 34.6 us -> 22 us
    all_to_all x2 -> x4, blocking collectives: 41.6 us -> 86.8 us  [exchange(): lax.all_to_all(value, AXES, split_axis=0, concat_axis=0, tiled=True, axis...]
    all_to_all x4 -> x1, waiting for transfers between devices: 31.1 us -> 0.01 us  [exchange(): lax.all_to_all(value, AXES, split_axis=0, concat_axis=0, tiled=True, axis...]
    pallas_call x8 -> x9, Pallas kernels: 38.8 us -> 21.8 us  [call(): pl.pallas_call(kernel, in_specs=[smem if operand.dtype == jnp.int32 else...]
    all_to_all x4 -> x1, starting transfers between devices: 23.6 us -> 8.1 us  [exchange(): lax.all_to_all(value, AXES, split_axis=0, concat_axis=0, tiled=True, axis...]
    ppermute x6, starting transfers between devices: 11 us -> 13.9 us  [permute(): lax.ppermute(value, AXES, [(number(*a), number(*b)) for a, b in pairs])]
  transfers between devices with their start and end apart: 10 -> 7, of which waited for: 6 -> 4; matrix products, arithmetic and copies ran while one was open for 0% -> 0% of each run, Pallas kernels for 12% -> 5%
where the time goes in v2:
time: 178 us; the launch traced here: 177 us
  blocking collectives  86.8 us (49%)
  waiting for transfers between devices  42.7 us (24%)
  starting transfers between devices  22 us (12%)
  Pallas kernels  21.8 us (12%)
  local copies, waits for them, and re-layouts  3.16 us (2%)
    all_to_all x4, blocking collectives, exchange(): lax.all_to_all(value, AXES, split_axis=0, concat_axis=0, tiled=True, axis...  86.8 us
    ppermute x6, waiting for transfers between devices, permute(): lax.ppermute(value, AXES, [(number(*a), number(*b)) for a, b in pairs])  42.7 us
    pallas_call x9, Pallas kernels, call(): pl.pallas_call(kernel, in_specs=[smem if operand.dtype == jnp.int32 else...  21.8 us
    ppermute x6, starting transfers between devices, permute(): lax.ppermute(value, AXES, [(number(*a), number(*b)) for a, b in pairs])  13.9 us
    all_to_all x1, starting transfers between devices, exchange(): lax.all_to_all(value, AXES, split_axis=0, concat_axis=0, tiled=True, axis...  8.1 us
  transfers between devices with their start and end apart: 7, of which 4 were waited for; matrix products, arithmetic and copies ran while one was open for 0% of the time, Pallas kernels for 5%

profile of v2, /device:TPU:25, one launch (start us, length us, event | category | flops | bytes accessed | tf_op | source)
XLA Modules:
  0.0 176.6 jit_solution(2084038379329212149)
XLA Ops:
  0.0 1.3 fusion
  1.3 1.3 collective-permute-start
  2.6 2.0 %collective-permute-start.1 = (bf16[8,256,128]{2,1,0:T(8,128)(2,1)S(1)}, bf16[8,256,128]{2,1,0:T(8,128)(2,1)S(1)}, u32[]{:S(2)}, u32[]{:S(2)}) collective-permute-start(bf16[8,256,128]{2,1,0:T(8,128)(2,1)S(1)} %get-tuple-element.20.own_ref), channel_id=1, source_target_pairs={{8,0},{9,1},{10,2},{11,3},{12,4},{13,5},{14,6},{15,7},{16,24},{17,... | collective-permute-start | bytes 1572872 | tf_op jit(solution)/shard_map/ppermute | solution.py:236
  4.6 9.6 %collective-permute-done.refs_0_ = bf16[8,256,128]{2,1,0:T(8,128)(2,1)S(1)} collective-permute-done((bf16[8,256,128]{2,1,0:T(8,128)(2,1)S(1)}, bf16[8,256,128]{2,1,0:T(8,128)(2,1)S(1)}, u32[]{:S(2)}, u32[]{:S(2)}) %collective-permute-start) | collective-permute-done | bytes 524320 | tf_op jit(solution)/shard_map/ppermute | solution.py:236
  14.2 1.3 collective-permute-start.2
  15.5 0.0 copy-done.5
  15.5 0.0 copy-done
  15.5 2.5 %project.2 = (bf16[8,256,128]{2,1,0:T(8,128)(2,1)S(1)}, bf16[16,128,256]{2,1,0:T(8,128)(2,1)}) custom-call(s32[1]{0:T(128)} %bitcast.flag_ref, bf16[8,256,128]{2,1,0:T(8,128)(2,1)S(1)} %get-tuple-element.20.own_ref, f32[2,128]{1,0:T(2,128)S(1)} %copy-done.5, bf16[2,128,512]{2,1,0:T(8,128)(2,1)S(1)} %copy-done, ...), custom_call_target="tpu_custom_call" | custom-call | tf_op jit(solution)/shard_map/project/pallas_call | solution.py:197
  18.1 8.1 %all-to-all-start = ((bf16[16,128,256]{2,1,0:T(8,128)(2,1)}), bf16[16,128,256]{2,1,0:T(8,128)(2,1)S(1)}, u32[]{:S(2)}, u32[]{:S(2)}) async-start(bf16[16,128,256]{2,1,0:T(8,128)(2,1)} %get-tuple-element.14), calls=%async_computation | async-start | bytes 2097152 | tf_op jit(solution)/shard_map/all_to_all | solution.py:250
  26.2 0.0 collective-permute-done.1.own_ref
  26.2 0.8 copy-done.8
  27.0 15.1 %collective-permute-done.2.refs_0_ = bf16[8,256,128]{2,1,0:T(8,128)(2,1)} collective-permute-done((bf16[8,256,128]{2,1,0:T(8,128)(2,1)S(1)}, bf16[8,256,128]{2,1,0:T(8,128)(2,1)}, u32[]{:S(2)}, u32[]{:S(2)}) %collective-permute-start.2) | collective-permute-done | bytes 524320 | tf_op jit(solution)/shard_map/ppermute | solution.py:236
  42.1 1.0 copy-done.9
  43.1 2.6 %project.3 = (bf16[8,256,128]{2,1,0:T(8,128)(2,1)S(1)}, bf16[16,128,256]{2,1,0:T(8,128)(2,1)S(1)}) custom-call(s32[1]{0:T(128)} %bitcast.flag_ref, bf16[8,256,128]{2,1,0:T(8,128)(2,1)S(1)} %copy-done.9, f32[2,128]{1,0:T(2,128)S(1)} %copy-done.5, bf16[2,128,512]{2,1,0:T(8,128)(2,1)S(1)} %copy-done, bf16[8,256,128]{2,1,0:T(8,128)(2,1)} %collective-permute-done.2.refs_0_), custom_call_target="tpu_custom_call" | custom-call | flops 20000000000 | tf_op jit(solution)/shard_map/project/pallas_call | solution.py:197
  45.8 0.0 all-to-all-done.near_ref
  45.8 22.5 %all_to_all.25.far_ref = bf16[16,128,256]{2,1,0:T(8,128)(2,1)S(1)} all-to-all(bf16[16,128,256]{2,1,0:T(8,128)(2,1)S(1)} %get-tuple-element.15), channel_id=1, replica_groups={{0,16,1,17,2,18,3,19,4,20,5,21,6,22,7,23},{24,8,25,9,26,10,27,11,28,12,..., dimensions={0} | all-to-all | bytes 2097152 | tf_op jit(solution)/shard_map/all_to_all | solution.py:250
  68.3 0.7 outgoing.1
  69.0 17.6 %all_to_all.26 = bf16[16,8,16,256]{3,2,1,0:T(8,128)(2,1)S(1)} all-to-all(bf16[16,8,16,256]{3,2,1,0:T(8,128)(2,1)S(1)} %outgoing.1), channel_id=1, replica_groups={{0,16,1,17,2,18,3,19,4,20,5,21,6,22,7,23},{24,8,25,9,26,10,27,11,28,12,..., dimensions={0} | all-to-all | bytes 2097152 | tf_op jit(solution)/shard_map/all_to_all | solution.py:250
  86.7 6.5 %combine_project.1 = (bf16[16,256,128]{2,1,0:T(8,128)(2,1)S(1)}, bf16[16,256,256]{2,1,0:T(8,128)(2,1)S(1)}) custom-call(bf16[8,256,128]{2,1,0:T(8,128)(2,1)S(1)} %get-tuple-element.12.near_ref, bf16[8,256,128]{2,1,0:T(8,128)(2,1)S(1)} %get-tuple-element.13.far_ref, bf16[16,128,256]{2,1,0:T(8,128)(2,1)S(1)} %bitcast.6, f32[2,128]{1,0:T(2,128)S(1)} %copy-done.5, ...), custom_call_target="tpu_custom_call" | custom-call | tf_op jit(solution)/shard_map/combine_project/pallas_call | solution.py:197
  93.2 28.9 %all_to_all.27 = bf16[16,256,256]{2,1,0:T(8,128)(2,1)S(1)} all-to-all(bf16[16,256,256]{2,1,0:T(8,128)(2,1)S(1)} %get-tuple-element.17), channel_id=1, replica_groups={{0,16,1,17,2,18,3,19,4,20,5,21,6,22,7,23},{24,8,25,9,26,10,27,11,28,12,..., dimensions={0} | all-to-all | bytes 4194304 | tf_op jit(solution)/shard_map/all_to_all | solution.py:250
  122.1 0.5 incoming.1
  122.6 17.7 %all_to_all.28.got_ref = bf16[16,128,256]{2,1,0:T(8,128)(2,1)S(1)} all-to-all(bf16[16,128,256]{2,1,0:T(8,128)(2,1)S(1)} %incoming.1), channel_id=1, replica_groups={{0,16,1,17,2,18,3,19,4,20,5,21,6,22,7,23},{24,8,25,9,26,10,27,11,28,12,..., dimensions={0} | all-to-all | bytes 2097152 | tf_op jit(solution)/shard_map/all_to_all | solution.py:250
  140.4 3.9 %combine_transition.2 = bf16[8,256,128]{2,1,0:T(8,128)(2,1)S(1)} custom-call(bf16[16,256,128]{2,1,0:T(8,128)(2,1)S(1)} %get-tuple-element.16.pair_ref, bf16[16,128,256]{2,1,0:T(8,128)(2,1)S(1)} %all_to_all.28.got_ref, f32[2,128]{1,0:T(2,128)S(1)} %copy-done.5, bf16[2,128,128]{2,1,0:T(8,128)(2,1)S(1)} %copy-done.2, f32[2,128]{1,0:T(2,128)S(1)} %copy-done.6, ...), custom_call_target="tpu_custom_call" | custom-call | tf_op jit(solution)/shard_map/combine_transition/pallas_call | solution.py:197
  144.3 3.4 %collective-permute-start.5 = (bf16[8,256,128]{2,1,0:T(8,128)(2,1)S(1)}, bf16[8,256,128]{2,1,0:T(8,128)(2,1)S(1)}, u32[]{:S(2)}, u32[]{:S(2)}) collective-permute-start(bf16[8,256,128]{2,1,0:T(8,128)(2,1)S(1)} %combine_transition.2), channel_id=1, source_target_pairs={{8,16},{9,17},{10,18},{11,19},{12,20},{13,21},{14,22},{15,23},{16,... | collective-permute-start | bytes 1572872 | tf_op jit(solution)/shard_map/ppermute | solution.py:236
  147.6 1.3 collective-permute-start.4
  148.9 3.9 %combine_transition.3.top_ref = bf16[8,256,128]{2,1,0:T(8,128)(2,1)S(1)} custom-call(bf16[16,256,128]{2,1,0:T(8,128)(2,1)S(1)} %get-tuple-element.16.pair_ref, bf16[16,128,256]{2,1,0:T(8,128)(2,1)S(1)} %all_to_all.28.got_ref, f32[2,128]{1,0:T(2,128)S(1)} %copy-done.5, bf16[2,128,128]{2,1,0:T(8,128)(2,1)S(1)} %copy-done.2, f32[2,128]{1,0:T(2,128)S(1)} %copy-done.6, ...), custom_call_target="tpu_custom_call" | custom-call | flops 20000000000 | tf_op jit(solution)/shard_map/combine_transition/pallas_call | solution.py:197
  152.8 4.7 %collective-permute-start.3 = (bf16[8,256,128]{2,1,0:T(8,128)(2,1)S(1)}, bf16[8,256,128]{2,1,0:T(8,128)(2,1)S(1)}, u32[]{:S(2)}, u32[]{:S(2)}) collective-permute-start(bf16[8,256,128]{2,1,0:T(8,128)(2,1)S(1)} %combine_transition.3.top_ref), channel_id=1, source_target_pairs={{8,24},{9,25},{10,26},{11,27},{12,28},{13,29},{14,30},{15,31},{16,... | collective-permute-start | bytes 1572872 | tf_op jit(solution)/shard_map/ppermute | solution.py:236
  157.5 15.5 %collective-permute-done.5.bottom_ref = bf16[8,256,128]{2,1,0:T(8,128)(2,1)S(1)} collective-permute-done((bf16[8,256,128]{2,1,0:T(8,128)(2,1)S(1)}, bf16[8,256,128]{2,1,0:T(8,128)(2,1)S(1)}, u32[]{:S(2)}, u32[]{:S(2)}) %collective-permute-start.5) | collective-permute-done | bytes 524320 | tf_op jit(solution)/shard_map/ppermute | solution.py:236
  173.0 2.5 %collective-permute-done.4.top_ref = bf16[8,256,128]{2,1,0:T(8,128)(2,1)S(1)} collective-permute-done((bf16[8,256,128]{2,1,0:T(8,128)(2,1)S(1)}, bf16[8,256,128]{2,1,0:T(8,128)(2,1)S(1)}, u32[]{:S(2)}, u32[]{:S(2)}) %collective-permute-start.4) | collective-permute-done | bytes 524320 | tf_op jit(solution)/shard_map/ppermute | solution.py:236
  175.5 0.1 join.1.far_ref
  175.6 0.0 collective-permute-done.3.bottom_ref
  175.6 1.1 pick.1
  (16 shorter events, 0.0 us)
Async XLA Ops:
  0.0 15.5 %copy-start.5 = (f32[2,128]{1,0:T(2,128)S(1)}, f32[2,128]{1,0:T(2,128)}, u32[]{:S(2)}) copy-start(f32[2,128]{1,0:T(2,128)} %gain_ref.9) | copy-start | bytes 3076
  0.0 15.5 %copy-start = (bf16[2,128,512]{2,1,0:T(8,128)(2,1)S(1)}, bf16[2,128,512]{2,1,0:T(8,128)(2,1)}, u32[]{:S(2)}) copy-start(bf16[2,128,512]{2,1,0:T(8,128)(2,1)} %proj_ref.5) | copy-start | bytes 786436
  1.3 12.9 %collective-permute-start = (bf16[8,256,128]{2,1,0:T(8,128)(2,1)S(1)}, bf16[8,256,128]{2,1,0:T(8,128)(2,1)S(1)}, u32[]{:S(2)}, u32[]{:S(2)}) collective-permute-start(bf16[8,256,128]{2,1,0:T(8,128)(2,1)S(1)} %get-tuple-element.19), channel_id=1, source_target_pairs={{0,16},{1,17},{2,18},{3,19},{4,20},{5,21},{6,22},{7,23},{8,24},{9,... | collective-permute-start | bytes 1572872 | tf_op jit(solution)/shard_map/ppermute | solution.py:236
  2.6 23.6 %collective-permute-start.1 = (bf16[8,256,128]{2,1,0:T(8,128)(2,1)S(1)}, bf16[8,256,128]{2,1,0:T(8,128)(2,1)S(1)}, u32[]{:S(2)}, u32[]{:S(2)}) collective-permute-start(bf16[8,256,128]{2,1,0:T(8,128)(2,1)S(1)} %get-tuple-element.20.own_ref), channel_id=1, source_target_pairs={{8,0},{9,1},{10,2},{11,3},{12,4},{13,5},{14,6},{15,7},{16,24},{17,... | collective-permute-start | bytes 1572872 | tf_op jit(solution)/shard_map/ppermute | solution.py:236
  14.2 27.9 %collective-permute-start.2 = (bf16[8,256,128]{2,1,0:T(8,128)(2,1)S(1)}, bf16[8,256,128]{2,1,0:T(8,128)(2,1)}, u32[]{:S(2)}, u32[]{:S(2)}) collective-permute-start(bf16[8,256,128]{2,1,0:T(8,128)(2,1)S(1)} %collective-permute-done.refs_0_), channel_id=1, source_target_pairs={{0,8},{1,9},{2,10},{3,11},{4,12},{5,13},{6,14},{7,15},{24,16},{25,... | collective-permute-start | bytes 1572872 | tf_op jit(solution)/shard_map/ppermute | solution.py:236
  18.1 27.7 %all-to-all-start = ((bf16[16,128,256]{2,1,0:T(8,128)(2,1)}), bf16[16,128,256]{2,1,0:T(8,128)(2,1)S(1)}, u32[]{:S(2)}, u32[]{:S(2)}) async-start(bf16[16,128,256]{2,1,0:T(8,128)(2,1)} %get-tuple-element.14), calls=%async_computation | async-start | bytes 2097152 | tf_op jit(solution)/shard_map/all_to_all | solution.py:250
  26.2 0.8 copy-start.8
  42.1 1.0 copy-start.9
  68.3 18.4 %copy-start.2 = (bf16[2,128,128]{2,1,0:T(8,128)(2,1)S(1)}, bf16[2,128,128]{2,1,0:T(8,128)(2,1)}, u32[]{:S(2)}) copy-start(bf16[2,128,128]{2,1,0:T(8,128)(2,1)} %gate_ref.5) | copy-start | bytes 196612
  68.3 18.4 %copy-start.3 = (bf16[2,128,128]{2,1,0:T(8,128)(2,1)S(1)}, bf16[2,128,128]{2,1,0:T(8,128)(2,1)}, u32[]{:S(2)}) copy-start(bf16[2,128,128]{2,1,0:T(8,128)(2,1)} %out_ref.5) | copy-start | bytes 196612
  68.3 18.4 %copy-start.6 = (f32[2,128]{1,0:T(2,128)S(1)}, f32[2,128]{1,0:T(2,128)}, u32[]{:S(2)}) copy-start(f32[2,128]{1,0:T(2,128)} %mid_gain_ref.5) | copy-start | bytes 3076
  122.1 18.3 %copy-start.1 = (bf16[128,1024]{1,0:T(8,128)(2,1)S(1)}, bf16[128,1024]{1,0:T(8,128)(2,1)}, u32[]{:S(2)}) copy-start(bf16[128,1024]{1,0:T(8,128)(2,1)} %up_ref.3) | copy-start | bytes 786436
  122.1 18.3 %copy-start.4 = (bf16[512,128]{1,0:T(8,128)(2,1)S(1)}, bf16[512,128]{1,0:T(8,128)(2,1)}, u32[]{:S(2)}) copy-start(bf16[512,128]{1,0:T(8,128)(2,1)} %down_ref.3) | copy-start | bytes 393220
  122.1 18.3 %copy-start.7 = (f32[128]{0:T(128)S(1)}, f32[128]{0:T(128)}, u32[]{:S(2)}) copy-start(f32[128]{0:T(128)} %param.15) | copy-start | bytes 1540
  144.3 28.8 %collective-permute-start.5 = (bf16[8,256,128]{2,1,0:T(8,128)(2,1)S(1)}, bf16[8,256,128]{2,1,0:T(8,128)(2,1)S(1)}, u32[]{:S(2)}, u32[]{:S(2)}) collective-permute-start(bf16[8,256,128]{2,1,0:T(8,128)(2,1)S(1)} %combine_transition.2), channel_id=1, source_target_pairs={{8,16},{9,17},{10,18},{11,19},{12,20},{13,21},{14,22},{15,23},{16,... | collective-permute-start | bytes 1572872 | tf_op jit(solution)/shard_map/ppermute | solution.py:236
  147.6 27.9 %collective-permute-start.4 = (bf16[8,256,128]{2,1,0:T(8,128)(2,1)S(1)}, bf16[8,256,128]{2,1,0:T(8,128)(2,1)S(1)}, u32[]{:S(2)}, u32[]{:S(2)}) collective-permute-start(bf16[8,256,128]{2,1,0:T(8,128)(2,1)S(1)} %combine_transition.2), channel_id=1, source_target_pairs={{0,8},{1,9},{2,10},{3,11},{4,12},{5,13},{6,14},{7,15},{24,16},{25,... | collective-permute-start | bytes 1572872 | tf_op jit(solution)/shard_map/ppermute | solution.py:236
  152.8 22.7 %collective-permute-start.3 = (bf16[8,256,128]{2,1,0:T(8,128)(2,1)S(1)}, bf16[8,256,128]{2,1,0:T(8,128)(2,1)S(1)}, u32[]{:S(2)}, u32[]{:S(2)}) collective-permute-start(bf16[8,256,128]{2,1,0:T(8,128)(2,1)S(1)} %combine_transition.3.top_ref), channel_id=1, source_target_pairs={{8,24},{9,25},{10,26},{11,27},{12,28},{13,29},{14,30},{15,31},{16,... | collective-permute-start | bytes 1572872 | tf_op jit(solution)/shard_map/ppermute | solution.py:236

commit v3 on v2

--- a/solution.py
+++ b/solution.py
@@ -11,18 +11,15 @@
 epsilon = 1e-05
 LANES = 128
 VMEM_BYTES = 24 * 1024 * 1024
-DIAGONAL = 0
+SHARES = (8, 1, 3, 4)
 FAR_FLOPS = 20_000_000_000
 AXES = ("groups", "seq", "role")
 
 
-def sigmoid(values):
-    return 0.5 * jnp.tanh(0.5 * values) + 0.5
-
-
 def norm_lanes(values, gain):
-    average = jnp.mean(values, axis=-1, keepdims=True)
-    centred = values - average
+    channels = values.shape[-1]
+    share = jnp.full((channels, channels), 1.0 / channels, jnp.bfloat16)
+    centred = values.astype(jnp.float32) - dot(values, share, (1, 0))
     spread = jnp.mean(centred * centred, axis=-1, keepdims=True)
     return (centred * lax.rsqrt(spread + epsilon) * gain).astype(jnp.bfloat16)
 
@@ -37,20 +34,19 @@
     return [slice(start, start + LANES) for start in range(0, width, LANES)]
 
 
-def project(normed, proj_ref, which, sent_ref, columns, scratch_ref, rows):
-    parts, block, _ = sent_ref.shape
+def project(normed, proj_ref, which, sent_ref, columns, rows, first=0):
+    parts = sent_ref.shape[0]
     lanes = LANES
     inner = proj_ref.shape[2] // 4
-    half = block // 2
+    half = inner // parts * rows
     for side in range(2):
         base = 2 * side * inner
-        value = dot(proj_ref[which, :, base : base + inner], normed, (0, 1))
-        gate = dot(proj_ref[which, :, base + inner : base + 2 * inner], normed, (0, 1))
-        value = value * sigmoid(gate)
-        for row in range(rows):
-            scratch_ref[pl.ds(row, inner, stride=rows), :] = value[:, row * lanes : (row + 1) * lanes]
-        sent_ref[:, side * half : (side + 1) * half, columns] = (
-            scratch_ref[: inner * rows].reshape(parts, half, lanes).astype(jnp.bfloat16)
+        both = dot(proj_ref[which, :, base : base + 2 * inner], normed, (0, 1))
+        value = (both[:inner] * jax.nn.sigmoid(both[inner:])).astype(jnp.bfloat16)
+        value = jnp.stack([value[:, row * lanes : (row + 1) * lanes] for row in range(rows)])
+        start = first + side * half
+        sent_ref[:, start : start + half, columns] = jnp.swapaxes(value, 0, 1).reshape(
+            parts, half, lanes
         )
 
 
@@ -65,30 +61,41 @@
         inner * rows, lanes
     )
     normed = norm_lanes(pair, gain_ref[which : which + 1])
-    gating = sigmoid(dot(normed, gate_ref[which], (1, 0)))
+    gating = jax.nn.sigmoid(dot(normed, gate_ref[which], (1, 0)))
     mid_gain = jnp.broadcast_to(mid_gain_ref[which : which + 1], (lanes, inner)).T
     updates = []
     for row in range(rows):
         mid = (scratch_ref[pl.ds(row, inner, stride=rows), :] * mid_gain).astype(jnp.bfloat16)
         updates.append(dot(mid, out_ref[which], (0, 0)))
     update = jnp.concatenate(updates, axis=0)
-    return (pair + gating * update).astype(jnp.bfloat16)
+    return (pair.astype(jnp.float32) + gating * update).astype(jnp.bfloat16)
 
 
 def flat(pair):
     rows, lanes, channels = pair.shape
-    return pair.astype(jnp.float32).reshape(rows * lanes, channels)
-
-
-def first_kernel(flag_ref, own_ref, gain_ref, proj_ref, *refs):
-    other_refs, (pair_ref, sent_ref, scratch_ref) = refs[:-3], refs[-3:]
+    return pair.reshape(rows * lanes, channels)
+
+
+def near_kernel(flag_ref, own_ref, gain_ref, proj_ref, *refs):
+    other_refs, (pair_ref, sent_ref) = refs[:-2], refs[-2:]
     rows, width, _ = pair_ref.shape
     for columns in column_blocks(width):
         other = jnp.concatenate([flat(ref[:, columns]) for ref in other_refs], axis=0)
         pair = jnp.where(flag_ref[0] == 1, flat(own_ref[:rows, columns]), other)
-        pair_ref[:, columns] = pair.astype(jnp.bfloat16).reshape(rows, LANES, -1)
-        normed = norm_lanes(pair, gain_ref[0:1])
-        project(normed, proj_ref, 0, sent_ref, columns, scratch_ref, rows)
+        pair_ref[:, columns] = pair.reshape(rows, LANES, -1)
+        project(norm_lanes(pair, gain_ref[0:1]), proj_ref, 0, sent_ref, columns, rows)
+
+
+def far_kernel(flag_ref, near_ref, own_ref, gain_ref, proj_ref, *refs):
+    other_refs, (pair_ref, sent_ref) = refs[:-2], refs[-2:]
+    rows, width, _ = pair_ref.shape
+    first = near_ref.shape[1]
+    sent_ref[:, :first] = near_ref[...]
+    for columns in column_blocks(width):
+        other = jnp.concatenate([flat(ref[:, columns]) for ref in other_refs], axis=0)
+        pair = jnp.where(flag_ref[0] == 1, flat(own_ref[:rows, columns]), other)
+        pair_ref[:, columns] = pair.reshape(rows, LANES, -1)
+        project(norm_lanes(pair, gain_ref[0:1]), proj_ref, 0, sent_ref, columns, rows, first)
 
 
 def middle_kernel(
@@ -103,8 +110,8 @@
             scratch_ref,
         )
         pair_out_ref[:, columns] = current.reshape(rows, LANES, -1)
-        normed = norm_lanes(current.astype(jnp.float32), gain_ref[1:2])
-        project(normed, proj_ref, 1, sent_ref, columns, scratch_ref, rows)
+        normed = norm_lanes(current, gain_ref[1:2])
+        project(normed, proj_ref, 1, sent_ref, columns, rows)
 
 
 def last_kernel(
@@ -120,26 +127,27 @@
         current = combine(
             flat(pair_ref[slot * rows : (slot + 1) * rows, columns]), rows, 1,
             gain_ref, gate_ref, mid_gain_ref, out_ref, got, scratch_ref,
-        ).astype(jnp.float32)
+        )
         normed = norm_lanes(current, trans_gain_ref[...])
-        total = current
+        total = current.astype(jnp.float32)
         for start in range(0, hidden_width, block):
             stop = start + block
             gate = dot(normed, up_ref[:, start:stop], (1, 0))
             value = dot(normed, up_ref[:, hidden_width + start : hidden_width + stop], (1, 0))
-            hidden = (gate * sigmoid(gate) * value).astype(jnp.bfloat16)
+            hidden = (gate * jax.nn.sigmoid(gate) * value).astype(jnp.bfloat16)
             total = total + dot(hidden, down_ref[start:stop], (1, 0))
         pair_out_ref[:, columns] = total.astype(jnp.bfloat16).reshape(rows, LANES, -1)
 
 
-def outgoing_kernel(side_ref, near_ref, far_ref, sent_ref):
-    parts, block, width = near_ref.shape
+def outgoing_kernel(side_ref, got_ref, sent_ref):
+    parts, block, width = got_ref.shape
+    block = block // 2
     per, rows = sent_ref.shape[1], sent_ref.shape[2] // 2
     count = parts * rows
     side = side_ref[0]
     slots = [
-        ref[...].astype(jnp.float32).reshape(parts, 2, per, rows, width)
-        for ref in (near_ref, far_ref)
+        part.astype(jnp.float32).reshape(parts, 2, per, rows, width)
+        for part in (got_ref[:, :block], got_ref[:, block:])
     ]
     for item in range(per):
         left, right = [
@@ -173,8 +181,8 @@
 
 def join_kernel(top_ref, bottom_ref, out_ref):
     rows = top_ref.shape[0]
-    out_ref[:rows] = top_ref[...]
-    out_ref[rows:] = bottom_ref[...]
+    out_ref[rows:] = top_ref[...]
+    out_ref[:rows] = bottom_ref[...]
 
 
 def pick_kernel(flag_ref, top_ref, bottom_ref, far_ref, out_ref):
@@ -188,6 +196,20 @@
     @pl.when(flag_ref[0] == 0)
     def _():
         out_ref[...] = far_ref[...]
+
+
+def split_kernel(pair_ref, *refs):
+    out_refs, sems = refs[:-1], refs[-1]
+    copies, start = [], 0
+    for place, out_ref in enumerate(out_refs):
+        height = out_ref.shape[0]
+        source = pair_ref.at[pl.ds(start, height)]
+        copies.append(pltpu.make_async_copy(source, out_ref, sems.at[place]))
+        start += height
+    for copy in copies:
+        copy.start()
+    for copy in copies:
+        copy.wait()
 
 
 def call(kernel, name, out_shape, scratch, *operands, flops=0):
@@ -257,36 +279,46 @@
     other_side_flag = 1 - side_flag
     home_flag = home.astype(jnp.int32).reshape(1)
 
-    low, high = pair_rep[:own], pair_rep[own:]
-    hopped = permute(high, [((g, s, c), (g ^ 1, s, c)) for g, s, c in every])
-    direct = permute(low, [((g, s, c), (g, across(s), c)) for g, s, c in every if not at_home(g, s)])
-    cut = own * DIAGONAL // 8
-    diagonal = permute(
-        high[:cut],
-        [((g, s, c), (g ^ 1, across(s), c)) for g, s, c in every if not at_home(g, s)],
-    )
-    relayed = permute(hopped[cut:], [((g, s, c), (g, across(s), c)) for g, s, c in every if at_home(g, s)])
-
-    scratch = [pltpu.VMEM((inner * rows, LANES), jnp.float32)]
-
     def shape(*dims):
         return jax.ShapeDtypeStruct(dims, jnp.bfloat16)
 
-    def first(own_rows, other_rows, flops):
-        return call(
-            first_kernel, "project",
-            [shape(own, width, channels), shape(parts, 2 * per * own, width)], scratch,
-            home_flag, own_rows, tri_gain, tri_proj, *other_rows, flops=flops,
-        )
-
-    near, near_sent = first(low, [hopped], 0)
-    near_got = exchange(near_sent)
-    far, far_sent = first(direct, [relayed], FAR_FLOPS)
-    far_got = exchange(far_sent)
+    heights = [own * share // 8 for share in SHARES]
+    away = [(g, s, c) for g, s, c in every if not at_home(g, s)]
+    low, middle, *high = pl.pallas_call(
+        split_kernel,
+        in_specs=[pl.BlockSpec(memory_space=pltpu.HBM)],
+        out_specs=[pl.BlockSpec(memory_space=pltpu.VMEM)] * len(heights),
+        out_shape=[shape(height, width, channels) for height in heights],
+        scratch_shapes=[pltpu.SemaphoreType.DMA((len(heights),))],
+        compiler_params=pltpu.CompilerParams(vmem_limit_bytes=VMEM_BYTES),
+        name="split",
+    )(pltpu.with_memory_space_constraint(pair_rep, pltpu.HBM))
+    hopped = [permute(part, [((g, s, c), (g ^ 1, s, c)) for g, s, c in every]) for part in high]
+    direct = permute(low, [((g, s, c), (g, across(s), c)) for g, s, c in away])
+    relayed = [
+        permute(part, [((g, s, c), (g, across(s), c)) for g, s, c in every if at_home(g, s)])
+        for part in hopped
+    ]
+    diagonal = permute(middle, [((g, s, c), (g ^ 1, across(s), c)) for g, s, c in away])
+    stepped = permute(middle, [((g, s, c), (g ^ 1, s, c)) for g, s, c in every if at_home(g, s)])
+
+    scratch = [pltpu.VMEM((inner * rows, LANES), jnp.float32)]
+
+    near, near_sent = call(
+        near_kernel, "project",
+        [shape(own, width, channels), shape(parts, 2 * per * own, width)], [],
+        home_flag, low, tri_gain, tri_proj, stepped, *hopped, flops=0,
+    )
+    far, sent = call(
+        far_kernel, "project",
+        [shape(own, width, channels), shape(parts, 2 * per * rows, width)], [],
+        home_flag, near_sent, direct, tri_gain, tri_proj, diagonal, *relayed,
+    )
+    got = exchange(sent)
 
     product = call(
         outgoing_kernel, "outgoing", shape(parts, per, rows, width), [],
-        side_flag, near_got, far_got,
+        side_flag, got,
     )
     back = exchange(product).reshape(parts, per * rows, width)
 
@@ -322,7 +354,7 @@
     from_near = permute(
         near_out, [((g, s, c), (g ^ 1, s, c)) for g, s, c in every if not at_home(g, s)]
     )
-    far = call(join_kernel, "join", shape(rows, width, channels), [], from_home, from_away)
+    far = call(join_kernel, "join", shape(rows, width, channels), [], from_away, from_home)
     return call(pick_kernel, "pick", shape(rows, width, channels), [], home_flag, near_out, from_near, far, flops=0)
 
 

time: 178 us -> 171 us (0.961)
  blocking collectives: 86.8 us -> 94.5 us
  starting transfers between devices: 22 us -> 15.2 us
  waiting for transfers between devices: 42.7 us -> 39.9 us
  Pallas kernels: 21.8 us -> 19.5 us
    all_to_all x1 -> x0, starting transfers between devices: 8.1 us -> none  [exchange(): lax.all_to_all(value, AXES, split_axis=0, concat_axis=0, tiled=True, axis...]
    all_to_all x4, blocking collectives: 86.8 us -> 94.5 us  [exchange(): lax.all_to_all(value, AXES, split_axis=0, concat_axis=0, tiled=True, axis...]
    pallas_call x9, Pallas kernels: 21.8 us -> 18.2 us  [call(): pl.pallas_call(kernel, in_specs=[smem if operand.dtype == jnp.int32 else...]
    ppermute x6 -> x10, waiting for transfers between devices: 42.7 us -> 39.9 us  [permute(): lax.ppermute(value, AXES, [(number(*a), number(*b)) for a, b in pairs])]
    ppermute x6 -> x10, starting transfers between devices: 13.9 us -> 15.2 us  [permute(): lax.ppermute(value, AXES, [(number(*a), number(*b)) for a, b in pairs])]
  transfers between devices with their start and end apart: 7 -> 10, of which waited for: 4 -> 7; matrix products, arithmetic and copies ran while one was open for 0% -> 0% of each run, Pallas kernels for 5% -> 3%
where the time goes in v3:
time: 171 us
  blocking collectives  94.5 us (55%)
  waiting for transfers between devices  39.9 us (23%)
  Pallas kernels  19.5 us (11%)
  starting transfers between devices  15.2 us (9%)
    all_to_all x4, blocking collectives, exchange(): lax.all_to_all(value, AXES, split_axis=0, concat_axis=0, tiled=True, axis...  94.5 us
    ppermute x10, waiting for transfers between devices, permute(): lax.ppermute(value, AXES, [(number(*a), number(*b)) for a, b in pairs])  39.9 us
    pallas_call x9, Pallas kernels, call(): pl.pallas_call(kernel, in_specs=[smem if operand.dtype == jnp.int32 else...  18.2 us
    ppermute x10, starting transfers between devices, permute(): lax.ppermute(value, AXES, [(number(*a), number(*b)) for a, b in pairs])  15.2 us
  transfers between devices with their start and end apart: 10, of which 7 were waited for; matrix products, arithmetic and copies ran while one was open for 0% of the time, Pallas kernels for 3%

profile of v3, /device:TPU:25, one launch (start us, length us, event | category | flops | bytes accessed | tf_op | source)
XLA Modules:
  0.0 170.9 jit_solution(6766074157666201296)
XLA Ops:
  0.0 1.3 split.1
  1.3 1.3 collective-permute-start.2
  2.6 2.0 %collective-permute-start.3 = (bf16[8,256,128]{2,1,0:T(8,128)(2,1)S(1)}, bf16[8,256,128]{2,1,0:T(8,128)(2,1)S(1)}, u32[]{:S(2)}, u32[]{:S(2)}) collective-permute-start(bf16[8,256,128]{2,1,0:T(8,128)(2,1)S(1)} %get-tuple-element.16.own_ref), channel_id=1, source_target_pairs={{8,0},{9,1},{10,2},{11,3},{12,4},{13,5},{14,6},{15,7},{16,24},{17,... | collective-permute-start | bytes 1572872 | tf_op jit(solution)/shard_map/ppermute | solution.py:258
  4.5 0.1 collective-permute-start.1
  4.6 3.9 %collective-permute-done.2.refs_2_ = bf16[4,256,128]{2,1,0:T(8,128)(2,1)S(1)} collective-permute-done((bf16[4,256,128]{2,1,0:T(8,128)(2,1)S(1)}, bf16[4,256,128]{2,1,0:T(8,128)(2,1)S(1)}, u32[]{:S(2)}, u32[]{:S(2)}) %collective-permute-start.2) | collective-permute-done | bytes 262176 | tf_op jit(solution)/shard_map/ppermute | solution.py:258
  8.5 1.3 collective-permute-start.6
  9.8 2.9 %collective-permute-done.1.refs_1_ = bf16[3,256,128]{2,1,0:T(8,128)(2,1)S(1)} collective-permute-done((bf16[3,256,128]{2,1,0:T(8,128)(2,1)S(1)}, bf16[3,256,128]{2,1,0:T(8,128)(2,1)S(1)}, u32[]{:S(2)}, u32[]{:S(2)}) %collective-permute-start.1) | collective-permute-done | bytes 196640 | tf_op jit(solution)/shard_map/ppermute | solution.py:258
  12.7 1.3 collective-permute-start.5
  14.0 1.3 collective-permute-start
  15.3 3.1 %collective-permute-start.4 = (bf16[1,256,128]{2,1,0:T(8,128)(2,1)S(1)}, bf16[1,256,128]{2,1,0:T(8,128)(2,1)S(1)}, u32[]{:S(2)}, u32[]{:S(2)}) collective-permute-start(bf16[1,256,128]{2,1,0:T(8,128)(2,1)S(1)} %get-tuple-element.17), channel_id=1, source_target_pairs={{8,16},{9,17},{10,18},{11,19},{12,20},{13,21},{14,22},{15,23},{16,... | collective-permute-start | bytes 196616 | tf_op jit(solution)/shard_map/ppermute | solution.py:258
  18.4 0.6 collective-permute-done.refs_0_
  19.0 0.9 copy-done
  20.0 0.7 copy-done.6
  20.7 1.4 project.2
  22.1 11.0 %collective-permute-done.4.refs_0_ = bf16[1,256,128]{2,1,0:T(8,128)(2,1)S(1)} collective-permute-done((bf16[1,256,128]{2,1,0:T(8,128)(2,1)S(1)}, bf16[1,256,128]{2,1,0:T(8,128)(2,1)S(1)}, u32[]{:S(2)}, u32[]{:S(2)}) %collective-permute-start.4) | collective-permute-done | bytes 65568 | tf_op jit(solution)/shard_map/ppermute | solution.py:258
  33.1 0.1 collective-permute-done.5.refs_1_
  33.2 1.6 project.3
  34.8 30.1 %all_to_all.20.got_ref = bf16[16,256,256]{2,1,0:T(8,128)(2,1)S(1)} all-to-all(bf16[16,256,256]{2,1,0:T(8,128)(2,1)S(1)} %get-tuple-element.23), channel_id=1, replica_groups={{0,16,1,17,2,18,3,19,4,20,5,21,6,22,7,23},{24,8,25,9,26,10,27,11,28,12,..., dimensions={0} | all-to-all | bytes 4194304 | tf_op jit(solution)/shard_map/all_to_all | solution.py:272
  64.9 0.7 outgoing.1
  65.7 17.7 %all_to_all.21 = bf16[16,8,16,256]{3,2,1,0:T(8,128)(2,1)S(1)} all-to-all(bf16[16,8,16,256]{3,2,1,0:T(8,128)(2,1)S(1)} %outgoing.1), channel_id=1, replica_groups={{0,16,1,17,2,18,3,19,4,20,5,21,6,22,7,23},{24,8,25,9,26,10,27,11,28,12,..., dimensions={0} | all-to-all | bytes 2097152 | tf_op jit(solution)/shard_map/all_to_all | solution.py:272
  83.4 5.4 %combine_project.1 = (bf16[16,256,128]{2,1,0:T(8,128)(2,1)S(1)}, bf16[16,256,256]{2,1,0:T(8,128)(2,1)S(1)}) custom-call(bf16[8,256,128]{2,1,0:T(8,128)(2,1)S(1)} %get-tuple-element.20.near_ref, bf16[8,256,128]{2,1,0:T(8,128)(2,1)S(1)} %get-tuple-element.22.far_ref, bf16[16,128,256]{2,1,0:T(8,128)(2,1)S(1)} %bitcast.6, f32[2,128]{1,0:T(2,128)S(1)} %copy-done.7, ...), custom_call_target="tpu_custom_call" | custom-call | tf_op jit(solution)/shard_map/combine_project/pallas_call | solution.py:219
  88.8 28.9 %all_to_all.22 = bf16[16,256,256]{2,1,0:T(8,128)(2,1)S(1)} all-to-all(bf16[16,256,256]{2,1,0:T(8,128)(2,1)S(1)} %get-tuple-element.25), channel_id=1, replica_groups={{0,16,1,17,2,18,3,19,4,20,5,21,6,22,7,23},{24,8,25,9,26,10,27,11,28,12,..., dimensions={0} | all-to-all | bytes 4194304 | tf_op jit(solution)/shard_map/all_to_all | solution.py:272
  117.7 0.5 incoming.1
  118.2 17.7 %all_to_all.23.got_ref = bf16[16,128,256]{2,1,0:T(8,128)(2,1)S(1)} all-to-all(bf16[16,128,256]{2,1,0:T(8,128)(2,1)S(1)} %incoming.1), channel_id=1, replica_groups={{0,16,1,17,2,18,3,19,4,20,5,21,6,22,7,23},{24,8,25,9,26,10,27,11,28,12,..., dimensions={0} | all-to-all | bytes 2097152 | tf_op jit(solution)/shard_map/all_to_all | solution.py:272
  135.9 3.8 %combine_transition.2 = bf16[8,256,128]{2,1,0:T(8,128)(2,1)S(1)} custom-call(bf16[16,256,128]{2,1,0:T(8,128)(2,1)S(1)} %get-tuple-element.24.pair_ref, bf16[16,128,256]{2,1,0:T(8,128)(2,1)S(1)} %all_to_all.23.got_ref, f32[2,128]{1,0:T(2,128)S(1)} %copy-done.7, bf16[2,128,128]{2,1,0:T(8,128)(2,1)S(1)} %copy-done.3, f32[2,128]{1,0:T(2,128)S(1)} %copy-done.8, ...), custom_call_target="tpu_custom_call" | custom-call | tf_op jit(solution)/shard_map/combine_transition/pallas_call | solution.py:219
  139.7 1.3 collective-permute-start.9
  141.0 2.0 %collective-permute-start.8 = (bf16[8,256,128]{2,1,0:T(8,128)(2,1)S(1)}, bf16[8,256,128]{2,1,0:T(8,128)(2,1)S(1)}, u32[]{:S(2)}, u32[]{:S(2)}) collective-permute-start(bf16[8,256,128]{2,1,0:T(8,128)(2,1)S(1)} %combine_transition.2), channel_id=1, source_target_pairs={{8,16},{9,17},{10,18},{11,19},{12,20},{13,21},{14,22},{15,23},{16,... | collective-permute-start | bytes 1572872 | tf_op jit(solution)/shard_map/ppermute | solution.py:258
  143.0 3.8 %combine_transition.3.top_ref = bf16[8,256,128]{2,1,0:T(8,128)(2,1)S(1)} custom-call(bf16[16,256,128]{2,1,0:T(8,128)(2,1)S(1)} %get-tuple-element.24.pair_ref, bf16[16,128,256]{2,1,0:T(8,128)(2,1)S(1)} %all_to_all.23.got_ref, f32[2,128]{1,0:T(2,128)S(1)} %copy-done.7, bf16[2,128,128]{2,1,0:T(8,128)(2,1)S(1)} %copy-done.3, f32[2,128]{1,0:T(2,128)S(1)} %copy-done.8, ...), custom_call_target="tpu_custom_call" | custom-call | flops 20000000000 | tf_op jit(solution)/shard_map/combine_transition/pallas_call | solution.py:219
  146.8 1.6 collective-permute-start.7
  148.4 19.1 %collective-permute-done.9.bottom_ref = bf16[8,256,128]{2,1,0:T(8,128)(2,1)S(1)} collective-permute-done((bf16[8,256,128]{2,1,0:T(8,128)(2,1)S(1)}, bf16[8,256,128]{2,1,0:T(8,128)(2,1)S(1)}, u32[]{:S(2)}, u32[]{:S(2)}) %collective-permute-start.9) | collective-permute-done | bytes 524320 | tf_op jit(solution)/shard_map/ppermute | solution.py:258
  167.6 2.2 %collective-permute-done.8.top_ref = bf16[8,256,128]{2,1,0:T(8,128)(2,1)S(1)} collective-permute-done((bf16[8,256,128]{2,1,0:T(8,128)(2,1)S(1)}, bf16[8,256,128]{2,1,0:T(8,128)(2,1)S(1)}, u32[]{:S(2)}, u32[]{:S(2)}) %collective-permute-start.8) | collective-permute-done | bytes 524320 | tf_op jit(solution)/shard_map/ppermute | solution.py:258
  169.8 1.1 pick.1
  (22 shorter events, 0.1 us)
Async XLA Ops:
  0.0 33.2 %copy-start.1 = (bf16[2,128,512]{2,1,0:T(8,128)(2,1)S(1)}, bf16[2,128,512]{2,1,0:T(8,128)(2,1)}, u32[]{:S(2)}) copy-start(bf16[2,128,512]{2,1,0:T(8,128)(2,1)} %proj_ref.5) | copy-start | bytes 786436
  1.3 7.2 %collective-permute-start.2 = (bf16[4,256,128]{2,1,0:T(8,128)(2,1)S(1)}, bf16[4,256,128]{2,1,0:T(8,128)(2,1)S(1)}, u32[]{:S(2)}, u32[]{:S(2)}) collective-permute-start(bf16[4,256,128]{2,1,0:T(8,128)(2,1)S(1)} %get-tuple-element.19), channel_id=1, source_target_pairs={{0,16},{1,17},{2,18},{3,19},{4,20},{5,21},{6,22},{7,23},{8,24},{9,... | collective-permute-start | bytes 786440 | tf_op jit(solution)/shard_map/ppermute | solution.py:258
  2.6 30.7 %collective-permute-start.3 = (bf16[8,256,128]{2,1,0:T(8,128)(2,1)S(1)}, bf16[8,256,128]{2,1,0:T(8,128)(2,1)S(1)}, u32[]{:S(2)}, u32[]{:S(2)}) collective-permute-start(bf16[8,256,128]{2,1,0:T(8,128)(2,1)S(1)} %get-tuple-element.16.own_ref), channel_id=1, source_target_pairs={{8,0},{9,1},{10,2},{11,3},{12,4},{13,5},{14,6},{15,7},{16,24},{17,... | collective-permute-start | bytes 1572872 | tf_op jit(solution)/shard_map/ppermute | solution.py:258
  4.5 8.2 %collective-permute-start.1 = (bf16[3,256,128]{2,1,0:T(8,128)(2,1)S(1)}, bf16[3,256,128]{2,1,0:T(8,128)(2,1)S(1)}, u32[]{:S(2)}, u32[]{:S(2)}) collective-permute-start(bf16[3,256,128]{2,1,0:T(8,128)(2,1)S(1)} %get-tuple-element.18), channel_id=1, source_target_pairs={{0,16},{1,17},{2,18},{3,19},{4,20},{5,21},{6,22},{7,23},{8,24},{9,... | collective-permute-start | bytes 589832 | tf_op jit(solution)/shard_map/ppermute | solution.py:258
  8.5 24.7 %collective-permute-start.6 = (bf16[4,256,128]{2,1,0:T(8,128)(2,1)S(1)}, bf16[4,256,128]{2,1,0:T(8,128)(2,1)S(1)}, u32[]{:S(2)}, u32[]{:S(2)}) collective-permute-start(bf16[4,256,128]{2,1,0:T(8,128)(2,1)S(1)} %collective-permute-done.2.refs_2_), channel_id=1, source_target_pairs={{0,8},{1,9},{2,10},{3,11},{4,12},{5,13},{6,14},{7,15},{24,16},{25,... | collective-permute-start | bytes 786440 | tf_op jit(solution)/shard_map/ppermute | solution.py:258
  12.7 20.5 %collective-permute-start.5 = (bf16[3,256,128]{2,1,0:T(8,128)(2,1)S(1)}, bf16[3,256,128]{2,1,0:T(8,128)(2,1)S(1)}, u32[]{:S(2)}, u32[]{:S(2)}) collective-permute-start(bf16[3,256,128]{2,1,0:T(8,128)(2,1)S(1)} %collective-permute-done.1.refs_1_), channel_id=1, source_target_pairs={{0,8},{1,9},{2,10},{3,11},{4,12},{5,13},{6,14},{7,15},{24,16},{25,... | collective-permute-start | bytes 589832 | tf_op jit(solution)/shard_map/ppermute | solution.py:258
  14.0 5.0 %collective-permute-start = (bf16[1,256,128]{2,1,0:T(8,128)(2,1)S(1)}, bf16[1,256,128]{2,1,0:T(8,128)(2,1)S(1)}, u32[]{:S(2)}, u32[]{:S(2)}) collective-permute-start(bf16[1,256,128]{2,1,0:T(8,128)(2,1)S(1)} %get-tuple-element.17), channel_id=1, source_target_pairs={{0,16},{1,17},{2,18},{3,19},{4,20},{5,21},{6,22},{7,23},{24,8},{25... | collective-permute-start | bytes 196616 | tf_op jit(solution)/shard_map/ppermute | solution.py:258
  15.3 17.8 %collective-permute-start.4 = (bf16[1,256,128]{2,1,0:T(8,128)(2,1)S(1)}, bf16[1,256,128]{2,1,0:T(8,128)(2,1)S(1)}, u32[]{:S(2)}, u32[]{:S(2)}) collective-permute-start(bf16[1,256,128]{2,1,0:T(8,128)(2,1)S(1)} %get-tuple-element.17), channel_id=1, source_target_pairs={{8,16},{9,17},{10,18},{11,19},{12,20},{13,21},{14,22},{15,23},{16,... | collective-permute-start | bytes 196616 | tf_op jit(solution)/shard_map/ppermute | solution.py:258
  19.0 1.0 copy-start
  20.0 0.7 copy-start.6
  64.9 18.5 %copy-start.3 = (bf16[2,128,128]{2,1,0:T(8,128)(2,1)S(1)}, bf16[2,128,128]{2,1,0:T(8,128)(2,1)}, u32[]{:S(2)}) copy-start(bf16[2,128,128]{2,1,0:T(8,128)(2,1)} %gate_ref.5) | copy-start | bytes 196612
  64.9 18.5 %copy-start.4 = (bf16[2,128,128]{2,1,0:T(8,128)(2,1)S(1)}, bf16[2,128,128]{2,1,0:T(8,128)(2,1)}, u32[]{:S(2)}) copy-start(bf16[2,128,128]{2,1,0:T(8,128)(2,1)} %out_ref.5) | copy-start | bytes 196612
  64.9 18.5 %copy-start.7 = (f32[2,128]{1,0:T(2,128)S(1)}, f32[2,128]{1,0:T(2,128)}, u32[]{:S(2)}) copy-start(f32[2,128]{1,0:T(2,128)} %gain_ref.9) | copy-start | bytes 3076
  64.9 18.5 %copy-start.8 = (f32[2,128]{1,0:T(2,128)S(1)}, f32[2,128]{1,0:T(2,128)}, u32[]{:S(2)}) copy-start(f32[2,128]{1,0:T(2,128)} %mid_gain_ref.5) | copy-start | bytes 3076
  117.7 18.2 %copy-start.2 = (bf16[128,1024]{1,0:T(8,128)(2,1)S(1)}, bf16[128,1024]{1,0:T(8,128)(2,1)}, u32[]{:S(2)}) copy-start(bf16[128,1024]{1,0:T(8,128)(2,1)} %up_ref.3) | copy-start | bytes 786436
  117.7 18.2 %copy-start.5 = (bf16[512,128]{1,0:T(8,128)(2,1)S(1)}, bf16[512,128]{1,0:T(8,128)(2,1)}, u32[]{:S(2)}) copy-start(bf16[512,128]{1,0:T(8,128)(2,1)} %down_ref.3) | copy-start | bytes 393220
  117.7 18.3 %copy-start.9 = (f32[128]{0:T(128)S(1)}, f32[128]{0:T(128)}, u32[]{:S(2)}) copy-start(f32[128]{0:T(128)} %param.15) | copy-start | bytes 1540
  139.7 27.9 %collective-permute-start.9 = (bf16[8,256,128]{2,1,0:T(8,128)(2,1)S(1)}, bf16[8,256,128]{2,1,0:T(8,128)(2,1)S(1)}, u32[]{:S(2)}, u32[]{:S(2)}) collective-permute-start(bf16[8,256,128]{2,1,0:T(8,128)(2,1)S(1)} %combine_transition.2), channel_id=1, source_target_pairs={{0,8},{1,9},{2,10},{3,11},{4,12},{5,13},{6,14},{7,15},{24,16},{25,... | collective-permute-start | bytes 1572872 | tf_op jit(solution)/shard_map/ppermute | solution.py:258
  141.0 28.8 %collective-permute-start.8 = (bf16[8,256,128]{2,1,0:T(8,128)(2,1)S(1)}, bf16[8,256,128]{2,1,0:T(8,128)(2,1)S(1)}, u32[]{:S(2)}, u32[]{:S(2)}) collective-permute-start(bf16[8,256,128]{2,1,0:T(8,128)(2,1)S(1)} %combine_transition.2), channel_id=1, source_target_pairs={{8,16},{9,17},{10,18},{11,19},{12,20},{13,21},{14,22},{15,23},{16,... | collective-permute-start | bytes 1572872 | tf_op jit(solution)/shard_map/ppermute | solution.py:258
  146.8 23.1 %collective-permute-start.7 = (bf16[8,256,128]{2,1,0:T(8,128)(2,1)S(1)}, bf16[8,256,128]{2,1,0:T(8,128)(2,1)S(1)}, u32[]{:S(2)}, u32[]{:S(2)}) collective-permute-start(bf16[8,256,128]{2,1,0:T(8,128)(2,1)S(1)} %combine_transition.3.top_ref), channel_id=1, source_target_pairs={{8,24},{9,25},{10,26},{11,27},{12,28},{13,29},{14,30},{15,31},{16,... | collective-permute-start | bytes 1572872 | tf_op jit(solution)/shard_map/ppermute | solution.py:258

commit v4 on v3

--- a/solution.py
+++ b/solution.py
@@ -86,18 +86,6 @@
         project(norm_lanes(pair, gain_ref[0:1]), proj_ref, 0, sent_ref, columns, rows)
 
 
-def far_kernel(flag_ref, near_ref, own_ref, gain_ref, proj_ref, *refs):
-    other_refs, (pair_ref, sent_ref) = refs[:-2], refs[-2:]
-    rows, width, _ = pair_ref.shape
-    first = near_ref.shape[1]
-    sent_ref[:, :first] = near_ref[...]
-    for columns in column_blocks(width):
-        other = jnp.concatenate([flat(ref[:, columns]) for ref in other_refs], axis=0)
-        pair = jnp.where(flag_ref[0] == 1, flat(own_ref[:rows, columns]), other)
-        pair_ref[:, columns] = pair.reshape(rows, LANES, -1)
-        project(norm_lanes(pair, gain_ref[0:1]), proj_ref, 0, sent_ref, columns, rows, first)
-
-
 def middle_kernel(
     near_ref, far_ref, got_ref, gain_ref, gate_ref, mid_gain_ref, out_ref, proj_ref,
     pair_out_ref, sent_ref, scratch_ref,
@@ -139,15 +127,14 @@
         pair_out_ref[:, columns] = total.astype(jnp.bfloat16).reshape(rows, LANES, -1)
 
 
-def outgoing_kernel(side_ref, got_ref, sent_ref):
-    parts, block, width = got_ref.shape
-    block = block // 2
+def outgoing_kernel(side_ref, near_ref, far_ref, sent_ref):
+    parts, block, width = near_ref.shape
     per, rows = sent_ref.shape[1], sent_ref.shape[2] // 2
     count = parts * rows
     side = side_ref[0]
     slots = [
-        part.astype(jnp.float32).reshape(parts, 2, per, rows, width)
-        for part in (got_ref[:, :block], got_ref[:, block:])
+        ref[...].astype(jnp.float32).reshape(parts, 2, per, rows, width)
+        for ref in (near_ref, far_ref)
     ]
     for item in range(per):
         left, right = [
@@ -198,14 +185,16 @@
         out_ref[...] = far_ref[...]
 
 
-def split_kernel(pair_ref, *refs):
-    out_refs, sems = refs[:-1], refs[-1]
-    copies, start = [], 0
-    for place, out_ref in enumerate(out_refs):
+def split_kernel(pair_ref, proj_ref, gain_ref, *refs):
+    (*out_refs, proj_out_ref, gain_out_ref), sems = refs[:-1], refs[-1]
+    moves, start = [(proj_ref, proj_out_ref), (gain_ref, gain_out_ref)], 0
+    for out_ref in out_refs:
         height = out_ref.shape[0]
-        source = pair_ref.at[pl.ds(start, height)]
-        copies.append(pltpu.make_async_copy(source, out_ref, sems.at[place]))
+        moves.append((pair_ref.at[pl.ds(start, height)], out_ref))
         start += height
+    copies = [
+        pltpu.make_async_copy(*move, sems.at[place]) for place, move in enumerate(moves)
+    ]
     for copy in copies:
         copy.start()
     for copy in copies:
@@ -284,15 +273,19 @@
 
     heights = [own * share // 8 for share in SHARES]
     away = [(g, s, c) for g, s, c in every if not at_home(g, s)]
-    low, middle, *high = pl.pallas_call(
+    low, middle, *high, first_proj, first_gain = pl.pallas_call(
         split_kernel,
-        in_specs=[pl.BlockSpec(memory_space=pltpu.HBM)],
-        out_specs=[pl.BlockSpec(memory_space=pltpu.VMEM)] * len(heights),
-        out_shape=[shape(height, width, channels) for height in heights],
-        scratch_shapes=[pltpu.SemaphoreType.DMA((len(heights),))],
+        in_specs=[pl.BlockSpec(memory_space=pltpu.HBM)] * 3,
+        out_specs=[pl.BlockSpec(memory_space=pltpu.VMEM)] * (len(heights) + 2),
+        out_shape=[shape(height, width, channels) for height in heights]
+        + [jax.ShapeDtypeStruct(value.shape, value.dtype) for value in (tri_proj, tri_gain)],
+        scratch_shapes=[pltpu.SemaphoreType.DMA((len(heights) + 2,))],
         compiler_params=pltpu.CompilerParams(vmem_limit_bytes=VMEM_BYTES),
         name="split",
-    )(pltpu.with_memory_space_constraint(pair_rep, pltpu.HBM))
+    )(*(
+        pltpu.with_memory_space_constraint(value, pltpu.HBM)
+        for value in (pair_rep, tri_proj, tri_gain)
+    ))
     hopped = [permute(part, [((g, s, c), (g ^ 1, s, c)) for g, s, c in every]) for part in high]
     direct = permute(low, [((g, s, c), (g, across(s), c)) for g, s, c in away])
     relayed = [
@@ -307,18 +300,19 @@
     near, near_sent = call(
         near_kernel, "project",
         [shape(own, width, channels), shape(parts, 2 * per * own, width)], [],
-        home_flag, low, tri_gain, tri_proj, stepped, *hopped, flops=0,
-    )
-    far, sent = call(
-        far_kernel, "project",
-        [shape(own, width, channels), shape(parts, 2 * per * rows, width)], [],
-        home_flag, near_sent, direct, tri_gain, tri_proj, diagonal, *relayed,
-    )
-    got = exchange(sent)
+        home_flag, low, first_gain, first_proj, stepped, *hopped, flops=0,
+    )
+    near_got = exchange(near_sent)
+    far, far_sent = call(
+        near_kernel, "project",
+        [shape(own, width, channels), shape(parts, 2 * per * own, width)], [],
+        home_flag, direct, first_gain, first_proj, diagonal, *relayed, flops=5 * FAR_FLOPS,
+    )
+    far_got = exchange(far_sent)
 
     product = call(
         outgoing_kernel, "outgoing", shape(parts, per, rows, width), [],
-        side_flag, got,
+        side_flag, near_got, far_got,
     )
     back = exchange(product).reshape(parts, per * rows, width)
 

time: 171 us -> 170 us (level)
  blocking collectives: 94.5 us -> 83.8 us
  starting transfers between devices: 15.2 us -> 22.8 us
  Pallas kernels: 19.5 us -> 21.4 us
    all_to_all x4, blocking collectives: 94.5 us -> 83.8 us  [exchange(): lax.all_to_all(value, AXES, split_axis=0, concat_axis=0, tiled=True, axis...]
    all_to_all x0 -> x1, starting transfers between devices: none -> 7.35 us  [exchange(): lax.all_to_all(value, AXES, split_axis=0, concat_axis=0, tiled=True, axis...]
    ppermute x10, waiting for transfers between devices: 39.9 us -> 33 us  [permute(): lax.ppermute(value, AXES, [(number(*a), number(*b)) for a, b in pairs])]
    all_to_all x0 -> x1, waiting for transfers between devices: none -> 6.47 us  [exchange(): lax.all_to_all(value, AXES, split_axis=0, concat_axis=0, tiled=True, axis...]
    pallas_call x9, Pallas kernels: 18.2 us -> 20.1 us  [call(): pl.pallas_call(kernel, in_specs=[smem if operand.dtype == jnp.int32 else...]
  transfers between devices with their start and end apart: 10 -> 11, of which waited for: 7 -> 8; matrix products, arithmetic and copies ran while one was open for 0% -> 0% of each run, Pallas kernels for 3% -> 5%
where the time goes in v4:
time: 170 us
  blocking collectives  83.8 us (49%)
  waiting for transfers between devices  39.5 us (23%)
  starting transfers between devices  22.8 us (13%)
  Pallas kernels  21.4 us (13%)
  local copies, waits for them, and re-layouts  1.88 us (1%)
    all_to_all x4, blocking collectives, exchange(): lax.all_to_all(value, AXES, split_axis=0, concat_axis=0, tiled=True, axis...  83.8 us
    ppermute x10, waiting for transfers between devices, permute(): lax.ppermute(value, AXES, [(number(*a), number(*b)) for a, b in pairs])  33 us
    pallas_call x9, Pallas kernels, call(): pl.pallas_call(kernel, in_specs=[smem if operand.dtype == jnp.int32 else...  20.1 us
    ppermute x10, starting transfers between devices, permute(): lax.ppermute(value, AXES, [(number(*a), number(*b)) for a, b in pairs])  15.5 us
    all_to_all x1, starting transfers between devices, exchange(): lax.all_to_all(value, AXES, split_axis=0, concat_axis=0, tiled=True, axis...  7.35 us
    all_to_all x1, waiting for transfers between devices, exchange(): lax.all_to_all(value, AXES, split_axis=0, concat_axis=0, tiled=True, axis...  6.47 us
  transfers between devices with their start and end apart: 11, of which 8 were waited for; matrix products, arithmetic and copies ran while one was open for 0% of the time, Pallas kernels for 5%

profile of v4, /device:TPU:25, one launch (start us, length us, event | category | flops | bytes accessed | tf_op | source)
XLA Modules:
  0.0 169.7 jit_solution(8831961034168423708)
XLA Ops:
  0.0 1.3 split.1
  1.3 1.3 collective-permute-start.2
  2.6 2.0 %collective-permute-start.3 = (bf16[8,256,128]{2,1,0:T(8,128)(2,1)S(1)}, bf16[8,256,128]{2,1,0:T(8,128)(2,1)S(1)}, u32[]{:S(2)}, u32[]{:S(2)}) collective-permute-start(bf16[8,256,128]{2,1,0:T(8,128)(2,1)S(1)} %get-tuple-element.18.own_ref), channel_id=1, source_target_pairs={{8,0},{9,1},{10,2},{11,3},{12,4},{13,5},{14,6},{15,7},{16,24},{17,... | collective-permute-start | bytes 1572872 | tf_op jit(solution)/shard_map/ppermute | solution.py:247
  4.7 3.9 %collective-permute-done.2.refs_2_ = bf16[4,256,128]{2,1,0:T(8,128)(2,1)S(1)} collective-permute-done((bf16[4,256,128]{2,1,0:T(8,128)(2,1)S(1)}, bf16[4,256,128]{2,1,0:T(8,128)(2,1)S(1)}, u32[]{:S(2)}, u32[]{:S(2)}) %collective-permute-start.2) | collective-permute-done | bytes 262176 | tf_op jit(solution)/shard_map/ppermute | solution.py:247
  8.6 1.3 collective-permute-start.6
  9.9 2.9 %collective-permute-done.1.refs_1_ = bf16[3,256,128]{2,1,0:T(8,128)(2,1)S(1)} collective-permute-done((bf16[3,256,128]{2,1,0:T(8,128)(2,1)S(1)}, bf16[3,256,128]{2,1,0:T(8,128)(2,1)S(1)}, u32[]{:S(2)}, u32[]{:S(2)}) %collective-permute-start.1) | collective-permute-done | bytes 196640 | tf_op jit(solution)/shard_map/ppermute | solution.py:247
  12.8 1.3 collective-permute-start.5
  14.1 1.3 collective-permute-start
  15.4 3.1 %collective-permute-start.4 = (bf16[1,256,128]{2,1,0:T(8,128)(2,1)S(1)}, bf16[1,256,128]{2,1,0:T(8,128)(2,1)S(1)}, u32[]{:S(2)}, u32[]{:S(2)}) collective-permute-start(bf16[1,256,128]{2,1,0:T(8,128)(2,1)S(1)} %get-tuple-element.21), channel_id=1, source_target_pairs={{8,16},{9,17},{10,18},{11,19},{12,20},{13,21},{14,22},{15,23},{16,... | collective-permute-start | bytes 196616 | tf_op jit(solution)/shard_map/ppermute | solution.py:247
  18.5 1.2 collective-permute-done.refs_0_
  19.7 2.4 %project.2 = (bf16[8,256,128]{2,1,0:T(8,128)(2,1)S(1)}, bf16[16,128,256]{2,1,0:T(8,128)(2,1)}) custom-call(s32[1]{0:T(128)} %bitcast.flag_ref, bf16[8,256,128]{2,1,0:T(8,128)(2,1)S(1)} %get-tuple-element.18.own_ref, f32[2,128]{1,0:T(2,128)S(1)} %get-tuple-element.19.gain_ref, bf16[2,128,512]{2,1,0:T(8,128)(2,1)S(1)} %get-tuple-element.20.proj_ref, ...), custom_call_target="tpu_custom_call" | custom-call | tf_op jit(solution)/shard_map/project/pallas_call | solution.py:208
  22.1 7.3 %all-to-all-start = ((bf16[16,128,256]{2,1,0:T(8,128)(2,1)}), bf16[16,128,256]{2,1,0:T(8,128)(2,1)S(1)}, u32[]{:S(2)}, u32[]{:S(2)}) async-start(bf16[16,128,256]{2,1,0:T(8,128)(2,1)} %get-tuple-element.26), calls=%async_computation | async-start | bytes 2097152 | tf_op jit(solution)/shard_map/all_to_all | solution.py:261
  29.5 3.7 %collective-permute-done.4.refs_0_ = bf16[1,256,128]{2,1,0:T(8,128)(2,1)S(1)} collective-permute-done((bf16[1,256,128]{2,1,0:T(8,128)(2,1)S(1)}, bf16[1,256,128]{2,1,0:T(8,128)(2,1)S(1)}, u32[]{:S(2)}, u32[]{:S(2)}) %collective-permute-start.4) | collective-permute-done | bytes 65568 | tf_op jit(solution)/shard_map/ppermute | solution.py:247
  33.4 0.8 copy-done.8
  34.2 1.0 copy-done.9
  35.3 2.5 %project.3 = (bf16[8,256,128]{2,1,0:T(8,128)(2,1)S(1)}, bf16[16,128,256]{2,1,0:T(8,128)(2,1)S(1)}) custom-call(s32[1]{0:T(128)} %bitcast.flag_ref, bf16[8,256,128]{2,1,0:T(8,128)(2,1)S(1)} %copy-done.9, f32[2,128]{1,0:T(2,128)S(1)} %get-tuple-element.19.gain_ref, bf16[2,128,512]{2,1,0:T(8,128)(2,1)S(1)} %get-tuple-element.20.proj_ref, ...), custom_call_target="tpu_custom_call" | custom-call | flops 99999997952 | tf_op jit(solution)/shard_map/project/pallas_call | solution.py:208
  37.8 6.5 %all-to-all-done.near_ref = bf16[16,128,256]{2,1,0:T(8,128)(2,1)S(1)} async-done(((bf16[16,128,256]{2,1,0:T(8,128)(2,1)}), bf16[16,128,256]{2,1,0:T(8,128)(2,1)S(1)}, u32[]{:S(2)}, u32[]{:S(2)}) %all-to-all-start) | async-done | bytes 1048608 | tf_op jit(solution)/shard_map/all_to_all | solution.py:261
  44.2 19.6 %all_to_all.25.far_ref = bf16[16,128,256]{2,1,0:T(8,128)(2,1)S(1)} all-to-all(bf16[16,128,256]{2,1,0:T(8,128)(2,1)S(1)} %get-tuple-element.27), channel_id=1, replica_groups={{0,16,1,17,2,18,3,19,4,20,5,21,6,22,7,23},{24,8,25,9,26,10,27,11,28,12,..., dimensions={0} | all-to-all | bytes 2097152 | tf_op jit(solution)/shard_map/all_to_all | solution.py:261
  63.9 0.7 outgoing.1
  64.6 17.6 %all_to_all.26 = bf16[16,8,16,256]{3,2,1,0:T(8,128)(2,1)S(1)} all-to-all(bf16[16,8,16,256]{3,2,1,0:T(8,128)(2,1)S(1)} %outgoing.1), channel_id=1, replica_groups={{0,16,1,17,2,18,3,19,4,20,5,21,6,22,7,23},{24,8,25,9,26,10,27,11,28,12,..., dimensions={0} | all-to-all | bytes 2097152 | tf_op jit(solution)/shard_map/all_to_all | solution.py:261
  82.3 5.3 %combine_project.1 = (bf16[16,256,128]{2,1,0:T(8,128)(2,1)S(1)}, bf16[16,256,256]{2,1,0:T(8,128)(2,1)S(1)}) custom-call(bf16[8,256,128]{2,1,0:T(8,128)(2,1)S(1)} %get-tuple-element.24.near_ref, bf16[8,256,128]{2,1,0:T(8,128)(2,1)S(1)} %get-tuple-element.25.far_ref, bf16[16,128,256]{2,1,0:T(8,128)(2,1)S(1)} %bitcast.6, f32[2,128]{1,0:T(2,128)S(1)} %copy-done.5, ...), custom_call_target="tpu_custom_call" | custom-call | tf_op jit(solution)/shard_map/combine_project/pallas_call | solution.py:208
  87.6 28.9 %all_to_all.27 = bf16[16,256,256]{2,1,0:T(8,128)(2,1)S(1)} all-to-all(bf16[16,256,256]{2,1,0:T(8,128)(2,1)S(1)} %get-tuple-element.29), channel_id=1, replica_groups={{0,16,1,17,2,18,3,19,4,20,5,21,6,22,7,23},{24,8,25,9,26,10,27,11,28,12,..., dimensions={0} | all-to-all | bytes 4194304 | tf_op jit(solution)/shard_map/all_to_all | solution.py:261
  116.5 0.5 incoming.1
  117.0 17.7 %all_to_all.28.got_ref = bf16[16,128,256]{2,1,0:T(8,128)(2,1)S(1)} all-to-all(bf16[16,128,256]{2,1,0:T(8,128)(2,1)S(1)} %incoming.1), channel_id=1, replica_groups={{0,16,1,17,2,18,3,19,4,20,5,21,6,22,7,23},{24,8,25,9,26,10,27,11,28,12,..., dimensions={0} | all-to-all | bytes 2097152 | tf_op jit(solution)/shard_map/all_to_all | solution.py:261
  134.7 3.8 %combine_transition.2 = bf16[8,256,128]{2,1,0:T(8,128)(2,1)S(1)} custom-call(bf16[16,256,128]{2,1,0:T(8,128)(2,1)S(1)} %get-tuple-element.28.pair_ref, bf16[16,128,256]{2,1,0:T(8,128)(2,1)S(1)} %all_to_all.28.got_ref, f32[2,128]{1,0:T(2,128)S(1)} %copy-done.5, bf16[2,128,128]{2,1,0:T(8,128)(2,1)S(1)} %copy-done.2, f32[2,128]{1,0:T(2,128)S(1)} %copy-done.6, ...), custom_call_target="tpu_custom_call" | custom-call | tf_op jit(solution)/shard_map/combine_transition/pallas_call | solution.py:208
  138.5 1.3 collective-permute-start.9
  139.8 2.3 %collective-permute-start.8 = (bf16[8,256,128]{2,1,0:T(8,128)(2,1)S(1)}, bf16[8,256,128]{2,1,0:T(8,128)(2,1)S(1)}, u32[]{:S(2)}, u32[]{:S(2)}) collective-permute-start(bf16[8,256,128]{2,1,0:T(8,128)(2,1)S(1)} %combine_transition.2), channel_id=1, source_target_pairs={{8,16},{9,17},{10,18},{11,19},{12,20},{13,21},{14,22},{15,23},{16,... | collective-permute-start | bytes 1572872 | tf_op jit(solution)/shard_map/ppermute | solution.py:247
  142.1 3.8 %combine_transition.3.top_ref = bf16[8,256,128]{2,1,0:T(8,128)(2,1)S(1)} custom-call(bf16[16,256,128]{2,1,0:T(8,128)(2,1)S(1)} %get-tuple-element.28.pair_ref, bf16[16,128,256]{2,1,0:T(8,128)(2,1)S(1)} %all_to_all.28.got_ref, f32[2,128]{1,0:T(2,128)S(1)} %copy-done.5, bf16[2,128,128]{2,1,0:T(8,128)(2,1)S(1)} %copy-done.2, f32[2,128]{1,0:T(2,128)S(1)} %copy-done.6, ...), custom_call_target="tpu_custom_call" | custom-call | flops 20000000000 | tf_op jit(solution)/shard_map/combine_transition/pallas_call | solution.py:208
  145.9 1.6 collective-permute-start.7
  147.5 18.8 %collective-permute-done.9.bottom_ref = bf16[8,256,128]{2,1,0:T(8,128)(2,1)S(1)} collective-permute-done((bf16[8,256,128]{2,1,0:T(8,128)(2,1)S(1)}, bf16[8,256,128]{2,1,0:T(8,128)(2,1)S(1)}, u32[]{:S(2)}, u32[]{:S(2)}) %collective-permute-start.9) | collective-permute-done | bytes 524320 | tf_op jit(solution)/shard_map/ppermute | solution.py:247
  166.4 2.2 %collective-permute-done.8.top_ref = bf16[8,256,128]{2,1,0:T(8,128)(2,1)S(1)} collective-permute-done((bf16[8,256,128]{2,1,0:T(8,128)(2,1)S(1)}, bf16[8,256,128]{2,1,0:T(8,128)(2,1)S(1)}, u32[]{:S(2)}, u32[]{:S(2)}) %collective-permute-start.8) | collective-permute-done | bytes 524320 | tf_op jit(solution)/shard_map/ppermute | solution.py:247
  168.6 1.1 pick.1
  (24 shorter events, 0.4 us)
Async XLA Ops:
  1.3 7.2 %collective-permute-start.2 = (bf16[4,256,128]{2,1,0:T(8,128)(2,1)S(1)}, bf16[4,256,128]{2,1,0:T(8,128)(2,1)S(1)}, u32[]{:S(2)}, u32[]{:S(2)}) collective-permute-start(bf16[4,256,128]{2,1,0:T(8,128)(2,1)S(1)} %get-tuple-element.23), channel_id=1, source_target_pairs={{0,16},{1,17},{2,18},{3,19},{4,20},{5,21},{6,22},{7,23},{8,24},{9,... | collective-permute-start | bytes 786440 | tf_op jit(solution)/shard_map/ppermute | solution.py:247
  2.6 30.8 %collective-permute-start.3 = (bf16[8,256,128]{2,1,0:T(8,128)(2,1)S(1)}, bf16[8,256,128]{2,1,0:T(8,128)(2,1)S(1)}, u32[]{:S(2)}, u32[]{:S(2)}) collective-permute-start(bf16[8,256,128]{2,1,0:T(8,128)(2,1)S(1)} %get-tuple-element.18.own_ref), channel_id=1, source_target_pairs={{8,0},{9,1},{10,2},{11,3},{12,4},{13,5},{14,6},{15,7},{16,24},{17,... | collective-permute-start | bytes 1572872 | tf_op jit(solution)/shard_map/ppermute | solution.py:247
  4.6 8.2 %collective-permute-start.1 = (bf16[3,256,128]{2,1,0:T(8,128)(2,1)S(1)}, bf16[3,256,128]{2,1,0:T(8,128)(2,1)S(1)}, u32[]{:S(2)}, u32[]{:S(2)}) collective-permute-start(bf16[3,256,128]{2,1,0:T(8,128)(2,1)S(1)} %get-tuple-element.22), channel_id=1, source_target_pairs={{0,16},{1,17},{2,18},{3,19},{4,20},{5,21},{6,22},{7,23},{8,24},{9,... | collective-permute-start | bytes 589832 | tf_op jit(solution)/shard_map/ppermute | solution.py:247
  8.6 24.8 %collective-permute-start.6 = (bf16[4,256,128]{2,1,0:T(8,128)(2,1)S(1)}, bf16[4,256,128]{2,1,0:T(8,128)(2,1)}, u32[]{:S(2)}, u32[]{:S(2)}) collective-permute-start(bf16[4,256,128]{2,1,0:T(8,128)(2,1)S(1)} %collective-permute-done.2.refs_2_), channel_id=1, source_target_pairs={{0,8},{1,9},{2,10},{3,11},{4,12},{5,13},{6,14},{7,15},{24,16},{25,... | collective-permute-start | bytes 786440 | tf_op jit(solution)/shard_map/ppermute | solution.py:247
  12.8 20.6 %collective-permute-start.5 = (bf16[3,256,128]{2,1,0:T(8,128)(2,1)S(1)}, bf16[3,256,128]{2,1,0:T(8,128)(2,1)}, u32[]{:S(2)}, u32[]{:S(2)}) collective-permute-start(bf16[3,256,128]{2,1,0:T(8,128)(2,1)S(1)} %collective-permute-done.1.refs_1_), channel_id=1, source_target_pairs={{0,8},{1,9},{2,10},{3,11},{4,12},{5,13},{6,14},{7,15},{24,16},{25,... | collective-permute-start | bytes 589832 | tf_op jit(solution)/shard_map/ppermute | solution.py:247
  14.1 5.6 %collective-permute-start = (bf16[1,256,128]{2,1,0:T(8,128)(2,1)S(1)}, bf16[1,256,128]{2,1,0:T(8,128)(2,1)S(1)}, u32[]{:S(2)}, u32[]{:S(2)}) collective-permute-start(bf16[1,256,128]{2,1,0:T(8,128)(2,1)S(1)} %get-tuple-element.21), channel_id=1, source_target_pairs={{0,16},{1,17},{2,18},{3,19},{4,20},{5,21},{6,22},{7,23},{24,8},{25... | collective-permute-start | bytes 196616 | tf_op jit(solution)/shard_map/ppermute | solution.py:247
  15.4 17.8 %collective-permute-start.4 = (bf16[1,256,128]{2,1,0:T(8,128)(2,1)S(1)}, bf16[1,256,128]{2,1,0:T(8,128)(2,1)S(1)}, u32[]{:S(2)}, u32[]{:S(2)}) collective-permute-start(bf16[1,256,128]{2,1,0:T(8,128)(2,1)S(1)} %get-tuple-element.21), channel_id=1, source_target_pairs={{8,16},{9,17},{10,18},{11,19},{12,20},{13,21},{14,22},{15,23},{16,... | collective-permute-start | bytes 196616 | tf_op jit(solution)/shard_map/ppermute | solution.py:247
  22.1 22.1 %all-to-all-start = ((bf16[16,128,256]{2,1,0:T(8,128)(2,1)}), bf16[16,128,256]{2,1,0:T(8,128)(2,1)S(1)}, u32[]{:S(2)}, u32[]{:S(2)}) async-start(bf16[16,128,256]{2,1,0:T(8,128)(2,1)} %get-tuple-element.26), calls=%async_computation | async-start | bytes 2097152 | tf_op jit(solution)/shard_map/all_to_all | solution.py:261
  33.4 0.8 copy-start.8
  34.2 1.0 copy-start.9
  63.8 18.4 %copy-start = (bf16[2,128,512]{2,1,0:T(8,128)(2,1)S(1)}, bf16[2,128,512]{2,1,0:T(8,128)(2,1)}, u32[]{:S(2)}) copy-start(bf16[2,128,512]{2,1,0:T(8,128)(2,1)} %proj_ref.3) | copy-start | bytes 786436
  63.8 18.4 %copy-start.2 = (bf16[2,128,128]{2,1,0:T(8,128)(2,1)S(1)}, bf16[2,128,128]{2,1,0:T(8,128)(2,1)}, u32[]{:S(2)}) copy-start(bf16[2,128,128]{2,1,0:T(8,128)(2,1)} %gate_ref.5) | copy-start | bytes 196612
  63.8 18.4 %copy-start.3 = (bf16[2,128,128]{2,1,0:T(8,128)(2,1)S(1)}, bf16[2,128,128]{2,1,0:T(8,128)(2,1)}, u32[]{:S(2)}) copy-start(bf16[2,128,128]{2,1,0:T(8,128)(2,1)} %out_ref.5) | copy-start | bytes 196612
  63.8 18.4 %copy-start.5 = (f32[2,128]{1,0:T(2,128)S(1)}, f32[2,128]{1,0:T(2,128)}, u32[]{:S(2)}) copy-start(f32[2,128]{1,0:T(2,128)} %gain_ref.7) | copy-start | bytes 3076
  63.8 18.4 %copy-start.6 = (f32[2,128]{1,0:T(2,128)S(1)}, f32[2,128]{1,0:T(2,128)}, u32[]{:S(2)}) copy-start(f32[2,128]{1,0:T(2,128)} %mid_gain_ref.5) | copy-start | bytes 3076
  116.5 18.2 %copy-start.1 = (bf16[128,1024]{1,0:T(8,128)(2,1)S(1)}, bf16[128,1024]{1,0:T(8,128)(2,1)}, u32[]{:S(2)}) copy-start(bf16[128,1024]{1,0:T(8,128)(2,1)} %up_ref.3) | copy-start | bytes 786436
  116.5 18.2 %copy-start.4 = (bf16[512,128]{1,0:T(8,128)(2,1)S(1)}, bf16[512,128]{1,0:T(8,128)(2,1)}, u32[]{:S(2)}) copy-start(bf16[512,128]{1,0:T(8,128)(2,1)} %down_ref.3) | copy-start | bytes 393220
  116.5 18.2 %copy-start.7 = (f32[128]{0:T(128)S(1)}, f32[128]{0:T(128)}, u32[]{:S(2)}) copy-start(f32[128]{0:T(128)} %param.15) | copy-start | bytes 1540
  138.5 27.9 %collective-permute-start.9 = (bf16[8,256,128]{2,1,0:T(8,128)(2,1)S(1)}, bf16[8,256,128]{2,1,0:T(8,128)(2,1)S(1)}, u32[]{:S(2)}, u32[]{:S(2)}) collective-permute-start(bf16[8,256,128]{2,1,0:T(8,128)(2,1)S(1)} %combine_transition.2), channel_id=1, source_target_pairs={{0,8},{1,9},{2,10},{3,11},{4,12},{5,13},{6,14},{7,15},{24,16},{25,... | collective-permute-start | bytes 1572872 | tf_op jit(solution)/shard_map/ppermute | solution.py:247
  139.8 28.8 %collective-permute-start.8 = (bf16[8,256,128]{2,1,0:T(8,128)(2,1)S(1)}, bf16[8,256,128]{2,1,0:T(8,128)(2,1)S(1)}, u32[]{:S(2)}, u32[]{:S(2)}) collective-permute-start(bf16[8,256,128]{2,1,0:T(8,128)(2,1)S(1)} %combine_transition.2), channel_id=1, source_target_pairs={{8,16},{9,17},{10,18},{11,19},{12,20},{13,21},{14,22},{15,23},{16,... | collective-permute-start | bytes 1572872 | tf_op jit(solution)/shard_map/ppermute | solution.py:247
  145.9 22.8 %collective-permute-start.7 = (bf16[8,256,128]{2,1,0:T(8,128)(2,1)S(1)}, bf16[8,256,128]{2,1,0:T(8,128)(2,1)S(1)}, u32[]{:S(2)}, u32[]{:S(2)}) collective-permute-start(bf16[8,256,128]{2,1,0:T(8,128)(2,1)S(1)} %combine_transition.3.top_ref), channel_id=1, source_target_pairs={{8,24},{9,25},{10,26},{11,27},{12,28},{13,29},{14,30},{15,31},{16,... | collective-permute-start | bytes 1572872 | tf_op jit(solution)/shard_map/ppermute | solution.py:247

commit v5 on v4

--- a/solution.py
+++ b/solution.py
@@ -11,7 +11,7 @@
 epsilon = 1e-05
 LANES = 128
 VMEM_BYTES = 24 * 1024 * 1024
-SHARES = (8, 1, 3, 4)
+SHARES = (8, 1, 4, 3)
 FAR_FLOPS = 20_000_000_000
 AXES = ("groups", "seq", "role")
 
@@ -154,16 +154,21 @@
     parts, _, per, rows, width = got_ref.shape
     half = width // 2
     own = rows // 2
-    for item in range(per):
-        right = got_ref[:, 1, item].reshape(parts * rows, width)
+    for item in range(0, per, 2):
+        pair = range(item, min(item + 2, per))
+        right = [got_ref[:, 1, each].reshape(parts * rows, width) for each in pair]
         for slot in range(2):
             side = side_ref[0] if slot == 0 else 1 - side_ref[0]
             place = pl.ds(pl.multiple_of(side * half, LANES), half)
-            left = got_ref[:, 0, item, :, place].reshape(parts * rows, half)
+            left = [got_ref[:, 0, each, :, place].reshape(parts * rows, half) for each in pair]
             start = (slot * per + item) * own
-            sent_ref[:, start : start + own] = (
-                dot(left, right, (0, 0)).reshape(parts, own, width).astype(jnp.bfloat16)
-            )
+            sent_ref[:, start : start + len(pair) * own] = jnp.concatenate(
+                [
+                    dot(one, other, (0, 0)).reshape(parts, own, width)
+                    for one, other in zip(left, right)
+                ],
+                axis=1,
+            ).astype(jnp.bfloat16)
 
 
 def join_kernel(top_ref, bottom_ref, out_ref):
@@ -265,7 +270,6 @@
     side = lax.axis_index("seq") // half_seq
     home = side == lax.axis_index("groups") % 2
     side_flag = side.astype(jnp.int32).reshape(1)
-    other_side_flag = 1 - side_flag
     home_flag = home.astype(jnp.int32).reshape(1)
 
     def shape(*dims):
@@ -349,7 +353,9 @@
         near_out, [((g, s, c), (g ^ 1, s, c)) for g, s, c in every if not at_home(g, s)]
     )
     far = call(join_kernel, "join", shape(rows, width, channels), [], from_away, from_home)
-    return call(pick_kernel, "pick", shape(rows, width, channels), [], home_flag, near_out, from_near, far, flops=0)
+    return call(
+        pick_kernel, "pick", shape(rows, width, channels), [], home_flag, near_out, from_near, far
+    )
 
 
 def solution(mesh):

time: 170 us -> 170 us (level)
  no operation moved by 1% of the time
where the time goes in v5:
time: 170 us
  blocking collectives  83.9 us (49%)
  waiting for transfers between devices  39.6 us (23%)
  starting transfers between devices  22.8 us (13%)
  Pallas kernels  21.4 us (13%)
  local copies, waits for them, and re-layouts  1.88 us (1%)
    all_to_all x4, blocking collectives, exchange(): lax.all_to_all(value, AXES, split_axis=0, concat_axis=0, tiled=True, axis...  83.9 us
    ppermute x10, waiting for transfers between devices, permute(): lax.ppermute(value, AXES, [(number(*a), number(*b)) for a, b in pairs])  33.1 us
    pallas_call x9, Pallas kernels, call(): pl.pallas_call(kernel, in_specs=[smem if operand.dtype == jnp.int32 else...  20.1 us
    ppermute x10, starting transfers between devices, permute(): lax.ppermute(value, AXES, [(number(*a), number(*b)) for a, b in pairs])  15.5 us
    all_to_all x1, starting transfers between devices, exchange(): lax.all_to_all(value, AXES, split_axis=0, concat_axis=0, tiled=True, axis...  7.35 us
    all_to_all x1, waiting for transfers between devices, exchange(): lax.all_to_all(value, AXES, split_axis=0, concat_axis=0, tiled=True, axis...  6.5 us
  transfers between devices with their start and end apart: 11, of which 8 were waited for; matrix products, arithmetic and copies ran while one was open for 0% of the time, Pallas kernels for 5%

profile of v5, /device:TPU:25, one launch (start us, length us, event | category | flops | bytes accessed | tf_op | source)
XLA Modules:
  0.0 169.7 jit_solution(2296662958447217191)
XLA Ops:
  0.0 1.3 split.1
  1.3 1.3 collective-permute-start.1
  2.6 2.0 %collective-permute-start.3 = (bf16[8,256,128]{2,1,0:T(8,128)(2,1)S(1)}, bf16[8,256,128]{2,1,0:T(8,128)(2,1)S(1)}, u32[]{:S(2)}, u32[]{:S(2)}) collective-permute-start(bf16[8,256,128]{2,1,0:T(8,128)(2,1)S(1)} %get-tuple-element.18.own_ref), channel_id=1, source_target_pairs={{8,0},{9,1},{10,2},{11,3},{12,4},{13,5},{14,6},{15,7},{16,24},{17,... | collective-permute-start | bytes 1572872 | tf_op jit(solution)/shard_map/ppermute | solution.py:252
  4.7 3.9 %collective-permute-done.1.refs_1_ = bf16[4,256,128]{2,1,0:T(8,128)(2,1)S(1)} collective-permute-done((bf16[4,256,128]{2,1,0:T(8,128)(2,1)S(1)}, bf16[4,256,128]{2,1,0:T(8,128)(2,1)S(1)}, u32[]{:S(2)}, u32[]{:S(2)}) %collective-permute-start.1) | collective-permute-done | bytes 262176 | tf_op jit(solution)/shard_map/ppermute | solution.py:252
  8.6 1.3 collective-permute-start.5
  9.9 2.9 %collective-permute-done.2.refs_2_ = bf16[3,256,128]{2,1,0:T(8,128)(2,1)S(1)} collective-permute-done((bf16[3,256,128]{2,1,0:T(8,128)(2,1)S(1)}, bf16[3,256,128]{2,1,0:T(8,128)(2,1)S(1)}, u32[]{:S(2)}, u32[]{:S(2)}) %collective-permute-start.2) | collective-permute-done | bytes 196640 | tf_op jit(solution)/shard_map/ppermute | solution.py:252
  12.8 1.3 collective-permute-start.6
  14.1 1.3 collective-permute-start
  15.4 3.1 %collective-permute-start.4 = (bf16[1,256,128]{2,1,0:T(8,128)(2,1)S(1)}, bf16[1,256,128]{2,1,0:T(8,128)(2,1)S(1)}, u32[]{:S(2)}, u32[]{:S(2)}) collective-permute-start(bf16[1,256,128]{2,1,0:T(8,128)(2,1)S(1)} %get-tuple-element.21), channel_id=1, source_target_pairs={{8,16},{9,17},{10,18},{11,19},{12,20},{13,21},{14,22},{15,23},{16,... | collective-permute-start | bytes 196616 | tf_op jit(solution)/shard_map/ppermute | solution.py:252
  18.5 1.2 collective-permute-done.refs_0_
  19.7 2.4 %project.2 = (bf16[8,256,128]{2,1,0:T(8,128)(2,1)S(1)}, bf16[16,128,256]{2,1,0:T(8,128)(2,1)}) custom-call(s32[1]{0:T(128)} %bitcast.flag_ref, bf16[8,256,128]{2,1,0:T(8,128)(2,1)S(1)} %get-tuple-element.18.own_ref, f32[2,128]{1,0:T(2,128)S(1)} %get-tuple-element.19.gain_ref, bf16[2,128,512]{2,1,0:T(8,128)(2,1)S(1)} %get-tuple-element.20.proj_ref, ...), custom_call_target="tpu_custom_call" | custom-call | tf_op jit(solution)/shard_map/project/pallas_call | solution.py:213
  22.1 7.3 %all-to-all-start = ((bf16[16,128,256]{2,1,0:T(8,128)(2,1)}), bf16[16,128,256]{2,1,0:T(8,128)(2,1)S(1)}, u32[]{:S(2)}, u32[]{:S(2)}) async-start(bf16[16,128,256]{2,1,0:T(8,128)(2,1)} %get-tuple-element.26), calls=%async_computation | async-start | bytes 2097152 | tf_op jit(solution)/shard_map/all_to_all | solution.py:266
  29.5 3.7 %collective-permute-done.4.refs_0_ = bf16[1,256,128]{2,1,0:T(8,128)(2,1)S(1)} collective-permute-done((bf16[1,256,128]{2,1,0:T(8,128)(2,1)S(1)}, bf16[1,256,128]{2,1,0:T(8,128)(2,1)S(1)}, u32[]{:S(2)}, u32[]{:S(2)}) %collective-permute-start.4) | collective-permute-done | bytes 65568 | tf_op jit(solution)/shard_map/ppermute | solution.py:252
  33.4 0.8 copy-done.8
  34.2 1.0 copy-done.9
  35.3 2.4 %project.3 = (bf16[8,256,128]{2,1,0:T(8,128)(2,1)S(1)}, bf16[16,128,256]{2,1,0:T(8,128)(2,1)S(1)}) custom-call(s32[1]{0:T(128)} %bitcast.flag_ref, bf16[8,256,128]{2,1,0:T(8,128)(2,1)S(1)} %copy-done.9, f32[2,128]{1,0:T(2,128)S(1)} %get-tuple-element.19.gain_ref, bf16[2,128,512]{2,1,0:T(8,128)(2,1)S(1)} %get-tuple-element.20.proj_ref, ...), custom_call_target="tpu_custom_call" | custom-call | flops 99999997952 | tf_op jit(solution)/shard_map/project/pallas_call | solution.py:213
  37.7 6.5 %all-to-all-done.near_ref = bf16[16,128,256]{2,1,0:T(8,128)(2,1)S(1)} async-done(((bf16[16,128,256]{2,1,0:T(8,128)(2,1)}), bf16[16,128,256]{2,1,0:T(8,128)(2,1)S(1)}, u32[]{:S(2)}, u32[]{:S(2)}) %all-to-all-start) | async-done | bytes 1048608 | tf_op jit(solution)/shard_map/all_to_all | solution.py:266
  44.2 19.6 %all_to_all.25.far_ref = bf16[16,128,256]{2,1,0:T(8,128)(2,1)S(1)} all-to-all(bf16[16,128,256]{2,1,0:T(8,128)(2,1)S(1)} %get-tuple-element.27), channel_id=1, replica_groups={{0,16,1,17,2,18,3,19,4,20,5,21,6,22,7,23},{24,8,25,9,26,10,27,11,28,12,..., dimensions={0} | all-to-all | bytes 2097152 | tf_op jit(solution)/shard_map/all_to_all | solution.py:266
  63.9 0.7 outgoing.1
  64.6 17.6 %all_to_all.26 = bf16[16,8,16,256]{3,2,1,0:T(8,128)(2,1)S(1)} all-to-all(bf16[16,8,16,256]{3,2,1,0:T(8,128)(2,1)S(1)} %outgoing.1), channel_id=1, replica_groups={{0,16,1,17,2,18,3,19,4,20,5,21,6,22,7,23},{24,8,25,9,26,10,27,11,28,12,..., dimensions={0} | all-to-all | bytes 2097152 | tf_op jit(solution)/shard_map/all_to_all | solution.py:266
  82.3 5.3 %combine_project.1 = (bf16[16,256,128]{2,1,0:T(8,128)(2,1)S(1)}, bf16[16,256,256]{2,1,0:T(8,128)(2,1)S(1)}) custom-call(bf16[8,256,128]{2,1,0:T(8,128)(2,1)S(1)} %get-tuple-element.24.near_ref, bf16[8,256,128]{2,1,0:T(8,128)(2,1)S(1)} %get-tuple-element.25.far_ref, bf16[16,128,256]{2,1,0:T(8,128)(2,1)S(1)} %bitcast.6, f32[2,128]{1,0:T(2,128)S(1)} %copy-done.5, ...), custom_call_target="tpu_custom_call" | custom-call | tf_op jit(solution)/shard_map/combine_project/pallas_call | solution.py:213
  87.6 28.9 %all_to_all.27 = bf16[16,256,256]{2,1,0:T(8,128)(2,1)S(1)} all-to-all(bf16[16,256,256]{2,1,0:T(8,128)(2,1)S(1)} %get-tuple-element.29), channel_id=1, replica_groups={{0,16,1,17,2,18,3,19,4,20,5,21,6,22,7,23},{24,8,25,9,26,10,27,11,28,12,..., dimensions={0} | all-to-all | bytes 4194304 | tf_op jit(solution)/shard_map/all_to_all | solution.py:266
  116.5 0.5 incoming.1
  117.0 17.7 %all_to_all.28.got_ref = bf16[16,128,256]{2,1,0:T(8,128)(2,1)S(1)} all-to-all(bf16[16,128,256]{2,1,0:T(8,128)(2,1)S(1)} %incoming.1), channel_id=1, replica_groups={{0,16,1,17,2,18,3,19,4,20,5,21,6,22,7,23},{24,8,25,9,26,10,27,11,28,12,..., dimensions={0} | all-to-all | bytes 2097152 | tf_op jit(solution)/shard_map/all_to_all | solution.py:266
  134.7 3.8 %combine_transition.2 = bf16[8,256,128]{2,1,0:T(8,128)(2,1)S(1)} custom-call(bf16[16,256,128]{2,1,0:T(8,128)(2,1)S(1)} %get-tuple-element.28.pair_ref, bf16[16,128,256]{2,1,0:T(8,128)(2,1)S(1)} %all_to_all.28.got_ref, f32[2,128]{1,0:T(2,128)S(1)} %copy-done.5, bf16[2,128,128]{2,1,0:T(8,128)(2,1)S(1)} %copy-done.2, f32[2,128]{1,0:T(2,128)S(1)} %copy-done.6, ...), custom_call_target="tpu_custom_call" | custom-call | tf_op jit(solution)/shard_map/combine_transition/pallas_call | solution.py:213
  138.5 1.3 collective-permute-start.9
  139.8 2.3 %collective-permute-start.8 = (bf16[8,256,128]{2,1,0:T(8,128)(2,1)S(1)}, bf16[8,256,128]{2,1,0:T(8,128)(2,1)S(1)}, u32[]{:S(2)}, u32[]{:S(2)}) collective-permute-start(bf16[8,256,128]{2,1,0:T(8,128)(2,1)S(1)} %combine_transition.2), channel_id=1, source_target_pairs={{8,16},{9,17},{10,18},{11,19},{12,20},{13,21},{14,22},{15,23},{16,... | collective-permute-start | bytes 1572872 | tf_op jit(solution)/shard_map/ppermute | solution.py:252
  142.1 3.8 %combine_transition.3.top_ref = bf16[8,256,128]{2,1,0:T(8,128)(2,1)S(1)} custom-call(bf16[16,256,128]{2,1,0:T(8,128)(2,1)S(1)} %get-tuple-element.28.pair_ref, bf16[16,128,256]{2,1,0:T(8,128)(2,1)S(1)} %all_to_all.28.got_ref, f32[2,128]{1,0:T(2,128)S(1)} %copy-done.5, bf16[2,128,128]{2,1,0:T(8,128)(2,1)S(1)} %copy-done.2, f32[2,128]{1,0:T(2,128)S(1)} %copy-done.6, ...), custom_call_target="tpu_custom_call" | custom-call | flops 20000000000 | tf_op jit(solution)/shard_map/combine_transition/pallas_call | solution.py:213
  145.9 1.6 collective-permute-start.7
  147.5 18.8 %collective-permute-done.9.bottom_ref = bf16[8,256,128]{2,1,0:T(8,128)(2,1)S(1)} collective-permute-done((bf16[8,256,128]{2,1,0:T(8,128)(2,1)S(1)}, bf16[8,256,128]{2,1,0:T(8,128)(2,1)S(1)}, u32[]{:S(2)}, u32[]{:S(2)}) %collective-permute-start.9) | collective-permute-done | bytes 524320 | tf_op jit(solution)/shard_map/ppermute | solution.py:252
  166.4 2.2 %collective-permute-done.8.top_ref = bf16[8,256,128]{2,1,0:T(8,128)(2,1)S(1)} collective-permute-done((bf16[8,256,128]{2,1,0:T(8,128)(2,1)S(1)}, bf16[8,256,128]{2,1,0:T(8,128)(2,1)S(1)}, u32[]{:S(2)}, u32[]{:S(2)}) %collective-permute-start.8) | collective-permute-done | bytes 524320 | tf_op jit(solution)/shard_map/ppermute | solution.py:252
  168.6 1.1 pick.1
  (24 shorter events, 0.4 us)
Async XLA Ops:
  1.3 7.2 %collective-permute-start.1 = (bf16[4,256,128]{2,1,0:T(8,128)(2,1)S(1)}, bf16[4,256,128]{2,1,0:T(8,128)(2,1)S(1)}, u32[]{:S(2)}, u32[]{:S(2)}) collective-permute-start(bf16[4,256,128]{2,1,0:T(8,128)(2,1)S(1)} %get-tuple-element.22), channel_id=1, source_target_pairs={{0,16},{1,17},{2,18},{3,19},{4,20},{5,21},{6,22},{7,23},{8,24},{9,... | collective-permute-start | bytes 786440 | tf_op jit(solution)/shard_map/ppermute | solution.py:252
  2.6 30.8 %collective-permute-start.3 = (bf16[8,256,128]{2,1,0:T(8,128)(2,1)S(1)}, bf16[8,256,128]{2,1,0:T(8,128)(2,1)S(1)}, u32[]{:S(2)}, u32[]{:S(2)}) collective-permute-start(bf16[8,256,128]{2,1,0:T(8,128)(2,1)S(1)} %get-tuple-element.18.own_ref), channel_id=1, source_target_pairs={{8,0},{9,1},{10,2},{11,3},{12,4},{13,5},{14,6},{15,7},{16,24},{17,... | collective-permute-start | bytes 1572872 | tf_op jit(solution)/shard_map/ppermute | solution.py:252
  4.6 8.2 %collective-permute-start.2 = (bf16[3,256,128]{2,1,0:T(8,128)(2,1)S(1)}, bf16[3,256,128]{2,1,0:T(8,128)(2,1)S(1)}, u32[]{:S(2)}, u32[]{:S(2)}) collective-permute-start(bf16[3,256,128]{2,1,0:T(8,128)(2,1)S(1)} %get-tuple-element.23), channel_id=1, source_target_pairs={{0,16},{1,17},{2,18},{3,19},{4,20},{5,21},{6,22},{7,23},{8,24},{9,... | collective-permute-start | bytes 589832 | tf_op jit(solution)/shard_map/ppermute | solution.py:252
  8.6 24.8 %collective-permute-start.5 = (bf16[4,256,128]{2,1,0:T(8,128)(2,1)S(1)}, bf16[4,256,128]{2,1,0:T(8,128)(2,1)}, u32[]{:S(2)}, u32[]{:S(2)}) collective-permute-start(bf16[4,256,128]{2,1,0:T(8,128)(2,1)S(1)} %collective-permute-done.1.refs_1_), channel_id=1, source_target_pairs={{0,8},{1,9},{2,10},{3,11},{4,12},{5,13},{6,14},{7,15},{24,16},{25,... | collective-permute-start | bytes 786440 | tf_op jit(solution)/shard_map/ppermute | solution.py:252
  12.8 20.6 %collective-permute-start.6 = (bf16[3,256,128]{2,1,0:T(8,128)(2,1)S(1)}, bf16[3,256,128]{2,1,0:T(8,128)(2,1)}, u32[]{:S(2)}, u32[]{:S(2)}) collective-permute-start(bf16[3,256,128]{2,1,0:T(8,128)(2,1)S(1)} %collective-permute-done.2.refs_2_), channel_id=1, source_target_pairs={{0,8},{1,9},{2,10},{3,11},{4,12},{5,13},{6,14},{7,15},{24,16},{25,... | collective-permute-start | bytes 589832 | tf_op jit(solution)/shard_map/ppermute | solution.py:252
  14.1 5.6 %collective-permute-start = (bf16[1,256,128]{2,1,0:T(8,128)(2,1)S(1)}, bf16[1,256,128]{2,1,0:T(8,128)(2,1)S(1)}, u32[]{:S(2)}, u32[]{:S(2)}) collective-permute-start(bf16[1,256,128]{2,1,0:T(8,128)(2,1)S(1)} %get-tuple-element.21), channel_id=1, source_target_pairs={{0,16},{1,17},{2,18},{3,19},{4,20},{5,21},{6,22},{7,23},{24,8},{25... | collective-permute-start | bytes 196616 | tf_op jit(solution)/shard_map/ppermute | solution.py:252
  15.4 17.8 %collective-permute-start.4 = (bf16[1,256,128]{2,1,0:T(8,128)(2,1)S(1)}, bf16[1,256,128]{2,1,0:T(8,128)(2,1)S(1)}, u32[]{:S(2)}, u32[]{:S(2)}) collective-permute-start(bf16[1,256,128]{2,1,0:T(8,128)(2,1)S(1)} %get-tuple-element.21), channel_id=1, source_target_pairs={{8,16},{9,17},{10,18},{11,19},{12,20},{13,21},{14,22},{15,23},{16,... | collective-permute-start | bytes 196616 | tf_op jit(solution)/shard_map/ppermute | solution.py:252
  22.1 22.1 %all-to-all-start = ((bf16[16,128,256]{2,1,0:T(8,128)(2,1)}), bf16[16,128,256]{2,1,0:T(8,128)(2,1)S(1)}, u32[]{:S(2)}, u32[]{:S(2)}) async-start(bf16[16,128,256]{2,1,0:T(8,128)(2,1)} %get-tuple-element.26), calls=%async_computation | async-start | bytes 2097152 | tf_op jit(solution)/shard_map/all_to_all | solution.py:266
  33.4 0.8 copy-start.8
  34.2 1.0 copy-start.9
  63.8 18.4 %copy-start = (bf16[2,128,512]{2,1,0:T(8,128)(2,1)S(1)}, bf16[2,128,512]{2,1,0:T(8,128)(2,1)}, u32[]{:S(2)}) copy-start(bf16[2,128,512]{2,1,0:T(8,128)(2,1)} %proj_ref.3) | copy-start | bytes 786436
  63.8 18.4 %copy-start.2 = (bf16[2,128,128]{2,1,0:T(8,128)(2,1)S(1)}, bf16[2,128,128]{2,1,0:T(8,128)(2,1)}, u32[]{:S(2)}) copy-start(bf16[2,128,128]{2,1,0:T(8,128)(2,1)} %gate_ref.5) | copy-start | bytes 196612
  63.8 18.4 %copy-start.3 = (bf16[2,128,128]{2,1,0:T(8,128)(2,1)S(1)}, bf16[2,128,128]{2,1,0:T(8,128)(2,1)}, u32[]{:S(2)}) copy-start(bf16[2,128,128]{2,1,0:T(8,128)(2,1)} %out_ref.5) | copy-start | bytes 196612
  63.8 18.4 %copy-start.5 = (f32[2,128]{1,0:T(2,128)S(1)}, f32[2,128]{1,0:T(2,128)}, u32[]{:S(2)}) copy-start(f32[2,128]{1,0:T(2,128)} %gain_ref.7) | copy-start | bytes 3076
  63.8 18.4 %copy-start.6 = (f32[2,128]{1,0:T(2,128)S(1)}, f32[2,128]{1,0:T(2,128)}, u32[]{:S(2)}) copy-start(f32[2,128]{1,0:T(2,128)} %mid_gain_ref.5) | copy-start | bytes 3076
  116.5 18.3 %copy-start.1 = (bf16[128,1024]{1,0:T(8,128)(2,1)S(1)}, bf16[128,1024]{1,0:T(8,128)(2,1)}, u32[]{:S(2)}) copy-start(bf16[128,1024]{1,0:T(8,128)(2,1)} %up_ref.3) | copy-start | bytes 786436
  116.5 18.3 %copy-start.4 = (bf16[512,128]{1,0:T(8,128)(2,1)S(1)}, bf16[512,128]{1,0:T(8,128)(2,1)}, u32[]{:S(2)}) copy-start(bf16[512,128]{1,0:T(8,128)(2,1)} %down_ref.3) | copy-start | bytes 393220
  116.5 18.3 %copy-start.7 = (f32[128]{0:T(128)S(1)}, f32[128]{0:T(128)}, u32[]{:S(2)}) copy-start(f32[128]{0:T(128)} %param.15) | copy-start | bytes 1540
  138.5 27.9 %collective-permute-start.9 = (bf16[8,256,128]{2,1,0:T(8,128)(2,1)S(1)}, bf16[8,256,128]{2,1,0:T(8,128)(2,1)S(1)}, u32[]{:S(2)}, u32[]{:S(2)}) collective-permute-start(bf16[8,256,128]{2,1,0:T(8,128)(2,1)S(1)} %combine_transition.2), channel_id=1, source_target_pairs={{0,8},{1,9},{2,10},{3,11},{4,12},{5,13},{6,14},{7,15},{24,16},{25,... | collective-permute-start | bytes 1572872 | tf_op jit(solution)/shard_map/ppermute | solution.py:252
  139.8 28.8 %collective-permute-start.8 = (bf16[8,256,128]{2,1,0:T(8,128)(2,1)S(1)}, bf16[8,256,128]{2,1,0:T(8,128)(2,1)S(1)}, u32[]{:S(2)}, u32[]{:S(2)}) collective-permute-start(bf16[8,256,128]{2,1,0:T(8,128)(2,1)S(1)} %combine_transition.2), channel_id=1, source_target_pairs={{8,16},{9,17},{10,18},{11,19},{12,20},{13,21},{14,22},{15,23},{16,... | collective-permute-start | bytes 1572872 | tf_op jit(solution)/shard_map/ppermute | solution.py:252
  145.9 22.8 %collective-permute-start.7 = (bf16[8,256,128]{2,1,0:T(8,128)(2,1)S(1)}, bf16[8,256,128]{2,1,0:T(8,128)(2,1)S(1)}, u32[]{:S(2)}, u32[]{:S(2)}) collective-permute-start(bf16[8,256,128]{2,1,0:T(8,128)(2,1)S(1)} %combine_transition.3.top_ref), channel_id=1, source_target_pairs={{8,24},{9,25},{10,26},{11,27},{12,28},{13,29},{14,30},{15,31},{16,... | collective-permute-start | bytes 1572872 | tf_op jit(solution)/shard_map/ppermute | solution.py:252

commit v6 on v5

--- a/solution.py
+++ b/solution.py
@@ -57,16 +57,20 @@
     average = jnp.mean(got, axis=0, keepdims=True)
     centred = got - average
     spread = jnp.mean(centred * centred, axis=0, keepdims=True)
-    scratch_ref[: inner * rows] = (centred * lax.rsqrt(spread + epsilon)).reshape(
-        inner * rows, lanes
-    )
+    centred = centred * lax.rsqrt(spread + epsilon)
     normed = norm_lanes(pair, gain_ref[which : which + 1])
     gating = jax.nn.sigmoid(dot(normed, gate_ref[which], (1, 0)))
     mid_gain = jnp.broadcast_to(mid_gain_ref[which : which + 1], (lanes, inner)).T
-    updates = []
-    for row in range(rows):
-        mid = (scratch_ref[pl.ds(row, inner, stride=rows), :] * mid_gain).astype(jnp.bfloat16)
-        updates.append(dot(mid, out_ref[which], (0, 0)))
+    if rows % 16 == 0:
+        mids = jnp.swapaxes((centred * mid_gain.reshape(inner, 1, lanes)).astype(jnp.bfloat16), 0, 1)
+        mids = [mids[row] for row in range(rows)]
+    else:
+        scratch_ref[: inner * rows] = centred.reshape(inner * rows, lanes)
+        mids = [
+            (scratch_ref[pl.ds(row, inner, stride=rows), :] * mid_gain).astype(jnp.bfloat16)
+            for row in range(rows)
+        ]
+    updates = [dot(mid, out_ref[which], (0, 0)) for mid in mids]
     update = jnp.concatenate(updates, axis=0)
     return (pair.astype(jnp.float32) + gating * update).astype(jnp.bfloat16)
 

time: 170 us -> 170 us (level)
  no operation moved by 1% of the time
where the time goes in v6:
time: 170 us; the launch traced here: 169 us
  blocking collectives  83.9 us (49%)
  waiting for transfers between devices  39.6 us (23%)
  starting transfers between devices  22.8 us (13%)
  Pallas kernels  20.8 us (12%)
  local copies, waits for them, and re-layouts  1.88 us (1%)
    all_to_all x4, blocking collectives, exchange(): lax.all_to_all(value, AXES, split_axis=0, concat_axis=0, tiled=True, axis...  83.9 us
    ppermute x10, waiting for transfers between devices, permute(): lax.ppermute(value, AXES, [(number(*a), number(*b)) for a, b in pairs])  33.1 us
    pallas_call x9, Pallas kernels, call(): pl.pallas_call(kernel, in_specs=[smem if operand.dtype == jnp.int32 else...  19.4 us
    ppermute x10, starting transfers between devices, permute(): lax.ppermute(value, AXES, [(number(*a), number(*b)) for a, b in pairs])  15.5 us
    all_to_all x1, starting transfers between devices, exchange(): lax.all_to_all(value, AXES, split_axis=0, concat_axis=0, tiled=True, axis...  7.35 us
    all_to_all x1, waiting for transfers between devices, exchange(): lax.all_to_all(value, AXES, split_axis=0, concat_axis=0, tiled=True, axis...  6.5 us
  transfers between devices with their start and end apart: 11, of which 8 were waited for; matrix products, arithmetic and copies ran while one was open for 0% of the time, Pallas kernels for 5%

profile of v6, /device:TPU:25, one launch (start us, length us, event | category | flops | bytes accessed | tf_op | source)
XLA Modules:
  0.0 169.1 jit_solution(505812831931579259)
XLA Ops:
  0.0 1.3 split.1
  1.3 1.3 collective-permute-start.1
  2.6 2.0 %collective-permute-start.3 = (bf16[8,256,128]{2,1,0:T(8,128)(2,1)S(1)}, bf16[8,256,128]{2,1,0:T(8,128)(2,1)S(1)}, u32[]{:S(2)}, u32[]{:S(2)}) collective-permute-start(bf16[8,256,128]{2,1,0:T(8,128)(2,1)S(1)} %get-tuple-element.18.own_ref), channel_id=1, source_target_pairs={{8,0},{9,1},{10,2},{11,3},{12,4},{13,5},{14,6},{15,7},{16,24},{17,... | collective-permute-start | bytes 1572872 | tf_op jit(solution)/shard_map/ppermute | solution.py:256
  4.7 3.9 %collective-permute-done.1.refs_1_ = bf16[4,256,128]{2,1,0:T(8,128)(2,1)S(1)} collective-permute-done((bf16[4,256,128]{2,1,0:T(8,128)(2,1)S(1)}, bf16[4,256,128]{2,1,0:T(8,128)(2,1)S(1)}, u32[]{:S(2)}, u32[]{:S(2)}) %collective-permute-start.1) | collective-permute-done | bytes 262176 | tf_op jit(solution)/shard_map/ppermute | solution.py:256
  8.6 1.3 collective-permute-start.5
  9.9 2.9 %collective-permute-done.2.refs_2_ = bf16[3,256,128]{2,1,0:T(8,128)(2,1)S(1)} collective-permute-done((bf16[3,256,128]{2,1,0:T(8,128)(2,1)S(1)}, bf16[3,256,128]{2,1,0:T(8,128)(2,1)S(1)}, u32[]{:S(2)}, u32[]{:S(2)}) %collective-permute-start.2) | collective-permute-done | bytes 196640 | tf_op jit(solution)/shard_map/ppermute | solution.py:256
  12.8 1.3 collective-permute-start.6
  14.1 1.3 collective-permute-start
  15.4 3.1 %collective-permute-start.4 = (bf16[1,256,128]{2,1,0:T(8,128)(2,1)S(1)}, bf16[1,256,128]{2,1,0:T(8,128)(2,1)S(1)}, u32[]{:S(2)}, u32[]{:S(2)}) collective-permute-start(bf16[1,256,128]{2,1,0:T(8,128)(2,1)S(1)} %get-tuple-element.21), channel_id=1, source_target_pairs={{8,16},{9,17},{10,18},{11,19},{12,20},{13,21},{14,22},{15,23},{16,... | collective-permute-start | bytes 196616 | tf_op jit(solution)/shard_map/ppermute | solution.py:256
  18.5 1.2 collective-permute-done.refs_0_
  19.7 2.4 %project.2 = (bf16[8,256,128]{2,1,0:T(8,128)(2,1)S(1)}, bf16[16,128,256]{2,1,0:T(8,128)(2,1)}) custom-call(s32[1]{0:T(128)} %bitcast.flag_ref, bf16[8,256,128]{2,1,0:T(8,128)(2,1)S(1)} %get-tuple-element.18.own_ref, f32[2,128]{1,0:T(2,128)S(1)} %get-tuple-element.19.gain_ref, bf16[2,128,512]{2,1,0:T(8,128)(2,1)S(1)} %get-tuple-element.20.proj_ref, ...), custom_call_target="tpu_custom_call" | custom-call | tf_op jit(solution)/shard_map/project/pallas_call | solution.py:217
  22.1 7.3 %all-to-all-start = ((bf16[16,128,256]{2,1,0:T(8,128)(2,1)}), bf16[16,128,256]{2,1,0:T(8,128)(2,1)S(1)}, u32[]{:S(2)}, u32[]{:S(2)}) async-start(bf16[16,128,256]{2,1,0:T(8,128)(2,1)} %get-tuple-element.26), calls=%async_computation | async-start | bytes 2097152 | tf_op jit(solution)/shard_map/all_to_all | solution.py:270
  29.5 3.7 %collective-permute-done.4.refs_0_ = bf16[1,256,128]{2,1,0:T(8,128)(2,1)S(1)} collective-permute-done((bf16[1,256,128]{2,1,0:T(8,128)(2,1)S(1)}, bf16[1,256,128]{2,1,0:T(8,128)(2,1)S(1)}, u32[]{:S(2)}, u32[]{:S(2)}) %collective-permute-start.4) | collective-permute-done | bytes 65568 | tf_op jit(solution)/shard_map/ppermute | solution.py:256
  33.4 0.8 copy-done.8
  34.2 1.0 copy-done.9
  35.3 2.4 %project.3 = (bf16[8,256,128]{2,1,0:T(8,128)(2,1)S(1)}, bf16[16,128,256]{2,1,0:T(8,128)(2,1)S(1)}) custom-call(s32[1]{0:T(128)} %bitcast.flag_ref, bf16[8,256,128]{2,1,0:T(8,128)(2,1)S(1)} %copy-done.9, f32[2,128]{1,0:T(2,128)S(1)} %get-tuple-element.19.gain_ref, bf16[2,128,512]{2,1,0:T(8,128)(2,1)S(1)} %get-tuple-element.20.proj_ref, ...), custom_call_target="tpu_custom_call" | custom-call | flops 99999997952 | tf_op jit(solution)/shard_map/project/pallas_call | solution.py:217
  37.7 6.5 %all-to-all-done.near_ref = bf16[16,128,256]{2,1,0:T(8,128)(2,1)S(1)} async-done(((bf16[16,128,256]{2,1,0:T(8,128)(2,1)}), bf16[16,128,256]{2,1,0:T(8,128)(2,1)S(1)}, u32[]{:S(2)}, u32[]{:S(2)}) %all-to-all-start) | async-done | bytes 1048608 | tf_op jit(solution)/shard_map/all_to_all | solution.py:270
  44.2 19.6 %all_to_all.25.far_ref = bf16[16,128,256]{2,1,0:T(8,128)(2,1)S(1)} all-to-all(bf16[16,128,256]{2,1,0:T(8,128)(2,1)S(1)} %get-tuple-element.27), channel_id=1, replica_groups={{0,16,1,17,2,18,3,19,4,20,5,21,6,22,7,23},{24,8,25,9,26,10,27,11,28,12,..., dimensions={0} | all-to-all | bytes 2097152 | tf_op jit(solution)/shard_map/all_to_all | solution.py:270
  63.9 0.7 outgoing.1
  64.6 17.6 %all_to_all.26 = bf16[16,8,16,256]{3,2,1,0:T(8,128)(2,1)S(1)} all-to-all(bf16[16,8,16,256]{3,2,1,0:T(8,128)(2,1)S(1)} %outgoing.1), channel_id=1, replica_groups={{0,16,1,17,2,18,3,19,4,20,5,21,6,22,7,23},{24,8,25,9,26,10,27,11,28,12,..., dimensions={0} | all-to-all | bytes 2097152 | tf_op jit(solution)/shard_map/all_to_all | solution.py:270
  82.3 4.7 %combine_project.1 = (bf16[16,256,128]{2,1,0:T(8,128)(2,1)S(1)}, bf16[16,256,256]{2,1,0:T(8,128)(2,1)S(1)}) custom-call(bf16[8,256,128]{2,1,0:T(8,128)(2,1)S(1)} %get-tuple-element.24.near_ref, bf16[8,256,128]{2,1,0:T(8,128)(2,1)S(1)} %get-tuple-element.25.far_ref, bf16[16,128,256]{2,1,0:T(8,128)(2,1)S(1)} %bitcast.6, f32[2,128]{1,0:T(2,128)S(1)} %copy-done.5, ...), custom_call_target="tpu_custom_call" | custom-call | tf_op jit(solution)/shard_map/combine_project/pallas_call | solution.py:217
  87.0 28.9 %all_to_all.27 = bf16[16,256,256]{2,1,0:T(8,128)(2,1)S(1)} all-to-all(bf16[16,256,256]{2,1,0:T(8,128)(2,1)S(1)} %get-tuple-element.29), channel_id=1, replica_groups={{0,16,1,17,2,18,3,19,4,20,5,21,6,22,7,23},{24,8,25,9,26,10,27,11,28,12,..., dimensions={0} | all-to-all | bytes 4194304 | tf_op jit(solution)/shard_map/all_to_all | solution.py:270
  115.9 0.5 incoming.1
  116.4 17.7 %all_to_all.28.got_ref = bf16[16,128,256]{2,1,0:T(8,128)(2,1)S(1)} all-to-all(bf16[16,128,256]{2,1,0:T(8,128)(2,1)S(1)} %incoming.1), channel_id=1, replica_groups={{0,16,1,17,2,18,3,19,4,20,5,21,6,22,7,23},{24,8,25,9,26,10,27,11,28,12,..., dimensions={0} | all-to-all | bytes 2097152 | tf_op jit(solution)/shard_map/all_to_all | solution.py:270
  134.1 3.8 %combine_transition.2 = bf16[8,256,128]{2,1,0:T(8,128)(2,1)S(1)} custom-call(bf16[16,256,128]{2,1,0:T(8,128)(2,1)S(1)} %get-tuple-element.28.pair_ref, bf16[16,128,256]{2,1,0:T(8,128)(2,1)S(1)} %all_to_all.28.got_ref, f32[2,128]{1,0:T(2,128)S(1)} %copy-done.5, bf16[2,128,128]{2,1,0:T(8,128)(2,1)S(1)} %copy-done.2, f32[2,128]{1,0:T(2,128)S(1)} %copy-done.6, ...), custom_call_target="tpu_custom_call" | custom-call | tf_op jit(solution)/shard_map/combine_transition/pallas_call | solution.py:217
  137.9 1.3 collective-permute-start.9
  139.2 2.3 %collective-permute-start.8 = (bf16[8,256,128]{2,1,0:T(8,128)(2,1)S(1)}, bf16[8,256,128]{2,1,0:T(8,128)(2,1)S(1)}, u32[]{:S(2)}, u32[]{:S(2)}) collective-permute-start(bf16[8,256,128]{2,1,0:T(8,128)(2,1)S(1)} %combine_transition.2), channel_id=1, source_target_pairs={{8,16},{9,17},{10,18},{11,19},{12,20},{13,21},{14,22},{15,23},{16,... | collective-permute-start | bytes 1572872 | tf_op jit(solution)/shard_map/ppermute | solution.py:256
  141.5 3.8 %combine_transition.3.top_ref = bf16[8,256,128]{2,1,0:T(8,128)(2,1)S(1)} custom-call(bf16[16,256,128]{2,1,0:T(8,128)(2,1)S(1)} %get-tuple-element.28.pair_ref, bf16[16,128,256]{2,1,0:T(8,128)(2,1)S(1)} %all_to_all.28.got_ref, f32[2,128]{1,0:T(2,128)S(1)} %copy-done.5, bf16[2,128,128]{2,1,0:T(8,128)(2,1)S(1)} %copy-done.2, f32[2,128]{1,0:T(2,128)S(1)} %copy-done.6, ...), custom_call_target="tpu_custom_call" | custom-call | flops 20000000000 | tf_op jit(solution)/shard_map/combine_transition/pallas_call | solution.py:217
  145.3 1.6 collective-permute-start.7
  146.9 18.8 %collective-permute-done.9.bottom_ref = bf16[8,256,128]{2,1,0:T(8,128)(2,1)S(1)} collective-permute-done((bf16[8,256,128]{2,1,0:T(8,128)(2,1)S(1)}, bf16[8,256,128]{2,1,0:T(8,128)(2,1)S(1)}, u32[]{:S(2)}, u32[]{:S(2)}) %collective-permute-start.9) | collective-permute-done | bytes 524320 | tf_op jit(solution)/shard_map/ppermute | solution.py:256
  165.7 2.2 %collective-permute-done.8.top_ref = bf16[8,256,128]{2,1,0:T(8,128)(2,1)S(1)} collective-permute-done((bf16[8,256,128]{2,1,0:T(8,128)(2,1)S(1)}, bf16[8,256,128]{2,1,0:T(8,128)(2,1)S(1)}, u32[]{:S(2)}, u32[]{:S(2)}) %collective-permute-start.8) | collective-permute-done | bytes 524320 | tf_op jit(solution)/shard_map/ppermute | solution.py:256
  168.0 1.1 pick.1
  (24 shorter events, 0.4 us)
Async XLA Ops:
  1.3 7.2 %collective-permute-start.1 = (bf16[4,256,128]{2,1,0:T(8,128)(2,1)S(1)}, bf16[4,256,128]{2,1,0:T(8,128)(2,1)S(1)}, u32[]{:S(2)}, u32[]{:S(2)}) collective-permute-start(bf16[4,256,128]{2,1,0:T(8,128)(2,1)S(1)} %get-tuple-element.22), channel_id=1, source_target_pairs={{0,16},{1,17},{2,18},{3,19},{4,20},{5,21},{6,22},{7,23},{8,24},{9,... | collective-permute-start | bytes 786440 | tf_op jit(solution)/shard_map/ppermute | solution.py:256
  2.6 30.8 %collective-permute-start.3 = (bf16[8,256,128]{2,1,0:T(8,128)(2,1)S(1)}, bf16[8,256,128]{2,1,0:T(8,128)(2,1)S(1)}, u32[]{:S(2)}, u32[]{:S(2)}) collective-permute-start(bf16[8,256,128]{2,1,0:T(8,128)(2,1)S(1)} %get-tuple-element.18.own_ref), channel_id=1, source_target_pairs={{8,0},{9,1},{10,2},{11,3},{12,4},{13,5},{14,6},{15,7},{16,24},{17,... | collective-permute-start | bytes 1572872 | tf_op jit(solution)/shard_map/ppermute | solution.py:256
  4.6 8.2 %collective-permute-start.2 = (bf16[3,256,128]{2,1,0:T(8,128)(2,1)S(1)}, bf16[3,256,128]{2,1,0:T(8,128)(2,1)S(1)}, u32[]{:S(2)}, u32[]{:S(2)}) collective-permute-start(bf16[3,256,128]{2,1,0:T(8,128)(2,1)S(1)} %get-tuple-element.23), channel_id=1, source_target_pairs={{0,16},{1,17},{2,18},{3,19},{4,20},{5,21},{6,22},{7,23},{8,24},{9,... | collective-permute-start | bytes 589832 | tf_op jit(solution)/shard_map/ppermute | solution.py:256
  8.6 24.8 %collective-permute-start.5 = (bf16[4,256,128]{2,1,0:T(8,128)(2,1)S(1)}, bf16[4,256,128]{2,1,0:T(8,128)(2,1)}, u32[]{:S(2)}, u32[]{:S(2)}) collective-permute-start(bf16[4,256,128]{2,1,0:T(8,128)(2,1)S(1)} %collective-permute-done.1.refs_1_), channel_id=1, source_target_pairs={{0,8},{1,9},{2,10},{3,11},{4,12},{5,13},{6,14},{7,15},{24,16},{25,... | collective-permute-start | bytes 786440 | tf_op jit(solution)/shard_map/ppermute | solution.py:256
  12.8 20.6 %collective-permute-start.6 = (bf16[3,256,128]{2,1,0:T(8,128)(2,1)S(1)}, bf16[3,256,128]{2,1,0:T(8,128)(2,1)}, u32[]{:S(2)}, u32[]{:S(2)}) collective-permute-start(bf16[3,256,128]{2,1,0:T(8,128)(2,1)S(1)} %collective-permute-done.2.refs_2_), channel_id=1, source_target_pairs={{0,8},{1,9},{2,10},{3,11},{4,12},{5,13},{6,14},{7,15},{24,16},{25,... | collective-permute-start | bytes 589832 | tf_op jit(solution)/shard_map/ppermute | solution.py:256
  14.1 5.6 %collective-permute-start = (bf16[1,256,128]{2,1,0:T(8,128)(2,1)S(1)}, bf16[1,256,128]{2,1,0:T(8,128)(2,1)S(1)}, u32[]{:S(2)}, u32[]{:S(2)}) collective-permute-start(bf16[1,256,128]{2,1,0:T(8,128)(2,1)S(1)} %get-tuple-element.21), channel_id=1, source_target_pairs={{0,16},{1,17},{2,18},{3,19},{4,20},{5,21},{6,22},{7,23},{24,8},{25... | collective-permute-start | bytes 196616 | tf_op jit(solution)/shard_map/ppermute | solution.py:256
  15.4 17.8 %collective-permute-start.4 = (bf16[1,256,128]{2,1,0:T(8,128)(2,1)S(1)}, bf16[1,256,128]{2,1,0:T(8,128)(2,1)S(1)}, u32[]{:S(2)}, u32[]{:S(2)}) collective-permute-start(bf16[1,256,128]{2,1,0:T(8,128)(2,1)S(1)} %get-tuple-element.21), channel_id=1, source_target_pairs={{8,16},{9,17},{10,18},{11,19},{12,20},{13,21},{14,22},{15,23},{16,... | collective-permute-start | bytes 196616 | tf_op jit(solution)/shard_map/ppermute | solution.py:256
  22.1 22.1 %all-to-all-start = ((bf16[16,128,256]{2,1,0:T(8,128)(2,1)}), bf16[16,128,256]{2,1,0:T(8,128)(2,1)S(1)}, u32[]{:S(2)}, u32[]{:S(2)}) async-start(bf16[16,128,256]{2,1,0:T(8,128)(2,1)} %get-tuple-element.26), calls=%async_computation | async-start | bytes 2097152 | tf_op jit(solution)/shard_map/all_to_all | solution.py:270
  33.4 0.8 copy-start.8
  34.2 1.0 copy-start.9
  63.8 18.4 %copy-start = (bf16[2,128,512]{2,1,0:T(8,128)(2,1)S(1)}, bf16[2,128,512]{2,1,0:T(8,128)(2,1)}, u32[]{:S(2)}) copy-start(bf16[2,128,512]{2,1,0:T(8,128)(2,1)} %proj_ref.3) | copy-start | bytes 786436
  63.8 18.4 %copy-start.2 = (bf16[2,128,128]{2,1,0:T(8,128)(2,1)S(1)}, bf16[2,128,128]{2,1,0:T(8,128)(2,1)}, u32[]{:S(2)}) copy-start(bf16[2,128,128]{2,1,0:T(8,128)(2,1)} %gate_ref.5) | copy-start | bytes 196612
  63.8 18.4 %copy-start.3 = (bf16[2,128,128]{2,1,0:T(8,128)(2,1)S(1)}, bf16[2,128,128]{2,1,0:T(8,128)(2,1)}, u32[]{:S(2)}) copy-start(bf16[2,128,128]{2,1,0:T(8,128)(2,1)} %out_ref.5) | copy-start | bytes 196612
  63.8 18.4 %copy-start.5 = (f32[2,128]{1,0:T(2,128)S(1)}, f32[2,128]{1,0:T(2,128)}, u32[]{:S(2)}) copy-start(f32[2,128]{1,0:T(2,128)} %gain_ref.7) | copy-start | bytes 3076
  63.8 18.4 %copy-start.6 = (f32[2,128]{1,0:T(2,128)S(1)}, f32[2,128]{1,0:T(2,128)}, u32[]{:S(2)}) copy-start(f32[2,128]{1,0:T(2,128)} %mid_gain_ref.5) | copy-start | bytes 3076
  115.9 18.3 %copy-start.1 = (bf16[128,1024]{1,0:T(8,128)(2,1)S(1)}, bf16[128,1024]{1,0:T(8,128)(2,1)}, u32[]{:S(2)}) copy-start(bf16[128,1024]{1,0:T(8,128)(2,1)} %up_ref.3) | copy-start | bytes 786436
  115.9 18.3 %copy-start.4 = (bf16[512,128]{1,0:T(8,128)(2,1)S(1)}, bf16[512,128]{1,0:T(8,128)(2,1)}, u32[]{:S(2)}) copy-start(bf16[512,128]{1,0:T(8,128)(2,1)} %down_ref.3) | copy-start | bytes 393220
  115.9 18.3 %copy-start.7 = (f32[128]{0:T(128)S(1)}, f32[128]{0:T(128)}, u32[]{:S(2)}) copy-start(f32[128]{0:T(128)} %param.15) | copy-start | bytes 1540
  137.9 27.9 %collective-permute-start.9 = (bf16[8,256,128]{2,1,0:T(8,128)(2,1)S(1)}, bf16[8,256,128]{2,1,0:T(8,128)(2,1)S(1)}, u32[]{:S(2)}, u32[]{:S(2)}) collective-permute-start(bf16[8,256,128]{2,1,0:T(8,128)(2,1)S(1)} %combine_transition.2), channel_id=1, source_target_pairs={{0,8},{1,9},{2,10},{3,11},{4,12},{5,13},{6,14},{7,15},{24,16},{25,... | collective-permute-start | bytes 1572872 | tf_op jit(solution)/shard_map/ppermute | solution.py:256
  139.2 28.8 %collective-permute-start.8 = (bf16[8,256,128]{2,1,0:T(8,128)(2,1)S(1)}, bf16[8,256,128]{2,1,0:T(8,128)(2,1)S(1)}, u32[]{:S(2)}, u32[]{:S(2)}) collective-permute-start(bf16[8,256,128]{2,1,0:T(8,128)(2,1)S(1)} %combine_transition.2), channel_id=1, source_target_pairs={{8,16},{9,17},{10,18},{11,19},{12,20},{13,21},{14,22},{15,23},{16,... | collective-permute-start | bytes 1572872 | tf_op jit(solution)/shard_map/ppermute | solution.py:256
  145.3 22.8 %collective-permute-start.7 = (bf16[8,256,128]{2,1,0:T(8,128)(2,1)S(1)}, bf16[8,256,128]{2,1,0:T(8,128)(2,1)S(1)}, u32[]{:S(2)}, u32[]{:S(2)}) collective-permute-start(bf16[8,256,128]{2,1,0:T(8,128)(2,1)S(1)} %combine_transition.3.top_ref), channel_id=1, source_target_pairs={{8,24},{9,25},{10,26},{11,27},{12,28},{13,29},{14,30},{15,31},{16,... | collective-permute-start | bytes 1572872 | tf_op jit(solution)/shard_map/ppermute | solution.py:256

commit v7 on v6

--- a/solution.py
+++ b/solution.py
@@ -50,7 +50,7 @@
         )
 
 
-def combine(pair, rows, which, gain_ref, gate_ref, mid_gain_ref, out_ref, got, scratch_ref):
+def combine(pair, normed, rows, which, gate_ref, mid_gain_ref, out_ref, got, scratch_ref):
     lanes = got.shape[2]
     inner = out_ref.shape[1]
     got = got.astype(jnp.float32).reshape(inner, rows, lanes)
@@ -58,7 +58,6 @@
     centred = got - average
     spread = jnp.mean(centred * centred, axis=0, keepdims=True)
     centred = centred * lax.rsqrt(spread + epsilon)
-    normed = norm_lanes(pair, gain_ref[which : which + 1])
     gating = jax.nn.sigmoid(dot(normed, gate_ref[which], (1, 0)))
     mid_gain = jnp.broadcast_to(mid_gain_ref[which : which + 1], (lanes, inner)).T
     if rows % 16 == 0:
@@ -81,33 +80,39 @@
 
 
 def near_kernel(flag_ref, own_ref, gain_ref, proj_ref, *refs):
-    other_refs, (pair_ref, sent_ref) = refs[:-2], refs[-2:]
+    other_refs, (pair_ref, normed_ref, sent_ref) = refs[:-3], refs[-3:]
     rows, width, _ = pair_ref.shape
     for columns in column_blocks(width):
         other = jnp.concatenate([flat(ref[:, columns]) for ref in other_refs], axis=0)
         pair = jnp.where(flag_ref[0] == 1, flat(own_ref[:rows, columns]), other)
         pair_ref[:, columns] = pair.reshape(rows, LANES, -1)
-        project(norm_lanes(pair, gain_ref[0:1]), proj_ref, 0, sent_ref, columns, rows)
+        normed = norm_lanes(pair, gain_ref[0:1])
+        normed_ref[:, columns] = normed.reshape(rows, LANES, -1)
+        project(normed, proj_ref, 0, sent_ref, columns, rows)
 
 
 def middle_kernel(
-    near_ref, far_ref, got_ref, gain_ref, gate_ref, mid_gain_ref, out_ref, proj_ref,
-    pair_out_ref, sent_ref, scratch_ref,
+    near_ref, far_ref, near_normed_ref, far_normed_ref, got_ref, gain_ref, gate_ref, mid_gain_ref, out_ref, proj_ref,
+    pair_out_ref, normed_ref, sent_ref, scratch_ref,
 ):
     rows, width, _ = pair_out_ref.shape
     for columns in column_blocks(width):
         pair = jnp.concatenate([flat(near_ref[:, columns]), flat(far_ref[:, columns])], axis=0)
+        normed = jnp.concatenate(
+            [flat(near_normed_ref[:, columns]), flat(far_normed_ref[:, columns])], axis=0
+        )
         current = combine(
-            pair, rows, 0, gain_ref, gate_ref, mid_gain_ref, out_ref, got_ref[:, :, columns],
+            pair, normed, rows, 0, gate_ref, mid_gain_ref, out_ref, got_ref[:, :, columns],
             scratch_ref,
         )
         pair_out_ref[:, columns] = current.reshape(rows, LANES, -1)
         normed = norm_lanes(current, gain_ref[1:2])
+        normed_ref[:, columns] = normed.reshape(rows, LANES, -1)
         project(normed, proj_ref, 1, sent_ref, columns, rows)
 
 
 def last_kernel(
-    slot, pair_ref, got_ref, gain_ref, gate_ref, mid_gain_ref, out_ref, trans_gain_ref, up_ref,
+    slot, pair_ref, normed_ref, got_ref, gate_ref, mid_gain_ref, out_ref, trans_gain_ref, up_ref,
     down_ref, pair_out_ref, scratch_ref,
 ):
     rows, width, _ = pair_out_ref.shape
@@ -117,8 +122,8 @@
     for columns in column_blocks(width):
         got = got_ref[:, slot * size : (slot + 1) * size, columns]
         current = combine(
-            flat(pair_ref[slot * rows : (slot + 1) * rows, columns]), rows, 1,
-            gain_ref, gate_ref, mid_gain_ref, out_ref, got, scratch_ref,
+            flat(pair_ref[slot * rows : (slot + 1) * rows, columns]),
+            flat(normed_ref[slot * rows : (slot + 1) * rows, columns]), rows, 1, gate_ref, mid_gain_ref, out_ref, got, scratch_ref,
         )
         normed = norm_lanes(current, trans_gain_ref[...])
         total = current.astype(jnp.float32)
@@ -305,15 +310,15 @@
 
     scratch = [pltpu.VMEM((inner * rows, LANES), jnp.float32)]
 
-    near, near_sent = call(
+    near, near_normed, near_sent = call(
         near_kernel, "project",
-        [shape(own, width, channels), shape(parts, 2 * per * own, width)], [],
+        [shape(own, width, channels)] * 2 + [shape(parts, 2 * per * own, width)], [],
         home_flag, low, first_gain, first_proj, stepped, *hopped, flops=0,
     )
     near_got = exchange(near_sent)
-    far, far_sent = call(
+    far, far_normed, far_sent = call(
         near_kernel, "project",
-        [shape(own, width, channels), shape(parts, 2 * per * own, width)], [],
+        [shape(own, width, channels)] * 2 + [shape(parts, 2 * per * own, width)], [],
         home_flag, direct, first_gain, first_proj, diagonal, *relayed, flops=5 * FAR_FLOPS,
     )
     far_got = exchange(far_sent)
@@ -324,10 +329,10 @@
     )
     back = exchange(product).reshape(parts, per * rows, width)
 
-    current, sent = call(
+    current, normed, sent = call(
         middle_kernel, "combine_project",
-        [shape(rows, width, channels), shape(parts, 2 * per * rows, width)], scratch,
-        near, far, back, tri_gain, tri_gate, tri_mid_gain, tri_out, tri_proj,
+        [shape(rows, width, channels)] * 2 + [shape(parts, 2 * per * rows, width)], scratch,
+        near, far, near_normed, far_normed, back, tri_gain, tri_gate, tri_mid_gain, tri_out, tri_proj,
     )
     got = exchange(sent).reshape(parts, 2, per, rows, width)
 
@@ -340,7 +345,7 @@
         return call(
             functools.partial(last_kernel, slot), "combine_transition",
             shape(own, width, channels), scratch,
-            current, back, tri_gain, tri_gate, tri_mid_gain, tri_out, trans_gain[None],
+            current, normed, back, tri_gate, tri_mid_gain, tri_out, trans_gain[None],
             trans_up, trans_down, flops=flops,
         )
 

time: 170 us -> 169 us (level)
  no operation moved by 1% of the time
where the time goes in v7:
time: 169 us; the launch traced here: 168 us
  blocking collectives  83.9 us (50%)
  waiting for transfers between devices  39.2 us (23%)
  starting transfers between devices  23.6 us (14%)
  Pallas kernels  19.4 us (11%)
    all_to_all x4, blocking collectives, exchange(): lax.all_to_all(value, AXES, split_axis=0, concat_axis=0, tiled=True, axis...  83.9 us
    ppermute x10, waiting for transfers between devices, permute(): lax.ppermute(value, AXES, [(number(*a), number(*b)) for a, b in pairs])  32.6 us
    pallas_call x9, Pallas kernels, call(): pl.pallas_call(kernel, in_specs=[smem if operand.dtype == jnp.int32 else...  18.1 us
    ppermute x10, starting transfers between devices, permute(): lax.ppermute(value, AXES, [(number(*a), number(*b)) for a, b in pairs])  15.9 us
    all_to_all x1, starting transfers between devices, exchange(): lax.all_to_all(value, AXES, split_axis=0, concat_axis=0, tiled=True, axis...  7.78 us
    all_to_all x1, waiting for transfers between devices, exchange(): lax.all_to_all(value, AXES, split_axis=0, concat_axis=0, tiled=True, axis...  6.56 us
  transfers between devices with their start and end apart: 11, of which 8 were waited for; matrix products, arithmetic and copies ran while one was open for 0% of the time, Pallas kernels for 5%

profile of v7, /device:TPU:25, one launch (start us, length us, event | category | flops | bytes accessed | tf_op | source)
XLA Modules:
  0.0 168.0 jit_solution(14260532256378122732)
XLA Ops:
  0.0 1.3 split.1
  1.3 1.3 collective-permute-start.1
  2.6 2.8 %collective-permute-start.3 = (bf16[8,256,128]{2,1,0:T(8,128)(2,1)S(1)}, bf16[8,256,128]{2,1,0:T(8,128)(2,1)}, u32[]{:S(2)}, u32[]{:S(2)}) collective-permute-start(bf16[8,256,128]{2,1,0:T(8,128)(2,1)S(1)} %get-tuple-element.21.own_ref), channel_id=1, source_target_pairs={{8,0},{9,1},{10,2},{11,3},{12,4},{13,5},{14,6},{15,7},{16,24},{17,... | collective-permute-start | bytes 1572872 | tf_op jit(solution)/shard_map/ppermute | solution.py:261
  5.4 3.2 %collective-permute-done.1.refs_1_ = bf16[4,256,128]{2,1,0:T(8,128)(2,1)S(1)} collective-permute-done((bf16[4,256,128]{2,1,0:T(8,128)(2,1)S(1)}, bf16[4,256,128]{2,1,0:T(8,128)(2,1)S(1)}, u32[]{:S(2)}, u32[]{:S(2)}) %collective-permute-start.1) | collective-permute-done | bytes 262176 | tf_op jit(solution)/shard_map/ppermute | solution.py:261
  8.6 1.3 collective-permute-start.5
  9.9 2.9 %collective-permute-done.2.refs_2_ = bf16[3,256,128]{2,1,0:T(8,128)(2,1)S(1)} collective-permute-done((bf16[3,256,128]{2,1,0:T(8,128)(2,1)S(1)}, bf16[3,256,128]{2,1,0:T(8,128)(2,1)S(1)}, u32[]{:S(2)}, u32[]{:S(2)}) %collective-permute-start.2) | collective-permute-done | bytes 196640 | tf_op jit(solution)/shard_map/ppermute | solution.py:261
  12.8 1.3 collective-permute-start.6
  14.1 1.3 collective-permute-start
  15.4 2.6 %collective-permute-start.4 = (bf16[1,256,128]{2,1,0:T(8,128)(2,1)S(1)}, bf16[1,256,128]{2,1,0:T(8,128)(2,1)S(1)}, u32[]{:S(2)}, u32[]{:S(2)}) collective-permute-start(bf16[1,256,128]{2,1,0:T(8,128)(2,1)S(1)} %get-tuple-element.24), channel_id=1, source_target_pairs={{8,16},{9,17},{10,18},{11,19},{12,20},{13,21},{14,22},{15,23},{16,... | collective-permute-start | bytes 196616 | tf_op jit(solution)/shard_map/ppermute | solution.py:261
  18.0 1.2 collective-permute-done.refs_0_
  19.3 2.4 %project.2 = (bf16[8,256,128]{2,1,0:T(8,128)(2,1)S(1)}, bf16[8,256,128]{2,1,0:T(8,128)(2,1)S(1)}, bf16[16,128,256]{2,1,0:T(8,128)(2,1)}) custom-call(s32[1]{0:T(128)} %bitcast.flag_ref, bf16[8,256,128]{2,1,0:T(8,128)(2,1)S(1)} %get-tuple-element.21.own_ref, f32[2,128]{1,0:T(2,128)S(1)} %get-tuple-element.22.gain_ref, ...), custom_call_target="tpu_custom_call" | custom-call | tf_op jit(solution)/shard_map/project/pallas_call | solution.py:222
  21.7 7.8 %all-to-all-start = ((bf16[16,128,256]{2,1,0:T(8,128)(2,1)}), bf16[16,128,256]{2,1,0:T(8,128)(2,1)S(1)}, u32[]{:S(2)}, u32[]{:S(2)}) async-start(bf16[16,128,256]{2,1,0:T(8,128)(2,1)} %get-tuple-element.31), calls=%async_computation | async-start | bytes 2097152 | tf_op jit(solution)/shard_map/all_to_all | solution.py:275
  29.5 3.7 %collective-permute-done.4.refs_0_ = bf16[1,256,128]{2,1,0:T(8,128)(2,1)S(1)} collective-permute-done((bf16[1,256,128]{2,1,0:T(8,128)(2,1)S(1)}, bf16[1,256,128]{2,1,0:T(8,128)(2,1)S(1)}, u32[]{:S(2)}, u32[]{:S(2)}) %collective-permute-start.4) | collective-permute-done | bytes 65568 | tf_op jit(solution)/shard_map/ppermute | solution.py:261
  33.4 2.6 %project.3 = (bf16[8,256,128]{2,1,0:T(8,128)(2,1)S(1)}, bf16[8,256,128]{2,1,0:T(8,128)(2,1)S(1)}, bf16[16,128,256]{2,1,0:T(8,128)(2,1)S(1)}) custom-call(s32[1]{0:T(128)} %bitcast.flag_ref, bf16[8,256,128]{2,1,0:T(8,128)(2,1)} %collective-permute-done.3.own_ref, f32[2,128]{1,0:T(2,128)S(1)} %get-tuple-element.22.gain_ref, ...), custom_call_target="tpu_custom_call" | custom-call | flops 99999997952 | tf_op jit(solution)/shard_map/project/pallas_call | solution.py:222
  36.0 0.8 copy-done.1
  36.9 0.8 copy-done.3
  37.7 6.6 %all-to-all-done.near_ref = bf16[16,128,256]{2,1,0:T(8,128)(2,1)S(1)} async-done(((bf16[16,128,256]{2,1,0:T(8,128)(2,1)}), bf16[16,128,256]{2,1,0:T(8,128)(2,1)S(1)}, u32[]{:S(2)}, u32[]{:S(2)}) %all-to-all-start) | async-done | bytes 1048608 | tf_op jit(solution)/shard_map/all_to_all | solution.py:275
  44.2 19.6 %all_to_all.25.far_ref = bf16[16,128,256]{2,1,0:T(8,128)(2,1)S(1)} all-to-all(bf16[16,128,256]{2,1,0:T(8,128)(2,1)S(1)} %get-tuple-element.32), channel_id=1, replica_groups={{0,16,1,17,2,18,3,19,4,20,5,21,6,22,7,23},{24,8,25,9,26,10,27,11,28,12,..., dimensions={0} | all-to-all | bytes 2097152 | tf_op jit(solution)/shard_map/all_to_all | solution.py:275
  63.9 0.7 outgoing.1
  64.6 17.6 %all_to_all.26 = bf16[16,8,16,256]{3,2,1,0:T(8,128)(2,1)S(1)} all-to-all(bf16[16,8,16,256]{3,2,1,0:T(8,128)(2,1)S(1)} %outgoing.1), channel_id=1, replica_groups={{0,16,1,17,2,18,3,19,4,20,5,21,6,22,7,23},{24,8,25,9,26,10,27,11,28,12,..., dimensions={0} | all-to-all | bytes 2097152 | tf_op jit(solution)/shard_map/all_to_all | solution.py:275
  82.3 4.0 %combine_project.1 = (bf16[16,256,128]{2,1,0:T(8,128)(2,1)S(1)}, bf16[16,256,128]{2,1,0:T(8,128)(2,1)S(1)}, bf16[16,256,256]{2,1,0:T(8,128)(2,1)S(1)}) custom-call(bf16[8,256,128]{2,1,0:T(8,128)(2,1)S(1)} %get-tuple-element.27.near_ref, bf16[8,256,128]{2,1,0:T(8,128)(2,1)S(1)} %copy-done.2, bf16[8,256,128]{2,1,0:T(8,128)(2,1)S(1)} %get-tuple-element.29.near_normed_ref, ...), custom_call_target="tpu_custom_call" | custom-call | tf_op jit(solution)/shard_map/combine_project/pallas_call | solution.py:222
  86.3 28.9 %all_to_all.27 = bf16[16,256,256]{2,1,0:T(8,128)(2,1)S(1)} all-to-all(bf16[16,256,256]{2,1,0:T(8,128)(2,1)S(1)} %get-tuple-element.35), channel_id=1, replica_groups={{0,16,1,17,2,18,3,19,4,20,5,21,6,22,7,23},{24,8,25,9,26,10,27,11,28,12,..., dimensions={0} | all-to-all | bytes 4194304 | tf_op jit(solution)/shard_map/all_to_all | solution.py:275
  115.2 0.5 incoming.1
  115.7 17.7 %all_to_all.28.got_ref = bf16[16,128,256]{2,1,0:T(8,128)(2,1)S(1)} all-to-all(bf16[16,128,256]{2,1,0:T(8,128)(2,1)S(1)} %incoming.1), channel_id=1, replica_groups={{0,16,1,17,2,18,3,19,4,20,5,21,6,22,7,23},{24,8,25,9,26,10,27,11,28,12,..., dimensions={0} | all-to-all | bytes 2097152 | tf_op jit(solution)/shard_map/all_to_all | solution.py:275
  133.4 3.4 %combine_transition.2 = bf16[8,256,128]{2,1,0:T(8,128)(2,1)S(1)} custom-call(bf16[16,256,128]{2,1,0:T(8,128)(2,1)S(1)} %get-tuple-element.33.pair_ref, bf16[16,256,128]{2,1,0:T(8,128)(2,1)S(1)} %get-tuple-element.34.normed_ref, bf16[16,128,256]{2,1,0:T(8,128)(2,1)S(1)} %all_to_all.28.got_ref, bf16[2,128,128]{2,1,0:T(8,128)(2,1)S(1)} %copy-done.5, ...), custom_call_target="tpu_custom_call" | custom-call | tf_op jit(solution)/shard_map/combine_transition/pallas_call | solution.py:222
  136.8 1.3 collective-permute-start.9
  138.1 2.4 %collective-permute-start.8 = (bf16[8,256,128]{2,1,0:T(8,128)(2,1)S(1)}, bf16[8,256,128]{2,1,0:T(8,128)(2,1)S(1)}, u32[]{:S(2)}, u32[]{:S(2)}) collective-permute-start(bf16[8,256,128]{2,1,0:T(8,128)(2,1)S(1)} %combine_transition.2), channel_id=1, source_target_pairs={{8,16},{9,17},{10,18},{11,19},{12,20},{13,21},{14,22},{15,23},{16,... | collective-permute-start | bytes 1572872 | tf_op jit(solution)/shard_map/ppermute | solution.py:261
  140.5 3.4 %combine_transition.3.top_ref = bf16[8,256,128]{2,1,0:T(8,128)(2,1)S(1)} custom-call(bf16[16,256,128]{2,1,0:T(8,128)(2,1)S(1)} %get-tuple-element.33.pair_ref, bf16[16,256,128]{2,1,0:T(8,128)(2,1)S(1)} %get-tuple-element.34.normed_ref, bf16[16,128,256]{2,1,0:T(8,128)(2,1)S(1)} %all_to_all.28.got_ref, bf16[2,128,128]{2,1,0:T(8,128)(2,1)S(1)} %copy-done.5, ...), custom_call_target="tpu_custom_call" | custom-call | flops 20000000000 | tf_op jit(solution)/shard_map/combine_transition/pallas_call | solution.py:222
  143.9 1.7 collective-permute-start.7
  145.5 19.1 %collective-permute-done.9.bottom_ref = bf16[8,256,128]{2,1,0:T(8,128)(2,1)S(1)} collective-permute-done((bf16[8,256,128]{2,1,0:T(8,128)(2,1)S(1)}, bf16[8,256,128]{2,1,0:T(8,128)(2,1)S(1)}, u32[]{:S(2)}, u32[]{:S(2)}) %collective-permute-start.9) | collective-permute-done | bytes 524320 | tf_op jit(solution)/shard_map/ppermute | solution.py:261
  164.7 2.2 %collective-permute-done.8.top_ref = bf16[8,256,128]{2,1,0:T(8,128)(2,1)S(1)} collective-permute-done((bf16[8,256,128]{2,1,0:T(8,128)(2,1)S(1)}, bf16[8,256,128]{2,1,0:T(8,128)(2,1)S(1)}, u32[]{:S(2)}, u32[]{:S(2)}) %collective-permute-start.8) | collective-permute-done | bytes 524320 | tf_op jit(solution)/shard_map/ppermute | solution.py:261
  166.9 1.1 pick.1
  (28 shorter events, 0.4 us)
Async XLA Ops:
  1.3 7.2 %collective-permute-start.1 = (bf16[4,256,128]{2,1,0:T(8,128)(2,1)S(1)}, bf16[4,256,128]{2,1,0:T(8,128)(2,1)S(1)}, u32[]{:S(2)}, u32[]{:S(2)}) collective-permute-start(bf16[4,256,128]{2,1,0:T(8,128)(2,1)S(1)} %get-tuple-element.25), channel_id=1, source_target_pairs={{0,16},{1,17},{2,18},{3,19},{4,20},{5,21},{6,22},{7,23},{8,24},{9,... | collective-permute-start | bytes 786440 | tf_op jit(solution)/shard_map/ppermute | solution.py:261
  2.6 30.8 %collective-permute-start.3 = (bf16[8,256,128]{2,1,0:T(8,128)(2,1)S(1)}, bf16[8,256,128]{2,1,0:T(8,128)(2,1)}, u32[]{:S(2)}, u32[]{:S(2)}) collective-permute-start(bf16[8,256,128]{2,1,0:T(8,128)(2,1)S(1)} %get-tuple-element.21.own_ref), channel_id=1, source_target_pairs={{8,0},{9,1},{10,2},{11,3},{12,4},{13,5},{14,6},{15,7},{16,24},{17,... | collective-permute-start | bytes 1572872 | tf_op jit(solution)/shard_map/ppermute | solution.py:261
  5.4 7.4 %collective-permute-start.2 = (bf16[3,256,128]{2,1,0:T(8,128)(2,1)S(1)}, bf16[3,256,128]{2,1,0:T(8,128)(2,1)S(1)}, u32[]{:S(2)}, u32[]{:S(2)}) collective-permute-start(bf16[3,256,128]{2,1,0:T(8,128)(2,1)S(1)} %get-tuple-element.26), channel_id=1, source_target_pairs={{0,16},{1,17},{2,18},{3,19},{4,20},{5,21},{6,22},{7,23},{8,24},{9,... | collective-permute-start | bytes 589832 | tf_op jit(solution)/shard_map/ppermute | solution.py:261
  8.6 24.8 %collective-permute-start.5 = (bf16[4,256,128]{2,1,0:T(8,128)(2,1)S(1)}, bf16[4,256,128]{2,1,0:T(8,128)(2,1)}, u32[]{:S(2)}, u32[]{:S(2)}) collective-permute-start(bf16[4,256,128]{2,1,0:T(8,128)(2,1)S(1)} %collective-permute-done.1.refs_1_), channel_id=1, source_target_pairs={{0,8},{1,9},{2,10},{3,11},{4,12},{5,13},{6,14},{7,15},{24,16},{25,... | collective-permute-start | bytes 786440 | tf_op jit(solution)/shard_map/ppermute | solution.py:261
  12.8 20.6 %collective-permute-start.6 = (bf16[3,256,128]{2,1,0:T(8,128)(2,1)S(1)}, bf16[3,256,128]{2,1,0:T(8,128)(2,1)}, u32[]{:S(2)}, u32[]{:S(2)}) collective-permute-start(bf16[3,256,128]{2,1,0:T(8,128)(2,1)S(1)} %collective-permute-done.2.refs_2_), channel_id=1, source_target_pairs={{0,8},{1,9},{2,10},{3,11},{4,12},{5,13},{6,14},{7,15},{24,16},{25,... | collective-permute-start | bytes 589832 | tf_op jit(solution)/shard_map/ppermute | solution.py:261
  14.1 5.2 %collective-permute-start = (bf16[1,256,128]{2,1,0:T(8,128)(2,1)S(1)}, bf16[1,256,128]{2,1,0:T(8,128)(2,1)S(1)}, u32[]{:S(2)}, u32[]{:S(2)}) collective-permute-start(bf16[1,256,128]{2,1,0:T(8,128)(2,1)S(1)} %get-tuple-element.24), channel_id=1, source_target_pairs={{0,16},{1,17},{2,18},{3,19},{4,20},{5,21},{6,22},{7,23},{24,8},{25... | collective-permute-start | bytes 196616 | tf_op jit(solution)/shard_map/ppermute | solution.py:261
  15.4 17.8 %collective-permute-start.4 = (bf16[1,256,128]{2,1,0:T(8,128)(2,1)S(1)}, bf16[1,256,128]{2,1,0:T(8,128)(2,1)S(1)}, u32[]{:S(2)}, u32[]{:S(2)}) collective-permute-start(bf16[1,256,128]{2,1,0:T(8,128)(2,1)S(1)} %get-tuple-element.24), channel_id=1, source_target_pairs={{8,16},{9,17},{10,18},{11,19},{12,20},{13,21},{14,22},{15,23},{16,... | collective-permute-start | bytes 196616 | tf_op jit(solution)/shard_map/ppermute | solution.py:261
  21.7 22.5 %all-to-all-start = ((bf16[16,128,256]{2,1,0:T(8,128)(2,1)}), bf16[16,128,256]{2,1,0:T(8,128)(2,1)S(1)}, u32[]{:S(2)}, u32[]{:S(2)}) async-start(bf16[16,128,256]{2,1,0:T(8,128)(2,1)} %get-tuple-element.31), calls=%async_computation | async-start | bytes 2097152 | tf_op jit(solution)/shard_map/all_to_all | solution.py:275
  36.0 0.8 copy-start.1
  36.9 0.8 copy-start.3
  63.8 18.4 %copy-start = (bf16[2,128,512]{2,1,0:T(8,128)(2,1)S(1)}, bf16[2,128,512]{2,1,0:T(8,128)(2,1)}, u32[]{:S(2)}) copy-start(bf16[2,128,512]{2,1,0:T(8,128)(2,1)} %proj_ref.3) | copy-start | bytes 786436
  63.8 18.4 %copy-start.2 = (bf16[8,256,128]{2,1,0:T(8,128)(2,1)S(1)}, bf16[8,256,128]{2,1,0:T(8,128)(2,1)}, u32[]{:S(2)}) copy-start(bf16[8,256,128]{2,1,0:T(8,128)(2,1)} %copy-done.1) | copy-start | bytes 1572868
  63.8 18.4 %copy-start.4 = (bf16[8,256,128]{2,1,0:T(8,128)(2,1)S(1)}, bf16[8,256,128]{2,1,0:T(8,128)(2,1)}, u32[]{:S(2)}) copy-start(bf16[8,256,128]{2,1,0:T(8,128)(2,1)} %copy-done.3) | copy-start | bytes 1572868
  63.8 18.4 %copy-start.5 = (bf16[2,128,128]{2,1,0:T(8,128)(2,1)S(1)}, bf16[2,128,128]{2,1,0:T(8,128)(2,1)}, u32[]{:S(2)}) copy-start(bf16[2,128,128]{2,1,0:T(8,128)(2,1)} %gate_ref.5) | copy-start | bytes 196612
  63.8 18.4 %copy-start.6 = (bf16[2,128,128]{2,1,0:T(8,128)(2,1)S(1)}, bf16[2,128,128]{2,1,0:T(8,128)(2,1)}, u32[]{:S(2)}) copy-start(bf16[2,128,128]{2,1,0:T(8,128)(2,1)} %out_ref.5) | copy-start | bytes 196612
  63.9 18.4 %copy-start.9 = (f32[2,128]{1,0:T(2,128)S(1)}, f32[2,128]{1,0:T(2,128)}, u32[]{:S(2)}) copy-start(f32[2,128]{1,0:T(2,128)} %mid_gain_ref.5) | copy-start | bytes 3076
  63.9 18.4 %copy-start.10 = (f32[2,128]{1,0:T(2,128)S(1)}, f32[2,128]{1,0:T(2,128)}, u32[]{:S(2)}) copy-start(f32[2,128]{1,0:T(2,128)} %gain_ref.3) | copy-start | bytes 3076
  115.2 18.3 %copy-start.7 = (bf16[128,1024]{1,0:T(8,128)(2,1)S(1)}, bf16[128,1024]{1,0:T(8,128)(2,1)}, u32[]{:S(2)}) copy-start(bf16[128,1024]{1,0:T(8,128)(2,1)} %up_ref.3) | copy-start | bytes 786436
  115.2 18.3 %copy-start.8 = (bf16[512,128]{1,0:T(8,128)(2,1)S(1)}, bf16[512,128]{1,0:T(8,128)(2,1)}, u32[]{:S(2)}) copy-start(bf16[512,128]{1,0:T(8,128)(2,1)} %down_ref.3) | copy-start | bytes 393220
  115.2 18.3 %copy-start.11 = (f32[128]{0:T(128)S(1)}, f32[128]{0:T(128)}, u32[]{:S(2)}) copy-start(f32[128]{0:T(128)} %param.15) | copy-start | bytes 1540
  136.8 27.9 %collective-permute-start.9 = (bf16[8,256,128]{2,1,0:T(8,128)(2,1)S(1)}, bf16[8,256,128]{2,1,0:T(8,128)(2,1)S(1)}, u32[]{:S(2)}, u32[]{:S(2)}) collective-permute-start(bf16[8,256,128]{2,1,0:T(8,128)(2,1)S(1)} %combine_transition.2), channel_id=1, source_target_pairs={{0,8},{1,9},{2,10},{3,11},{4,12},{5,13},{6,14},{7,15},{24,16},{25,... | collective-permute-start | bytes 1572872 | tf_op jit(solution)/shard_map/ppermute | solution.py:261
  138.1 28.8 %collective-permute-start.8 = (bf16[8,256,128]{2,1,0:T(8,128)(2,1)S(1)}, bf16[8,256,128]{2,1,0:T(8,128)(2,1)S(1)}, u32[]{:S(2)}, u32[]{:S(2)}) collective-permute-start(bf16[8,256,128]{2,1,0:T(8,128)(2,1)S(1)} %combine_transition.2), channel_id=1, source_target_pairs={{8,16},{9,17},{10,18},{11,19},{12,20},{13,21},{14,22},{15,23},{16,... | collective-permute-start | bytes 1572872 | tf_op jit(solution)/shard_map/ppermute | solution.py:261
  143.9 23.1 %collective-permute-start.7 = (bf16[8,256,128]{2,1,0:T(8,128)(2,1)S(1)}, bf16[8,256,128]{2,1,0:T(8,128)(2,1)S(1)}, u32[]{:S(2)}, u32[]{:S(2)}) collective-permute-start(bf16[8,256,128]{2,1,0:T(8,128)(2,1)S(1)} %combine_transition.3.top_ref), channel_id=1, source_target_pairs={{8,24},{9,25},{10,26},{11,27},{12,28},{13,29},{14,30},{15,31},{16,... | collective-permute-start | bytes 1572872 | tf_op jit(solution)/shard_map/ppermute | solution.py:261
